TPU v7x, 256 devices: a whole 4x4x8 slice. The times are simulated.
256 devices in a mesh: dom: 64 (over z, y, core), feat: 4 (over x).
Axes of the slice: x: 4, y: 4, z: 8, core: 2. Of those that a mesh axis runs over, the one named last changes fastest.
Arguments:
- quantized: bfloat16 [128, 524288], P('feat', 'dom'), may hold values from -4 to 4
- node_scale: float32 [524288], P('dom'), may hold values from 0.25 to 4
- send_rows: int32 [64, 64, 192], P('dom'), may hold values from 0 to 8191
- send_count: int32 [64, 64], P('dom'), may hold values from 1 to 192, 9216 in all within a row
- tile_cols: int32 [64, 64, 4], P('dom'), may hold values from 0 to 159, as said below
- edge_tiles: int32 [4096, 4, 128, 128], P('dom'), may hold values 0 or 1
- self_weight: bfloat16 [128, 256], P('feat'), may hold values from -0.5 to 0.5
- neighbor_weight: bfloat16 [128, 256], P('feat'), may hold values from -4 to 4
- hidden_bias: float32 [256], P('feat'), may hold values from -3 to 3
- upstream: bfloat16 [256, 524288], P('feat', 'dom'), may hold values from -6 to 6
Outputs:
- hidden: bfloat16 [256, 524288], P('feat', 'dom')
- grad_features: float32 [128, 524288], P('feat', 'dom')
- grad_self: float32 [128, 256], P('feat')
- grad_neighbor: float32 [128, 256], P('feat')
- grad_bias: float32 [256], P('feat')
Inputs may be any that keep to these rules, and one draw needn't show every extreme that they name: `send_rows`: indices of nodes within the sending partition. Each row of send_count sums to 9216 and its largest entry is exactly 192. `tile_cols`: in each partition every one of the 160 column tiles is named by some row tile.
All inputs are finite; a program needn't handle non-finite values. No bound on the sum of `edge_tiles` on one device may be relied on, other than what follows from the above.
Results may differ from a plain program's by a relative error of at most 0.008.
Values may be sent and summed in bfloat16 or wider, within the bound.
No kernel may reach another device: no remote copies, remote signals or barrier semaphores. Data moves between devices by JAX's collectives and lax.ppermute only.
A program may use at most 128 MiB of HBM per device.

v0:
```python
import jax
import jax.numpy as jnp
from jax import lax
from jax.sharding import PartitionSpec as P


def tile_sum(columns, tile_index, mask_tiles):
    feature_count = columns.shape[0]
    tile_width = mask_tiles.shape[-1]
    blocks = columns.reshape(feature_count, columns.shape[1] // tile_width, tile_width)
    picked = jnp.take(blocks, tile_index, axis=1)
    summed = jnp.einsum("ftkj,tkij->fti", picked, mask_tiles, preferred_element_type=jnp.float32)
    return summed.reshape(feature_count, -1)


def per_device(
    quantized,
    node_scale,
    send_rows,
    send_count,
    tile_cols,
    edge_tiles,
    self_weight,
    neighbor_weight,
    hidden_bias,
    upstream,
):
    feature_count, node_count = quantized.shape
    peer_count = lax.axis_size("dom")
    slot_count = send_rows.shape[2]
    tile_count = edge_tiles.shape[0]
    tile_width = edge_tiles.shape[-1]
    entry_count = edge_tiles.shape[1]
    features = (quantized.astype(jnp.float32) * node_scale[None, :]).astype(jnp.bfloat16)
    slot_index = lax.broadcasted_iota(jnp.int32, (peer_count, slot_count), 1)
    live_slots = (slot_index < send_count[0][:, None]).astype(jnp.bfloat16).reshape(1, -1)
    flat_rows = send_rows[0].reshape(-1)
    outgoing = jnp.take(features, flat_rows, axis=1) * live_slots
    halo_rows = lax.all_to_all(outgoing, "dom", split_axis=1, concat_axis=1, tiled=True)
    mask_tiles = edge_tiles.astype(jnp.bfloat16)
    degree = jnp.sum(edge_tiles, axis=(1, 3)).reshape(-1).astype(jnp.float32)
    denominator = degree + 1.0
    tile_index = tile_cols[0]
    joined = jnp.concatenate([features, halo_rows], axis=1)
    neighbor_sum = tile_sum(joined, tile_index, mask_tiles)
    aggregate = ((neighbor_sum + features.astype(jnp.float32)) / denominator[None, :]).astype(
        jnp.bfloat16
    )
    term = jnp.dot(self_weight.T, features, preferred_element_type=jnp.float32)
    summed = lax.psum_scatter(
        term + jnp.dot(neighbor_weight.T, aggregate, preferred_element_type=jnp.float32),
        "feat",
        scatter_dimension=0,
        tiled=True,
    )
    preact = summed + hidden_bias[:, None]
    sigmoid_z = jax.nn.sigmoid(preact)
    hidden = (preact * sigmoid_z).astype(jnp.bfloat16)
    slope = (upstream.astype(jnp.float32) * sigmoid_z * (1.0 + preact * (1.0 - sigmoid_z))).astype(
        jnp.bfloat16
    )
    slope_full = lax.all_gather(slope, "feat", axis=0, tiled=True)
    contract_nodes = (((1,), (1,)), ((), ()))
    local_self = lax.dot_general(
        features, slope_full, contract_nodes, preferred_element_type=jnp.float32
    )
    local_neighbor = lax.dot_general(
        aggregate, slope_full, contract_nodes, preferred_element_type=jnp.float32
    )
    local_bias = jnp.sum(slope.astype(jnp.float32), axis=1)
    grad_self, grad_neighbor, grad_bias = lax.psum((local_self, local_neighbor, local_bias), "dom")
    mean_grad = (
        jnp.dot(neighbor_weight, slope_full, preferred_element_type=jnp.float32)
        / denominator[None, :]
    )
    self_grad = jnp.dot(self_weight, slope_full, preferred_element_type=jnp.float32)
    mean_grad_b = mean_grad.astype(jnp.bfloat16).reshape(feature_count, tile_count, tile_width)
    contrib = jnp.einsum(
        "fti,tkij->tkfj", mean_grad_b, mask_tiles, preferred_element_type=jnp.float32
    )
    col_total = node_count // tile_width + halo_rows.shape[1] // tile_width
    segment_grad = jax.ops.segment_sum(
        contrib.reshape(tile_count * entry_count, feature_count, tile_width),
        tile_index.reshape(-1),
        num_segments=col_total,
    )
    joined_grad = segment_grad.transpose(1, 0, 2).reshape(feature_count, col_total * tile_width)
    local_grad = joined_grad[:, :node_count]
    halo_grad = joined_grad[:, node_count:]
    returning = lax.all_to_all(
        halo_grad.astype(jnp.bfloat16), "dom", split_axis=1, concat_axis=1, tiled=True
    ).astype(halo_grad.dtype)
    returning = returning * live_slots.astype(jnp.float32)
    returned = jnp.zeros((feature_count, node_count), jnp.float32).at[:, flat_rows].add(returning)
    grad_features = self_grad + mean_grad + (local_grad + returned)
    return (hidden, grad_features, grad_self, grad_neighbor, grad_bias)


def solution(mesh):
    return jax.shard_map(
        per_device,
        mesh=mesh,
        in_specs=(
            P("feat", "dom"),
            P("dom"),
            P("dom", None, None),
            P("dom", None),
            P("dom", None, None),
            P("dom", None, None, None),
            P("feat", None),
            P("feat", None),
            P("feat"),
            P("feat", "dom"),
        ),
        out_specs=(P("feat", "dom"), P("feat", "dom"), P("feat", None), P("feat", None), P("feat")),
        check_vma=False,
    )
```

profile of v0, /device:TPU:1, one launch (start us, length us, event | category | flops | bytes accessed | tf_op | source)
XLA Modules:
  0.0 554.7 jit_solution(14297237855608890314)
XLA Ops:
  7.2 2.6 copy.67
  9.8 0.9 reshape_squeeze.6
  10.8 2.5 multiply_convert_fusion.2
  13.4 43.6 %gather_fusion = bf16[12288,32]{1,0:T(8,128)(2,1)} fusion(bf16[32,8192]{0,1:T(8,128)(2,1)S(1)} %multiply_convert_fusion.2, s32[12288]{0:T(1024)S(1)} %broadcast_clamp_fusion), kind=kCustom, calls=%fused_computation | custom fusion | bytes 1622016 | tf_op jit(solution)/shard_map/jit(_take)/gather | solution.py:38
  56.9 3.5 copy.69
  60.6 1.1 select_multiply_fusion
  61.7 13.3 %all-to-all-start = ((bf16[32,64,192]{2,0,1:T(8,128)(2,1)}), bf16[32,64,192]{2,0,1:T(8,128)(2,1)}, u32[]{:S(2)}, u32[]{:S(2)}) async-start(bf16[32,64,192]{2,0,1:T(8,128)(2,1)} %select_multiply_fusion), calls=%async_computation | async-start | bytes 2097152 | tf_op jit(solution)/shard_map/all_to_all | solution.py:39
  75.1 0.2 reduce-scatter.4.cloned.1.call-start
  75.3 1.5 copy.71
  76.8 0.1 copy.72
  76.9 0.1 reshape.170
  77.0 0.1 copy.68
  77.2 6.9 %reduce_sum.18 = s32[64,128]{1,0:T(8,128)S(1)} reduce(s32[64,4,128,128]{3,2,1,0:T(8,128)} %param.15, s32[]{:T(128)} %constant.12.clone.1), dimensions={1,3}, to_apply=%region_0.1 | reduce | flops 4186112 | bytes 16809988 | tf_op jit(solution)/shard_map/reduce_sum | solution.py:41
  84.1 0.6 add_bitcast_fusion
  84.7 4.4 fusion.22
  89.2 13.8 %all-to-all-done = bf16[32,64,192]{2,0,1:T(8,128)(2,1)} async-done(((bf16[32,64,192]{2,0,1:T(8,128)(2,1)}), bf16[32,64,192]{2,0,1:T(8,128)(2,1)}, u32[]{:S(2)}, u32[]{:S(2)}) %all-to-all-start) | async-done | bytes 786464 | tf_op jit(solution)/shard_map/all_to_all | solution.py:39
  103.0 1.8 copy.70
  104.8 2.0 all_to_all.13
  106.8 1.5 copy_bitcast_fusion.1
  108.3 2.2 gather_fusion.1
  110.5 9.3 %fusion.12 = f32[32,64,128]{2,0,1:T(8,128)S(1)} fusion(s32[64,4,128,128]{3,2,1,0:T(8,128)} %param.15, bf16[64,4,32,128]{3,2,1,0:T(8,128)(2,1)} %bitcast.78, pred[64,4]{1,0:T(8,128)(4,1)S(1)} %copy.68), kind=kOutput, calls=%fused_computation.28 | convolution fusion | flops 273678336 | bytes 19923200 | tf_op jit(solution)/shard_map/ftkj,tkij->fti/dot_general | solution.py:12
  119.9 2.7 copy.89
  122.6 6.6 %fusion.4 = bf16[32,8192]{0,1:T(8,128)(2,1)S(1)} fusion(f32[32,64,128]{0,2,1:T(8,128)} %copy.89, f32[8192]{0:T(1024)S(1)} %copy-done.9, f32[8192]{0:T(1024)S(1)} %copy-done.8, bf16[32,8192]{0,1:T(8,128)(2,1)} %copy.67), kind=kLoop, calls=%fused_computation.12 | loop fusion | flops 1835008 | bytes 2162688 | tf_op jit(solution)/shard_map/convert_element_type | solution.py:46
  129.2 1.3 copy-done.3
  130.5 7.9 %fusion = f32[256,8192]{0,1:T(8,128)} fusion(f32[8192,256]{1,0:T(8,128)} %fusion.22, bf16[32,8192]{0,1:T(8,128)(2,1)S(1)} %fusion.4, bf16[32,256]{1,0:T(8,128)(2,1)S(1)} %copy-done), kind=kOutput, calls=%fused_computation.5 | convolution fusion | flops 136314880 | bytes 17317888 | tf_op jit(solution)/shard_map/dot_general | solution.py:51
  138.4 8.9 %copy.92 = f32[256,8192]{1,0:T(8,128)} copy(f32[256,8192]{0,1:T(8,128)} %fusion) | data formatting | bytes 16777216
  147.3 0.3 all-gather.2.cloned.1.call-start
  147.6 0.9 copy-done.6
  148.5 1.8 copy.76
  150.3 77.3 %reduce-scatter.4.cloned.1.call-done = f32[64,8192]{1,0:T(8,128)} async-done(((f32[256,8192]{1,0:T(8,128)}), f32[64,8192]{1,0:T(8,128)}) %reduce-scatter.4.cloned.1.call-update) | async-done | bytes 2097168
  227.7 3.8 copy.93
  231.5 6.0 %convert_reduce_fusion = (f32[64]{0:T(128)}, bf16[64,8192]{0,1:T(8,128)(2,1)}, bf16[64,8192]{0,1:T(8,128)(2,1)}) fusion(f32[64,8192]{0,1:T(8,128)} %copy.93, f32[64]{0:T(128)S(1)} %copy-done.14, bf16[64,8192]{0,1:T(8,128)(2,1)} %copy.76), kind=kLoop, calls=%fused_computation.13 | loop fusion | flops 7864256 | bytes 5243392 | tf_op jit(solution)/shard_map/reduce_sum | solution.py:70
  237.4 2.7 copy.77
  240.2 0.1 reshape.178
  240.3 50.5 %all-gather.2.cloned.1.call-done = bf16[256,8192]{1,0:T(8,128)(2,1)} async-done(((bf16[64,8192]{1,0:T(8,128)(2,1)}), bf16[256,8192]{1,0:T(8,128)(2,1)}) %all-gather.2.cloned.1.call-update) | async-done | bytes 4194320 | tf_op jit(solution)/shard_map/all_gather | solution.py:62
  290.8 3.0 convolution_divide_fusion
  293.8 1.0 copy-done.5
  294.8 0.1 copy.97
  295.0 9.0 %fusion.5 = f32[64,32,4,128]{3,1,2,0:T(8,128)} fusion(s32[64,4,128,128]{3,2,1,0:T(8,128)} %param.15, bf16[32,64,128,1]{2,1,0,3:T(8,128)(2,1)S(1)} %bitcast.80), kind=kOutput, calls=%fused_computation.17 | convolution fusion | flops 272629760 | bytes 21495808 | tf_op jit(solution)/shard_map/fti,tkij->tkfj/dot_general | solution.py:78
  304.0 1.9 broadcast_in_dim.33
  305.9 34.0 %scatter_fusion = f32[160,32,128]{2,1,0:T(8,128)} fusion(f32[160,32,128]{2,1,0:T(8,128)} %broadcast_in_dim.33, s32[256]{0:T(256)S(1)} %reshape.178, f32[256,32,128]{2,1,0:T(8,128)} %bitcast.77), kind=kCustom, calls=%fused_computation.2 | custom fusion | flops 1048576 | bytes 12583936 | tf_op jit(solution)/shard_map/scatter-add | solution.py:82
  339.8 1.9 copy_bitcast_fusion
  341.8 1.5 copy-done.4
  343.3 1.0 slice.17
  344.2 2.3 all_to_all.14
  346.5 1.5 copy.81
  348.1 10.8 %all-to-all-start.1 = ((bf16[32,64,192]{2,0,1:T(8,128)(2,1)}), bf16[32,64,192]{2,0,1:T(8,128)(2,1)}, u32[]{:S(2)}, u32[]{:S(2)}) async-start(bf16[32,64,192]{2,0,1:T(8,128)(2,1)} %copy.81), calls=%async_computation.1 | async-start | bytes 2097152 | tf_op jit(solution)/shard_map/all_to_all | solution.py:90
  358.9 0.3 all-reduce.3.cloned.1.call-start
  359.3 2.7 copy.85
  362.0 3.6 fusion.2
  365.6 2.7 copy.83
  368.4 4.9 fusion.24
  373.3 2.0 fusion.23
  375.3 11.5 %all-to-all-done.1 = bf16[32,64,192]{2,0,1:T(8,128)(2,1)} async-done(((bf16[32,64,192]{2,0,1:T(8,128)(2,1)}), bf16[32,64,192]{2,0,1:T(8,128)(2,1)}, u32[]{:S(2)}, u32[]{:S(2)}) %all-to-all-start.1) | async-done | bytes 786464 | tf_op jit(solution)/shard_map/all_to_all | solution.py:90
  386.8 1.8 copy.82
  388.7 2.0 reshape.157
  390.7 1.5 multiply_bitcast_fusion
  392.2 4.0 copy.84
  396.2 63.5 %scatter_fusion.1 = f32[32,8192]{0,1:T(8,128)} fusion(f32[32,8192]{0,1:T(8,128)} %copy.83, s32[12288]{0:T(1024)S(1)} %bitcast.82, f32[12288,32]{1,0:T(8,128)} %copy.84), kind=kCustom, calls=%fused_computation.3 | custom fusion | flops 393216 | bytes 4767744 | tf_op jit(solution)/shard_map/scatter-add | solution.py:94
  459.7 3.6 copy.86
  463.3 80.9 %all-reduce.3.cloned.1.call-done = (f32[32,256]{1,0:T(8,128)}, f32[32,256]{1,0:T(8,128)}, f32[64]{0:T(128)}) async-done(((f32[32,256]{1,0:T(8,128)}, f32[32,256]{1,0:T(8,128)}, f32[64]{0:T(128)}), (f32[32,256]{1,0:T(8,128)}, f32[32,256]{1,0:T(8,128)}, f32[64]{0:T(128)})) %all-reduce.3.cloned.1.call-update) | async-done | bytes 65808 | tf_op jit(solution)/shard_map/psum | solution.py:71
  544.2 1.4 copy.107
  545.6 1.4 copy.108
  547.0 1.2 copy.109
  (38 shorter events, 0.5 us)
Async XLA Ops:
  7.2 123.4 %copy-start = (bf16[32,256]{1,0:T(8,128)(2,1)S(1)}, bf16[32,256]{1,0:T(8,128)(2,1)}, u32[]{:S(2)}) copy-start(bf16[32,256]{1,0:T(8,128)(2,1)} %param.17) | copy-start | bytes 49156
  13.3 47.2 %copy-start.7 = (s32[1,64,192]{2,1,0:T(8,128)S(1)}, s32[1,64,192]{2,1,0:T(8,128)}, u32[]{:S(2)}) copy-start(s32[1,64,192]{2,1,0:T(8,128)} %param.12) | copy-start | bytes 147460
  13.4 47.1 %copy-start.13 = (s32[1,64]{1,0:T(1,128)S(1)}, s32[1,64]{1,0:T(1,128)}, u32[]{:S(2)}) copy-start(s32[1,64]{1,0:T(1,128)} %param.13) | copy-start | bytes 772
  60.5 16.3 %copy-start.12 = (s32[1,64,4]{1,2,0:T(4,128)S(1)}, s32[1,64,4]{1,2,0:T(4,128)}, u32[]{:S(2)}) copy-start(s32[1,64,4]{1,2,0:T(4,128)} %param.14) | copy-start | bytes 3076
  61.7 41.3 %all-to-all-start = ((bf16[32,64,192]{2,0,1:T(8,128)(2,1)}), bf16[32,64,192]{2,0,1:T(8,128)(2,1)}, u32[]{:S(2)}, u32[]{:S(2)}) async-start(bf16[32,64,192]{2,0,1:T(8,128)(2,1)} %select_multiply_fusion), calls=%async_computation | async-start | bytes 2097152 | tf_op jit(solution)/shard_map/all_to_all | solution.py:39
  75.1 152.6 %reduce-scatter.4.cloned.1.call-start = ((), (), s32[]{:S(2)}) async-start(), calls=%async_computation.4 | async-start | bytes 10485760
  77.1 7.6 %copy-start.10 = (bf16[32,256]{1,0:T(8,128)(2,1)S(1)}, bf16[32,256]{1,0:T(8,128)(2,1)}, u32[]{:S(2)}) copy-start(bf16[32,256]{1,0:T(8,128)(2,1)} %param.16) | copy-start | bytes 49156
  119.9 2.7 copy-start.8
  119.9 2.7 copy-start.9
  129.2 1.3 copy-start.3
  147.3 1.2 copy-start.6
  147.3 84.1 %copy-start.14 = (f32[64]{0:T(128)S(1)}, f32[64]{0:T(128)}, u32[]{:S(2)}) copy-start(f32[64]{0:T(128)} %param.18) | copy-start | bytes 772
  147.3 143.4 %all-gather.2.cloned.1.call-start = ((), (), s32[]{:S(2)}) async-start(), calls=%async_computation.3 | async-start | bytes 5242880 | tf_op jit(solution)/shard_map/all_gather | solution.py:62
  293.8 1.0 copy-start.5
  341.7 1.5 copy-start.4
  344.2 17.8 %copy-start.11 = (bf16[32,256]{1,0:T(8,128)(2,1)S(1)}, bf16[32,256]{1,0:T(8,128)(2,1)}, u32[]{:S(2)}) copy-start(bf16[32,256]{1,0:T(8,128)(2,1)} %param.16) | copy-start | bytes 49156
  348.1 38.8 %all-to-all-start.1 = ((bf16[32,64,192]{2,0,1:T(8,128)(2,1)}), bf16[32,64,192]{2,0,1:T(8,128)(2,1)}, u32[]{:S(2)}, u32[]{:S(2)}) async-start(bf16[32,64,192]{2,0,1:T(8,128)(2,1)} %copy.81), calls=%async_computation.1 | async-start | bytes 2097152 | tf_op jit(solution)/shard_map/all_to_all | solution.py:90
  358.9 185.3 %all-reduce.3.cloned.1.call-start = ((), (), s32[]{:S(2)}) async-start(), calls=%async_computation.5 | async-start | bytes 132096 | tf_op jit(solution)/shard_map/psum | solution.py:71
  368.4 4.9 copy-start.2
  396.2 152.0 %copy-start.1 = (bf16[32,256]{1,0:T(8,128)(2,1)S(1)}, bf16[32,256]{1,0:T(8,128)(2,1)}, u32[]{:S(2)}) copy-start(bf16[32,256]{1,0:T(8,128)(2,1)} %param.17) | copy-start | bytes 49156
Sparse Core Ops, SparseCore 0:
  147.4 80.1 reduce-scatter.3
  240.2 50.5 all-gather.1
  375.4 168.7 all-reduce.2
where the time goes:
time: 556 us; the launch traced here: 555 us
  waiting for transfers between devices  234 us (42%)
  other arithmetic  124 us (22%)
  local copies, waits for them, and re-layouts  113 us (20%)
  matrix products  44.2 us (8%)
  starting transfers between devices  25 us (4%)
  between operations  14 us (3%)
    psum x1, waiting for transfers between devices, per_device(): lax.psum((local_self, local_neighbor, local_bias), 'dom')  80.9 us
    unnamed x4, waiting for transfers between devices  77.4 us
    scatter-add x1, other arithmetic, per_device(): jnp.zeros((feature_count, node_count), jnp.float32).at[:, flat_rows]  63.5 us
    all_gather x1, waiting for transfers between devices, per_device(): slope_full = lax.all_gather(slope, 'feat', axis=0, tiled=True)  50.5 us
    gather x2, local copies, waits for them, and re-layouts, per_device(): outgoing = jnp.take(features, flat_rows, axis=1) * live_slots  47.1 us
    scatter-add x1, other arithmetic, per_device(): jax.ops.segment_sum(contrib.reshape(tile_count * entry_count, feature_cou...  34 us
    unnamed x41, local copies, waits for them, and re-layouts  32.3 us
    all_to_all x1, waiting for transfers between devices, per_device(): lax.all_to_all(outgoing, 'dom', split_axis=1, concat_axis=1, tiled=True)  13.8 us
  transfers between devices with their start and end apart: 5, of which 5 were waited for; matrix products, arithmetic and copies ran while one was open for 20% of the time, Pallas kernels for 0%

commit v1 on v0

v1 whole, which is shorter than its diff:
```python
import functools

import jax
import jax.numpy as jnp
from jax import lax
from jax.experimental import pallas as pl
from jax.experimental.pallas import tpu as pltpu
from jax.sharding import PartitionSpec as P

BF = jnp.bfloat16
F32 = jnp.float32
VMEM = pl.BlockSpec(memory_space=pltpu.VMEM)
SMEM = pl.BlockSpec(memory_space=pltpu.SMEM)
LANES = 128
CHUNK = 512
GROUP = 4


def params(limit=48 << 20, **kw):
    return pltpu.CompilerParams(vmem_limit_bytes=limit, **kw)


def cost(flops, nbytes):
    return pl.CostEstimate(flops=int(flops), bytes_accessed=int(nbytes), transcendentals=0)


def low_half(shape):
    return lax.broadcasted_iota(jnp.int32, shape, len(shape) - 1) < LANES // 2


def split_rest(tile):
    half = tile.shape[0] // 2
    a, b = tile[:half], tile[half:]
    low = low_half(a.shape)
    even = jnp.where(low, a, pltpu.roll(b, LANES // 2, 1))
    odd = jnp.where(low, pltpu.roll(a, LANES // 2, 1), b)
    return even, odd


def join_rest(even, odd):
    low = low_half(even.shape)
    a = jnp.where(low, even, pltpu.roll(odd, LANES // 2, 1))
    b = jnp.where(low, pltpu.roll(even, LANES // 2, 1), odd)
    return jnp.concatenate([a, b], axis=0)


def one_hot_rows(lo):
    rows = lax.broadcasted_iota(jnp.int32, (CHUNK, lo.shape[1]), 0)
    return jnp.where(rows == lo, 1.0, 0.0).astype(BF)


def gather_kernel(me_ref, quantized, scale, idx, feat_tiles, wire, *rest):
    blocks, (folded,) = rest[:4], rest[4:]
    feature_count, node_count = quantized.shape
    fold = node_count // CHUNK
    width = node_count // 4
    me = me_ref[0]
    for c in range(fold):
        at = pl.ds(c * CHUNK, CHUNK)
        part = (quantized[:, at].astype(F32) * scale[:, at]).astype(BF)
        folded[c * feature_count : (c + 1) * feature_count, :] = part
        for t in range(CHUNK // LANES):
            feat_tiles[c * (CHUNK // LANES) + t] = part[:, t * LANES : (t + 1) * LANES]
    per_block = width // CHUNK
    for s in range(4):
        first = lax.rem(me + s, 4) * per_block
        for c in range(per_block):
            src = pl.ds(pl.multiple_of((first + c) * feature_count, feature_count), feature_count)
            blocks[s][:, c * CHUNK : (c + 1) * CHUNK] = folded[src, :]

    def pick(base):
        rows = [idx[pl.ds(base + t, 1), :] for t in range(4)]
        row = jnp.concatenate(rows, axis=1)
        hi, lo = row >> 9, row & (CHUNK - 1)
        out = jnp.dot(folded[...], one_hot_rows(lo), preferred_element_type=F32)
        total = jnp.zeros((feature_count, row.shape[1]), F32)
        for c in range(fold):
            total = total + jnp.where(hi == c, out[c * feature_count : (c + 1) * feature_count], 0.0)
        return [total[:, t * LANES : (t + 1) * LANES] for t in range(4)]

    @pl.loop(0, 16)
    def _(g):
        tiles = pick(g * 4)
        for t in range(4):
            wire[g * 4 + t, 0:feature_count, :] = tiles[t].astype(BF)

    @pl.loop(0, 8)
    def _(g):
        tiles = pick(64 + g * 4)
        for t in range(4):
            even, odd = split_rest(tiles[t])
            wire[(g * 4 + t) * 2, feature_count:48, :] = even.astype(BF)
            wire[(g * 4 + t) * 2 + 1, feature_count:48, :] = odd.astype(BF)


def gather(me, quantized, scale, idx):
    rows, nodes = quantized.shape
    return pl.pallas_call(
        gather_kernel,
        out_shape=[
            jax.ShapeDtypeStruct((nodes // LANES, rows, LANES), BF),
            jax.ShapeDtypeStruct((64, 48, LANES), BF),
        ]
        + [jax.ShapeDtypeStruct((rows, nodes // 4), BF)] * 4,
        in_specs=[SMEM, VMEM, VMEM, VMEM],
        out_specs=[VMEM] * 6,
        scratch_shapes=[pltpu.VMEM((rows * nodes // CHUNK, CHUNK), BF)],
        compiler_params=params(),
        cost_estimate=cost(6.4e9, 4 << 20),
        name="gather_rows",
    )(me, quantized, scale, idx)


def mask_kernel(edges, mask, degree):
    ones = jnp.ones((8, LANES * 4), BF)
    parts = []
    for r in range(GROUP):
        m = edges[r].astype(F32).astype(BF)
        mask[r] = m
        flat = jnp.concatenate([m[k] for k in range(4)], axis=1)
        parts.append(
            lax.dot_general(ones, flat, (((1,), (1,)), ((), ())), preferred_element_type=F32)
        )
    degree[0] = jnp.concatenate(parts, axis=1)


def masks(edges):
    steps = edges.shape[0] // GROUP
    return pl.pallas_call(
        mask_kernel,
        grid=(steps,),
        out_shape=[
            jax.ShapeDtypeStruct(edges.shape, BF),
            jax.ShapeDtypeStruct((steps, 8, GROUP * LANES), F32),
        ],
        in_specs=[pl.BlockSpec((GROUP, 4, LANES, LANES), lambda i: (i, 0, 0, 0))],
        out_specs=[
            pl.BlockSpec((GROUP, 4, LANES, LANES), lambda i: (i, 0, 0, 0)),
            pl.BlockSpec((1, 8, GROUP * LANES), lambda i: (i, 0, 0)),
        ],
        compiler_params=params(),
        cost_estimate=cost(1e9, 24 << 20),
        name="mask_degree",
    )(edges)


def join_kernel(feat_tiles, wire, joined):
    local = feat_tiles.shape[0]
    joined[0:local] = feat_tiles[...]

    @pl.loop(0, 32)
    def _(q):
        even, odd = wire[2 * q], wire[2 * q + 1]
        joined[local + 3 * q] = even[0:32]
        joined[local + 3 * q + 2] = odd[0:32]
        joined[local + 3 * q + 1] = join_rest(even[32:48].astype(F32), odd[32:48].astype(F32)).astype(BF)


def join(feat_tiles, wire):
    count = feat_tiles.shape[0] + 96
    return pl.pallas_call(
        join_kernel,
        out_shape=jax.ShapeDtypeStruct((count,) + feat_tiles.shape[1:], BF),
        in_specs=[VMEM, VMEM],
        out_specs=VMEM,
        compiler_params=params(),
        cost_estimate=cost(1e6, 3 << 20),
        name="join_tiles",
    )(feat_tiles, wire)


def aggregate_kernel(shift, me_ref, cols, joined, mask, degree, out):
    step = pl.program_id(0)
    group = lax.rem(me_ref[0] + shift, 4) * 4 + step
    for r in range(GROUP):
        row = group * GROUP + r
        picked = jnp.concatenate([joined[cols[row, k]] for k in range(4)], axis=1)
        flat = jnp.concatenate([mask[r, k] for k in range(4)], axis=1)
        total = lax.dot_general(
            picked, flat, (((1,), (1,)), ((), ())), preferred_element_type=F32
        )
        own = joined[row].astype(F32)
        below = degree[0, 0:1, r * LANES : (r + 1) * LANES] + 1.0
        out[:, r * LANES : (r + 1) * LANES] = ((total + own) / below).astype(BF)


def aggregate(shift, me, cols, joined, mask, degree):
    rows = joined.shape[1]
    group = lambda i, me_ref, cols_ref: lax.rem(me_ref[0] + shift, 4) * 4 + i
    return pl.pallas_call(
        functools.partial(aggregate_kernel, shift),
        out_shape=jax.ShapeDtypeStruct((rows, 2048), BF),
        grid_spec=pltpu.PrefetchScalarGridSpec(
            num_scalar_prefetch=2,
            grid=(4,),
            in_specs=[
                pl.BlockSpec(joined.shape, lambda i, *_: (0, 0, 0)),
                pl.BlockSpec((GROUP, 4, LANES, LANES), lambda i, *p: (group(i, *p), 0, 0, 0)),
                pl.BlockSpec((1, 8, GROUP * LANES), lambda i, *p: (group(i, *p), 0, 0)),
            ],
            out_specs=pl.BlockSpec((rows, GROUP * LANES), lambda i, *_: (0, i)),
        ),
        compiler_params=params(),
        cost_estimate=cost(1e8, 4 << 20),
        name="aggregate",
    )(me, cols, joined, mask, degree)


def dense_kernel(me_ref, *refs):
    feats, aggs, ups = refs[0:4], refs[4:8], refs[8:12]
    self_w, neighbor_w, self_t, neighbor_t, bias, degree = refs[12:18]
    hiddens, means, sums, grads = refs[18:22], refs[22:26], refs[26:30], refs[30:34]
    both, up, slope_s, hid_s, mean_s, sum_s, grad_s = refs[34:]
    me = me_ref[0]
    step = pl.program_id(0)
    width = feats[0].shape[1]

    def block(s, size):
        return pl.ds(pl.multiple_of(lax.rem(me + 4 - s, 4) * size, size), size)

    for s in range(4):
        both[block(s, 32), :] = feats[s][...]
        at = pl.ds(pl.multiple_of(128 + lax.rem(me + 4 - s, 4) * 32, 32), 32)
        both[at, :] = aggs[s][...]
        up[block(s, 64), :] = ups[s][...]
    both[256:272, :] = jnp.ones((16, width), BF)
    preact = (
        jnp.dot(self_t[...], both[0:128, :], preferred_element_type=F32)
        + jnp.dot(neighbor_t[...], both[128:256, :], preferred_element_type=F32)
        + bias[...]
    )
    sig = jax.nn.sigmoid(preact)
    hid_s[...] = (preact * sig).astype(BF)
    slope = (up[...].astype(F32) * sig * (1.0 + preact * (1.0 - sig))).astype(BF)
    slope_s[...] = slope
    below = degree[me * 4 + step, 0:1, :] + 1.0
    mean = jnp.dot(neighbor_w[...], slope, preferred_element_type=F32) / below
    mean_s[...] = mean.astype(BF)
    sum_s[...] = (jnp.dot(self_w[...], slope, preferred_element_type=F32) + mean).astype(BF)
    for s in range(4):
        hiddens[s][...] = hid_s[block(s, 64), :]
        means[s][...] = mean_s[block(s, 32), :]
        sums[s][...] = sum_s[block(s, 32), :]
    part = lax.dot_general(
        both[...], slope, (((1,), (1,)), ((), ())), preferred_element_type=F32
    )

    @pl.when(step == 0)
    def _():
        grad_s[...] = part

    @pl.when(step > 0)
    def _():
        grad_s[...] += part

    @pl.when(step == pl.num_programs(0) - 1)
    def _():
        for s in range(4):
            grads[s][0:32, :] = grad_s[block(s, 32), :]
            at = pl.ds(pl.multiple_of(128 + lax.rem(me + 4 - s, 4) * 32, 32), 32)
            grads[s][32:64, :] = grad_s[at, :]
            grads[s][64:72, :] = grad_s[256:264, :]


def dense(me, feats, aggs, ups, weights, bias, degree):
    width = 512
    steps = feats[0].shape[1] // width
    narrow = lambda rows: pl.BlockSpec((rows, width), lambda i: (0, i))
    whole = lambda a: pl.BlockSpec(a.shape, lambda i: (0,) * a.ndim)
    nodes = feats[0].shape[1]
    out = lambda rows: [jax.ShapeDtypeStruct((rows, nodes), BF)] * 4
    got = pl.pallas_call(
        dense_kernel,
        grid=(steps,),
        out_shape=out(64) + out(32) + out(32) + [jax.ShapeDtypeStruct((72, 256), F32)] * 4,
        in_specs=[SMEM]
        + [narrow(32)] * 8
        + [narrow(64)] * 4
        + [whole(w) for w in weights]
        + [whole(bias), whole(degree)],
        out_specs=[narrow(64)] * 4
        + [narrow(32)] * 8
        + [pl.BlockSpec((72, 256), lambda i: (0, 0))] * 4,
        scratch_shapes=[
            pltpu.VMEM((272, width), BF),
            pltpu.VMEM((256, width), BF),
            pltpu.VMEM((256, width), BF),
            pltpu.VMEM((256, width), BF),
            pltpu.VMEM((128, width), BF),
            pltpu.VMEM((128, width), BF),
            pltpu.VMEM((272, 256), F32),
        ],
        compiler_params=params(),
        cost_estimate=cost(1e9, 6 << 20),
        name="dense",
    )(me, *feats, *aggs, *ups, *weights, bias, degree)
    return got[0:4], got[4:8], got[8:12], got[12:16]


def spread_kernel(me_ref, cols, *refs):
    means, mask, local, wire, mean_s, total = refs[0:4], refs[4], refs[5], refs[6], refs[7], refs[8]
    step = pl.program_id(0)
    me = me_ref[0]

    @pl.when(step == 0)
    def _():
        total[...] = jnp.zeros(total.shape, F32)
        for s in range(4):
            first = lax.rem(me + s, 4) * 16
            for t in range(16):
                mean_s[first + t] = means[s][:, t * LANES : (t + 1) * LANES]

    for r in range(GROUP):
        row = step * GROUP + r
        flat = jnp.concatenate([mask[r, k] for k in range(4)], axis=1)
        part = jnp.dot(mean_s[row], flat, preferred_element_type=F32)
        for k in range(4):
            at = cols[row, k]
            total[at] = total[at] + part[:, k * LANES : (k + 1) * LANES]

    @pl.when(step == pl.num_programs(0) - 1)
    def _():
        local[...] = total[0:64]

        @pl.loop(0, 32)
        def _(q):
            wire[2 * q, 0:32, :] = total[64 + 3 * q].astype(BF)
            wire[2 * q + 1, 0:32, :] = total[64 + 3 * q + 2].astype(BF)
            even, odd = split_rest(total[64 + 3 * q + 1])
            wire[2 * q, 32:48, :] = even.astype(BF)
            wire[2 * q + 1, 32:48, :] = odd.astype(BF)
            wire[2 * q, 48:56, :] = jnp.zeros((8, LANES), BF)
            wire[2 * q + 1, 48:56, :] = jnp.zeros((8, LANES), BF)


def spread(me, cols, means, mask):
    whole = lambda shape: pl.BlockSpec(shape, lambda i, *_: (0,) * len(shape))
    rows = means[0].shape[0]
    return pl.pallas_call(
        spread_kernel,
        out_shape=[
            jax.ShapeDtypeStruct((64, rows, LANES), F32),
            jax.ShapeDtypeStruct((64, 56, LANES), BF),
        ],
        grid_spec=pltpu.PrefetchScalarGridSpec(
            num_scalar_prefetch=2,
            grid=(mask.shape[0] // GROUP,),
            in_specs=[whole(means[0].shape)] * 4
            + [pl.BlockSpec((GROUP, 4, LANES, LANES), lambda i, *_: (i, 0, 0, 0))],
            out_specs=[whole((64, rows, LANES)), whole((64, 56, LANES))],
            scratch_shapes=[
                pltpu.VMEM((64, rows, LANES), BF),
                pltpu.VMEM((160, rows, LANES), F32),
            ],
        ),
        compiler_params=params(),
        cost_estimate=cost(5e8, 12 << 20),
        name="spread",
    )(me, cols, *means, mask)


def scatter_kernel(me_ref, idx, wire, local, *refs):
    sums, out, ret, acc = refs[0:4], refs[4], refs[5], refs[6]
    me = me_ref[0]
    fold = local.shape[0] * LANES // CHUNK

    @pl.loop(0, 32)
    def _(q):
        even, odd = wire[2 * q], wire[2 * q + 1]
        ret[2 * q] = even[0:32].astype(F32)
        ret[2 * q + 1] = odd[0:32].astype(F32)
        ret[64 + q] = join_rest(even[32:48].astype(F32), odd[32:48].astype(F32))

    acc[...] = jnp.zeros(acc.shape, F32)

    @pl.loop(0, 12)
    def _(g):
        row = jnp.concatenate([idx[pl.ds(g * 8 + t, 1), :] for t in range(8)], axis=1)
        hi, lo = row >> 9, row & (CHUNK - 1)
        value = jnp.concatenate([ret[g * 8 + t] for t in range(8)], axis=1)
        folded = jnp.concatenate(
            [jnp.where(hi == c, value, 0.0).astype(BF) for c in range(fold)], axis=0
        )
        acc[...] += lax.dot_general(
            folded, one_hot_rows(lo), (((1,), (1,)), ((), ())), preferred_element_type=F32
        )

    for c in range(fold):
        tiles = [local[c * 4 + t] for t in range(4)]
        out[:, c * CHUNK : (c + 1) * CHUNK] = acc[c * 32 : (c + 1) * 32, :] + jnp.concatenate(
            tiles, axis=1
        )
    for s in range(4):
        at = pl.ds(pl.multiple_of(lax.rem(me + s, 4) * 2048, 2048), 2048)
        out[:, at] = out[:, at] + sums[s][...].astype(F32)


def scatter(me, idx, wire, local, sums):
    rows = sums[0].shape[0]
    return pl.pallas_call(
        scatter_kernel,
        out_shape=jax.ShapeDtypeStruct((rows, 8192), F32),
        in_specs=[SMEM] + [VMEM] * 7,
        out_specs=VMEM,
        scratch_shapes=[
            pltpu.VMEM((96, rows, LANES), F32),
            pltpu.VMEM((rows * 16, CHUNK), F32),
        ],
        compiler_params=params(),
        cost_estimate=cost(6.4e9, 5 << 20),
        name="scatter_rows",
    )(me, idx, wire, local, *sums)


def place_kernel(me_ref, a, b, c, d, out):
    for s, piece in enumerate((a, b, c, d)):
        at = pl.ds(pl.multiple_of(lax.rem(me_ref[0] + s, 4) * 2048, 2048), 2048)
        out[:, at] = piece[...]


def place(me, pieces):
    rows = pieces[0].shape[0]
    return pl.pallas_call(
        place_kernel,
        out_shape=jax.ShapeDtypeStruct((rows, 8192), BF),
        in_specs=[SMEM] + [VMEM] * 4,
        out_specs=VMEM,
        compiler_params=params(),
        cost_estimate=cost(1e6, 2 << 20),
        name="place",
    )(me, *pieces)


def exchange(pieces, sign):
    got = [pieces[0]]
    for s in range(1, 4):
        got.append(lax.ppermute(pieces[s], "feat", [(q, (q + sign * s) % 4) for q in range(4)]))
    return got


def per_device(
    quantized,
    node_scale,
    send_rows,
    send_count,
    tile_cols,
    edge_tiles,
    self_weight,
    neighbor_weight,
    hidden_bias,
    upstream,
):
    feat = lax.axis_index("feat")
    dom = lax.axis_index("dom")
    me = feat.astype(jnp.int32).reshape(1)
    cols = tile_cols[0]

    slot = lax.broadcasted_iota(jnp.int32, (64, 192), 1)
    rows = jnp.where(slot < send_count[0][:, None], send_rows[0], -1)
    turned = jnp.concatenate([rows[:, 64:], rows[:, :64]], axis=1)
    rows = jnp.where(dom % 2 == 1, turned, rows)
    idx = jnp.concatenate([rows[:, :128], rows[:, 128:].reshape(32, 128)], axis=0)

    feat_tiles, wire, *feat_blocks = gather(me, quantized, node_scale.reshape(1, -1), idx)
    halo = lax.all_to_all(wire, "dom", split_axis=0, concat_axis=0, tiled=True)

    feats = exchange(feat_blocks, 1)
    up_blocks = [
        lax.dynamic_slice_in_dim(upstream, lax.rem(feat + s, 4) * 2048, 2048, axis=1)
        for s in range(4)
    ]
    ups = exchange(up_blocks, 1)
    small = jnp.concatenate(
        [
            self_weight.astype(F32),
            neighbor_weight.astype(F32),
            jnp.broadcast_to(jnp.pad(hidden_bias, (0, 192))[None, :], (8, 256)),
        ],
        axis=0,
    )
    small = lax.all_gather(small, "feat", axis=0)
    self_w = small[:, 0:32].reshape(128, 256).astype(BF)
    neighbor_w = small[:, 32:64].reshape(128, 256).astype(BF)
    bias = small[:, 64, 0:64].reshape(256, 1)
    weights = [self_w, neighbor_w, self_w.T, neighbor_w.T]

    mask, degree = masks(edge_tiles)
    joined = join(feat_tiles, halo)
    aggs = [None] * 4
    for s in (2, 1, 3, 0):
        aggs[s] = aggregate(s, me, cols, joined, mask, degree)
    aggs = exchange(aggs, 1)
    hiddens, means, sums, grads = dense(me, feats, aggs, ups, weights, bias, degree)
    means = exchange(means, -1)
    grads = exchange(grads, -1)
    means, hiddens, sums = lax.optimization_barrier((means, hiddens, sums))
    local, back = spread(me, cols, means, mask)

    grad = grads[0] + grads[1] + grads[2] + grads[3]
    flat = jnp.concatenate(
        [
            grad[0:64].reshape(2, 64, 128).transpose(1, 0, 2),
            jnp.pad(grad[64].reshape(64, 1, 4), ((0, 0), (0, 0), (0, 124))),
        ],
        axis=1,
    )
    high = flat.astype(BF)
    lower = (flat - high.astype(F32)).astype(BF)
    packed = jnp.concatenate([high, lower, jnp.zeros((64, 2, 128), BF)], axis=1)
    back = back.at[:, 48:56].set(packed)
    returned = lax.all_to_all(back, "dom", split_axis=0, concat_axis=0, tiled=True)

    hidden = place(me, exchange(hiddens, -1))
    sums = exchange(sums, -1)

    arrived = jnp.sum(returned[:, 48:56].astype(F32), axis=0)
    final = jnp.pad(arrived[0:3] + arrived[3:6], ((0, 5), (0, 0)))
    everyone = lax.all_to_all(
        jnp.broadcast_to(final[None], (64, 8, 128)), "dom", split_axis=0, concat_axis=0, tiled=True
    )
    grad_self = everyone[:, 0].reshape(32, 256)
    grad_neighbor = everyone[:, 1].reshape(32, 256)
    grad_bias = lax.dynamic_slice_in_dim(everyone[:, 2, 0:4].reshape(256), feat * 64, 64)
    grad_features = scatter(me, idx, returned, local, sums)
    return hidden, grad_features, grad_self, grad_neighbor, grad_bias


def solution(mesh):
    return jax.shard_map(
        per_device,
        mesh=mesh,
        in_specs=(
            P("feat", "dom"),
            P("dom"),
            P("dom", None, None),
            P("dom", None),
            P("dom", None, None),
            P("dom", None, None, None),
            P("feat", None),
            P("feat", None),
            P("feat"),
            P("feat", "dom"),
        ),
        out_specs=(P("feat", "dom"), P("feat", "dom"), P("feat", None), P("feat", None), P("feat")),
        check_vma=False,
    )
```

time: 556 us -> 201 us (0.36)
  waiting for transfers between devices: 234 us -> 19.7 us
  other arithmetic: 124 us -> 3.72 us
  local copies, waits for them, and re-layouts: 113 us -> 14.9 us
  Pallas kernels: 0 us -> 79.1 us
  matrix products: 44.2 us -> 0 us
  starting transfers between devices: 25 us -> 62 us
  blocking collectives: 0 us -> 18.6 us
  between operations: 14 us -> 1.07 us
    scatter-add x2 -> x0, other arithmetic: 97.5 us -> none  [the longest x1 63.5 us: per_device(): jnp.zeros((feature_count, node_count), jnp.float32).at[:, flat_rows]]
    psum x1 -> x0, waiting for transfers between devices: 80.9 us -> none  [per_device(): lax.psum((local_self, local_neighbor, local_bias), 'dom')]
    pallas_call x0 -> x11, Pallas kernels: none -> 79.1 us  [the longest x4 16.6 us: aggregate(): pl.pallas_call(functools.partial(aggregate_kernel, shift), out_shape=jax....]
    unnamed x4 -> x0, waiting for transfers between devices: 77.4 us -> none
    all_gather x1 -> x0, waiting for transfers between devices: 50.5 us -> none  [per_device(): slope_full = lax.all_gather(slope, 'feat', axis=0, tiled=True)]
    gather x3 -> x0, local copies, waits for them, and re-layouts: 49.3 us -> none  [the longest x2 47.1 us: per_device(): outgoing = jnp.take(features, flat_rows, axis=1) * live_slots]
    dot_general x8 -> x0, matrix products: 44.2 us -> none  [the longest x1 9.32 us: tile_sum(): jnp.einsum('ftkj,tkij->fti', picked, mask_tiles, preferred_element_type=j...]
    ppermute x0 -> x21, starting transfers between devices: none -> 26.7 us  [exchange(): lax.ppermute(pieces[s], 'feat', [(q, (q + sign * s) % 4) for q in range(4)])]
  transfers between devices with their start and end apart: 5 -> 24, of which waited for: 5 -> 7; matrix products, arithmetic and copies ran while one was open for 20% -> 2% of each run, Pallas kernels for 0% -> 23%
where the time goes in v1:
time: 201 us; the launch traced here: 199 us
  Pallas kernels  79.1 us (39%)
  starting transfers between devices  62 us (31%)
  waiting for transfers between devices  19.7 us (10%)
  blocking collectives  18.6 us (9%)
  local copies, waits for them, and re-layouts  14.9 us (7%)
  other arithmetic  3.72 us (2%)
    ppermute x21, starting transfers between devices, exchange(): lax.ppermute(pieces[s], 'feat', [(q, (q + sign * s) % 4) for q in range(4)])  26.7 us
    all_gather x1, blocking collectives, per_device(): small = lax.all_gather(small, 'feat', axis=0)  18.6 us
    pallas_call x4, Pallas kernels, aggregate(): pl.pallas_call(functools.partial(aggregate_kernel, shift), out_shape=jax....  16.6 us
    all_to_all x1, starting transfers between devices, per_device(): lax.all_to_all(back, 'dom', split_axis=0, concat_axis=0, tiled=True)  15.7 us
    pallas_call x1, Pallas kernels, spread(): pl.pallas_call(spread_kernel, out_shape=[jax.ShapeDtypeStruct((64, rows,...  15.5 us
    ppermute x21, waiting for transfers between devices, exchange(): lax.ppermute(pieces[s], 'feat', [(q, (q + sign * s) % 4) for q in range(4)])  14.2 us
    pallas_call x1, Pallas kernels, masks(): pl.pallas_call(mask_kernel, grid=(steps,), out_shape=[jax.ShapeDtypeStruc...  13.8 us
    all_to_all x1, starting transfers between devices, per_device(): halo = lax.all_to_all(wire, 'dom', split_axis=0, concat_axis=0, tiled=True)  13.1 us
  transfers between devices with their start and end apart: 24, of which 7 were waited for; matrix products, arithmetic and copies ran while one was open for 2% of the time, Pallas kernels for 23%

profile of v1, /device:TPU:1, one launch (start us, length us, event | category | flops | bytes accessed | tf_op | source)
XLA Modules:
  0.0 199.1 jit_solution(1547627161300816236)
XLA Ops:
  0.6 0.9 bitcast_select_fusion
  1.6 0.9 add_select_fusion
  2.7 1.0 copy-done.2
  3.7 0.8 copy-done.16
  4.5 12.3 %gather_rows.1 = (bf16[64,32,128]{2,1,0:T(8,128)(2,1)S(1)}, bf16[64,48,128]{2,1,0:T(8,128)(2,1)}, bf16[32,2048]{1,0:T(8,128)(2,1)S(1)}, bf16[32,2048]{1,0:T(8,12...) custom-call(s32[1]{0:T(128)} %bitcast.me_ref, bf16[32,8192]{1,0:T(8,128)(2,1)S(1)} %copy-done.2, ...), custom_call_target="tpu_custom_call" | custom-call | flops 6400000000 | bytes 4194304 | tf_op jit(solution)/shard_map/gather_rows/pallas_call | solution.py:98
  16.8 0.6 copy-done.17
  17.5 13.1 %all-to-all-start = ((bf16[64,48,128]{2,1,0:T(8,128)(2,1)}), bf16[64,48,128]{2,1,0:T(8,128)(2,1)S(1)}, u32[]{:S(2)}, u32[]{:S(2)}) async-start(bf16[64,48,128]{2,1,0:T(8,128)(2,1)} %get-tuple-element.60), calls=%async_computation | async-start | bytes 1572864 | tf_op jit(solution)/shard_map/all_to_all | solution.py:465
  30.6 1.3 collective-permute-start
  31.9 2.4 %collective-permute-start.1 = (bf16[32,2048]{1,0:T(8,128)(2,1)}, bf16[32,2048]{1,0:T(8,128)(2,1)}, u32[]{:S(2)}, u32[]{:S(2)}) collective-permute-start(bf16[32,2048]{1,0:T(8,128)(2,1)} %get-tuple-element.57), channel_id=1, source_target_pairs={{0,2},{1,3},{2,0},{3,1},{4,6},{5,7},{6,4},{7,5},{8,10},{9,11},{10,... | collective-permute-start | bytes 393224 | tf_op jit(solution)/shard_map/ppermute | solution.py:437
  34.4 1.2 collective-permute-start.2
  35.5 0.9 constant_dynamic-slice_fusion
  36.4 0.3 collective-permute-start.6
  36.7 0.9 collective-permute-start.7
  37.7 18.6 %all-gather = f32[288,256]{1,0:T(8,128)S(1)} all-gather(f32[72,256]{1,0:T(8,128)S(1)} %pad_maximum_fusion), channel_id=2, replica_groups=mesh['dom'=64,'feat'=4] {'feat'}, dimensions={0}, use_global_device_ids=true | all-gather | bytes 368640 | tf_op jit(solution)/shard_map/all_gather | solution.py:481
  56.4 0.7 convert.4
  57.1 13.8 %mask_degree.1 = (bf16[64,4,128,128]{3,2,1,0:T(8,128)(2,1)}, f32[16,8,512]{2,1,0:T(8,128)S(1)}) custom-call(s32[64,4,128,128]{3,2,1,0:T(8,128)} %edges.1), custom_call_target="tpu_custom_call" | custom-call | flops 1000000000 | bytes 25165824 | tf_op jit(solution)/shard_map/mask_degree/pallas_call | solution.py:129
  70.9 2.4 %join_tiles.1.joined = bf16[160,32,128]{2,1,0:T(8,128)(2,1)S(1)} custom-call(bf16[64,32,128]{2,1,0:T(8,128)(2,1)S(1)} %get-tuple-element.59.feat_tiles, bf16[64,48,128]{2,1,0:T(8,128)(2,1)S(1)} %all-to-all-done.wire), custom_call_target="tpu_custom_call" | custom-call | flops 1000000 | bytes 3145728 | tf_op jit(solution)/shard_map/join_tiles/pallas_call | solution.py:161
  73.4 4.2 %aggregate.7 = bf16[32,2048]{1,0:T(8,128)(2,1)S(1)} custom-call(s32[1]{0:T(128)} %bitcast.me_ref, s32[64,4]{1,0:T(8,128)S(1)} %bitcast.17, bf16[160,32,128]{2,1,0:T(8,128)(2,1)S(1)} %join_tiles.1.joined, bf16[64,4,128,128]{3,2,1,0:T(8,128)(2,1)} %get-tuple-element.61.mask.refs_4_, f32[16,8,512]{2,1,0:T(8,128)S(1)} %get-tuple-element.62.degree.refs_17_), custom_call_target="tpu_custom_call" | custom-call | flops 100000000 | bytes 4194304 | tf_op jit(solution)/shard_map/aggregate/pallas_call | solution.py:190
  77.6 4.1 %aggregate.6 = bf16[32,2048]{1,0:T(8,128)(2,1)S(1)} custom-call(s32[1]{0:T(128)} %bitcast.me_ref, s32[64,4]{1,0:T(8,128)S(1)} %bitcast.18, bf16[160,32,128]{2,1,0:T(8,128)(2,1)S(1)} %join_tiles.1.joined, bf16[64,4,128,128]{3,2,1,0:T(8,128)(2,1)} %get-tuple-element.61.mask.refs_4_, f32[16,8,512]{2,1,0:T(8,128)S(1)} %get-tuple-element.62.degree.refs_17_), custom_call_target="tpu_custom_call" | custom-call | flops 100000000 | bytes 4194304 | tf_op jit(solution)/shard_map/aggregate/pallas_call | solution.py:190
  81.7 4.1 %aggregate.5 = bf16[32,2048]{1,0:T(8,128)(2,1)S(1)} custom-call(s32[1]{0:T(128)} %bitcast.me_ref, s32[64,4]{1,0:T(8,128)S(1)} %bitcast.19, bf16[160,32,128]{2,1,0:T(8,128)(2,1)S(1)} %join_tiles.1.joined, bf16[64,4,128,128]{3,2,1,0:T(8,128)(2,1)} %get-tuple-element.61.mask.refs_4_, f32[16,8,512]{2,1,0:T(8,128)S(1)} %get-tuple-element.62.degree.refs_17_), custom_call_target="tpu_custom_call" | custom-call | flops 100000000 | bytes 4194304 | tf_op jit(solution)/shard_map/aggregate/pallas_call | solution.py:190
  85.9 2.1 %collective-permute-start.8 = (bf16[64,2048]{1,0:T(8,128)(2,1)}, bf16[64,2048]{1,0:T(8,128)(2,1)S(1)}, u32[]{:S(2)}, u32[]{:S(2)}) collective-permute-start(bf16[64,2048]{1,0:T(8,128)(2,1)} %get-tuple-element.95), channel_id=1, source_target_pairs={{0,3},{1,0},{2,1},{3,2},{4,7},{5,4},{6,5},{7,6},{8,11},{9,8},{10,9... | collective-permute-start | bytes 786440 | tf_op jit(solution)/shard_map/ppermute | solution.py:437
  88.1 1.1 collective-permute-start.4
  89.2 0.3 collective-permute-start.3
  89.7 0.1 copy.28
  89.8 0.7 slice_reduce_fusion.3
  90.5 0.1 reshape_squeeze.20.refs_16_
  90.7 4.1 %aggregate.4.refs_4_ = bf16[32,2048]{1,0:T(8,128)(2,1)S(1)} custom-call(s32[1]{0:T(128)} %bitcast.me_ref, s32[64,4]{1,0:T(8,128)S(1)} %bitcast.20, bf16[160,32,128]{2,1,0:T(8,128)(2,1)S(1)} %join_tiles.1.joined, bf16[64,4,128,128]{3,2,1,0:T(8,128)(2,1)} %get-tuple-element.61.mask.refs_4_, f32[16,8,512]{2,1,0:T(8,128)S(1)} %get-tuple-element.62.degree.refs_17_), custom_call_target="tpu_custom_call" | custom-call | flops 100000000 | bytes 4194304 | tf_op jit(solution)/shard_map/aggregate/pallas_call | solution.py:190
  94.8 0.5 collective-permute-done.5.refs_7_
  95.3 0.6 copy-done.12
  96.0 0.7 copy-done.14
  96.7 0.9 copy-done.6
  97.6 0.9 copy-done.13
  98.5 0.9 copy-done.15
  99.4 4.8 %dense.1 = (bf16[64,2048]{1,0:T(8,128)(2,1)S(1)}, bf16[64,2048]{1,0:T(8,128)(2,1)S(1)}, bf16[64,2048]{1,0:T(8,128)(2,1)S(1)}, bf16[64,2048]{1,0:T(8,128)(2,1)S(1...) custom-call(s32[1]{0:T(128)} %bitcast.me_ref, ...), custom_call_target="tpu_custom_call" | custom-call | flops 1000000000 | bytes 6291456 | tf_op jit(solution)/shard_map/dense/pallas_call | solution.py:272
  104.2 0.6 copy-done.9
  104.9 3.7 %collective-permute-start.15 = (f32[72,256]{1,0:T(8,128)S(1)}, f32[72,256]{1,0:T(8,128)S(1)}, u32[]{:S(2)}, u32[]{:S(2)}) collective-permute-start(f32[72,256]{1,0:T(8,128)S(1)} %get-tuple-element.85), channel_id=1, source_target_pairs={{0,3},{1,0},{2,1},{3,2},{4,7},{5,4},{6,5},{7,6},{8,11},{9,8},{10,9... | collective-permute-start | bytes 221192 | tf_op jit(solution)/shard_map/ppermute | solution.py:437
  108.5 0.7 collective-permute-start.17
  109.3 2.3 %collective-permute-start.10 = (bf16[32,2048]{1,0:T(8,128)(2,1)S(1)}, bf16[32,2048]{1,0:T(8,128)(2,1)S(1)}, u32[]{:S(2)}, u32[]{:S(2)}) collective-permute-start(bf16[32,2048]{1,0:T(8,128)(2,1)S(1)} %get-tuple-element.65), channel_id=1, source_target_pairs={{0,2},{1,3},{2,0},{3,1},{4,6},{5,7},{6,4},{7,5},{8,10},{9,11},{10,... | collective-permute-start | bytes 393224 | tf_op jit(solution)/shard_map/ppermute | solution.py:437
  111.6 0.3 collective-permute-start.11
  111.9 2.4 %collective-permute-start.9 = (bf16[32,2048]{1,0:T(8,128)(2,1)S(1)}, bf16[32,2048]{1,0:T(8,128)(2,1)S(1)}, u32[]{:S(2)}, u32[]{:S(2)}) collective-permute-start(bf16[32,2048]{1,0:T(8,128)(2,1)S(1)} %get-tuple-element.64), channel_id=1, source_target_pairs={{0,3},{1,0},{2,1},{3,2},{4,7},{5,4},{6,5},{7,6},{8,11},{9,8},{10,9... | collective-permute-start | bytes 393224 | tf_op jit(solution)/shard_map/ppermute | solution.py:437
  114.8 0.7 collective-permute-done.10.refs_2_
  115.5 1.4 collective-permute-done.11.refs_3_
  116.9 0.5 collective-permute-done.9.refs_1_
  117.3 15.5 %spread.1 = (f32[64,32,128]{2,1,0:T(8,128)S(1)}, bf16[64,56,128]{2,1,0:T(8,128)(2,1)}) custom-call(s32[1]{0:T(128)} %bitcast.me_ref, s32[64,4]{1,0:T(8,128)S(1)} %bitcast.21, bf16[32,2048]{1,0:T(8,128)(2,1)S(1)} %get-tuple-element.79.refs_0_, bf16[32,2048]{1,0:T(8,128)(2,1)S(1)} %collective-permute-done.9.refs_1_, ...), custom_call_target="tpu_custom_call" | custom-call | flops 500000000 | bytes 12582912 | tf_op jit(solution)/shard_map/spread/pallas_call | solution.py:339
  132.8 0.9 maximum_dynamic-update-slice_fusion
  133.7 0.1 copy-done
  133.8 15.7 %all-to-all-start.1 = ((bf16[64,56,128]{2,1,0:T(8,128)(2,1)}), bf16[64,56,128]{2,1,0:T(8,128)(2,1)S(1)}, u32[]{:S(2)}, u32[]{:S(2)}) async-start(bf16[64,56,128]{2,1,0:T(8,128)(2,1)} %maximum_dynamic-update-slice_fusion), calls=%async_computation.1 | async-start | bytes 1835008 | tf_op jit(solution)/shard_map/all_to_all | solution.py:511
  149.5 3.2 %collective-permute-start.12 = (bf16[64,2048]{1,0:T(8,128)(2,1)S(1)}, bf16[64,2048]{1,0:T(8,128)(2,1)S(1)}, u32[]{:S(2)}, u32[]{:S(2)}) collective-permute-start(bf16[64,2048]{1,0:T(8,128)(2,1)S(1)} %copy-done.4), channel_id=1, source_target_pairs={{0,3},{1,0},{2,1},{3,2},{4,7},{5,4},{6,5},{7,6},{8,11},{9,8},{10,9... | collective-permute-start | bytes 786440 | tf_op jit(solution)/shard_map/ppermute | solution.py:437
  152.8 0.6 collective-permute-start.14
  153.4 2.1 %collective-permute-start.18 = (bf16[32,2048]{1,0:T(8,128)(2,1)}, bf16[32,2048]{1,0:T(8,128)(2,1)S(1)}, u32[]{:S(2)}, u32[]{:S(2)}) collective-permute-start(bf16[32,2048]{1,0:T(8,128)(2,1)} %copy-done.11), channel_id=1, source_target_pairs={{0,3},{1,0},{2,1},{3,2},{4,7},{5,4},{6,5},{7,6},{8,11},{9,8},{10,9... | collective-permute-start | bytes 393224 | tf_op jit(solution)/shard_map/ppermute | solution.py:437
  155.5 1.7 collective-permute-start.19
  157.1 6.0 %collective-permute-done.12.b = bf16[64,2048]{1,0:T(8,128)(2,1)S(1)} collective-permute-done((bf16[64,2048]{1,0:T(8,128)(2,1)S(1)}, bf16[64,2048]{1,0:T(8,128)(2,1)S(1)}, u32[]{:S(2)}, u32[]{:S(2)}) %collective-permute-start.12) | collective-permute-done | bytes 262176 | tf_op jit(solution)/shard_map/ppermute | solution.py:437
  163.1 5.1 %collective-permute-done.14.d = bf16[64,2048]{1,0:T(8,128)(2,1)S(1)} collective-permute-done((bf16[64,2048]{1,0:T(8,128)(2,1)S(1)}, bf16[64,2048]{1,0:T(8,128)(2,1)S(1)}, u32[]{:S(2)}, u32[]{:S(2)}) %collective-permute-start.14) | collective-permute-done | bytes 262176 | tf_op jit(solution)/shard_map/ppermute | solution.py:437
  168.2 1.0 place.1
  169.3 5.6 %all-to-all-done.1.wire = bf16[64,56,128]{2,1,0:T(8,128)(2,1)S(1)} async-done(((bf16[64,56,128]{2,1,0:T(8,128)(2,1)}), bf16[64,56,128]{2,1,0:T(8,128)(2,1)S(1)}, u32[]{:S(2)}, u32[]{:S(2)}) %all-to-all-start.1) | async-done | bytes 917536 | tf_op jit(solution)/shard_map/all_to_all | solution.py:511
  174.9 0.7 broadcast_in_dim.22
  175.6 6.5 %all-to-all-start.2 = ((f32[64,8,128]{2,1,0:T(8,128)}), f32[64,8,128]{2,1,0:T(8,128)S(1)}, u32[]{:S(2)}, u32[]{:S(2)}) async-start(f32[64,8,128]{2,1,0:T(8,128)} %broadcast_in_dim.22), calls=%async_computation.2 | async-start | bytes 524288 | tf_op jit(solution)/shard_map/all_to_all | solution.py:518
  182.1 1.2 copy-done.1
  183.4 0.9 copy-done.20
  184.3 12.6 %scatter_rows.1 = f32[32,8192]{1,0:T(8,128)} custom-call(s32[1]{0:T(128)} %bitcast.me_ref, s32[96,128]{1,0:T(8,128)S(1)} %pad_add_fusion.idx, bf16[64,56,128]{2,1,0:T(8,128)(2,1)S(1)} %all-to-all-done.1.wire, f32[64,32,128]{2,1,0:T(8,128)S(1)} %copy-done.1, bf16[32,2048]{1,0:T(8,128)(2,1)S(1)} %copy-done.20, ...), custom_call_target="tpu_custom_call" | custom-call | flops 6400000000 | bytes 5242880 | tf_op jit(solution)/shard_map/scatter_rows/pallas_call | solution.py:400
  196.9 0.2 slice_reduce_fusion.1
  197.1 0.6 reshape_squeeze.17
  197.7 0.6 reshape_squeeze.18
  198.5 0.6 dynamic_slice.19
  (94 shorter events, 1.5 us)
Async XLA Ops:
  2.7 1.0 copy-start.2
  3.7 0.8 copy-start.16
  4.5 31.1 %copy-start.22 = (bf16[64,8192]{1,0:T(8,128)(2,1)S(1)}, bf16[64,8192]{1,0:T(8,128)(2,1)}, u32[]{:S(2)}) copy-start(bf16[64,8192]{1,0:T(8,128)(2,1)} %param.21) | copy-start | bytes 3145732
  4.5 33.1 %copy-start.24 = (bf16[32,256]{1,0:T(8,128)(2,1)S(1)}, bf16[32,256]{1,0:T(8,128)(2,1)}, u32[]{:S(2)}) copy-start(bf16[32,256]{1,0:T(8,128)(2,1)} %param.18) | copy-start | bytes 49156
  4.5 33.1 %copy-start.25 = (bf16[32,256]{1,0:T(8,128)(2,1)S(1)}, bf16[32,256]{1,0:T(8,128)(2,1)}, u32[]{:S(2)}) copy-start(bf16[32,256]{1,0:T(8,128)(2,1)} %param.19) | copy-start | bytes 49156
  4.5 33.2 %copy-start.27 = (f32[64]{0:T(128)S(1)}, f32[64]{0:T(128)}, u32[]{:S(2)}) copy-start(f32[64]{0:T(128)} %param.20) | copy-start | bytes 772
  4.5 51.8 %copy-start.26 = (s32[1,64,4]{1,2,0:T(4,128)S(1)}, s32[1,64,4]{1,2,0:T(4,128)}, u32[]{:S(2)}) copy-start(s32[1,64,4]{1,2,0:T(4,128)} %param.16) | copy-start | bytes 3076
  16.8 0.6 copy-start.17
  17.5 53.5 %all-to-all-start = ((bf16[64,48,128]{2,1,0:T(8,128)(2,1)}), bf16[64,48,128]{2,1,0:T(8,128)(2,1)S(1)}, u32[]{:S(2)}, u32[]{:S(2)}) async-start(bf16[64,48,128]{2,1,0:T(8,128)(2,1)} %get-tuple-element.60), calls=%async_computation | async-start | bytes 1572864 | tf_op jit(solution)/shard_map/all_to_all | solution.py:465
  30.6 55.2 %collective-permute-start = (bf16[32,2048]{1,0:T(8,128)(2,1)}, bf16[32,2048]{1,0:T(8,128)(2,1)}, u32[]{:S(2)}, u32[]{:S(2)}) collective-permute-start(bf16[32,2048]{1,0:T(8,128)(2,1)} %get-tuple-element.56), channel_id=1, source_target_pairs={{0,1},{1,2},{2,3},{3,0},{4,5},{5,6},{6,7},{7,4},{8,9},{9,10},{10,1... | collective-permute-start | bytes 393224 | tf_op jit(solution)/shard_map/ppermute | solution.py:437
  31.9 56.0 %collective-permute-start.1 = (bf16[32,2048]{1,0:T(8,128)(2,1)}, bf16[32,2048]{1,0:T(8,128)(2,1)}, u32[]{:S(2)}, u32[]{:S(2)}) collective-permute-start(bf16[32,2048]{1,0:T(8,128)(2,1)} %get-tuple-element.57), channel_id=1, source_target_pairs={{0,2},{1,3},{2,0},{3,1},{4,6},{5,7},{6,4},{7,5},{8,10},{9,11},{10,... | collective-permute-start | bytes 393224 | tf_op jit(solution)/shard_map/ppermute | solution.py:437
  34.4 53.7 %collective-permute-start.2 = (bf16[32,2048]{1,0:T(8,128)(2,1)}, bf16[32,2048]{1,0:T(8,128)(2,1)}, u32[]{:S(2)}, u32[]{:S(2)}) collective-permute-start(bf16[32,2048]{1,0:T(8,128)(2,1)} %get-tuple-element.58), channel_id=1, source_target_pairs={{0,3},{1,0},{2,1},{3,2},{4,7},{5,4},{6,5},{7,6},{8,11},{9,8},{10,9... | collective-permute-start | bytes 393224 | tf_op jit(solution)/shard_map/ppermute | solution.py:437
  36.4 52.8 %collective-permute-start.6 = (bf16[64,2048]{1,0:T(8,128)(2,1)}, bf16[64,2048]{1,0:T(8,128)(2,1)S(1)}, u32[]{:S(2)}, u32[]{:S(2)}) collective-permute-start(bf16[64,2048]{1,0:T(8,128)(2,1)} %get-tuple-element.96), channel_id=1, source_target_pairs={{0,1},{1,2},{2,3},{3,0},{4,5},{5,6},{6,7},{7,4},{8,9},{9,10},{10,1... | collective-permute-start | bytes 786440 | tf_op jit(solution)/shard_map/ppermute | solution.py:437
  36.7 58.1 %collective-permute-start.7 = (bf16[64,2048]{1,0:T(8,128)(2,1)}, bf16[64,2048]{1,0:T(8,128)(2,1)}, u32[]{:S(2)}, u32[]{:S(2)}) collective-permute-start(bf16[64,2048]{1,0:T(8,128)(2,1)} %get-tuple-element.98), channel_id=1, source_target_pairs={{0,2},{1,3},{2,0},{3,1},{4,6},{5,7},{6,4},{7,5},{8,10},{9,11},{10,... | collective-permute-start | bytes 786440 | tf_op jit(solution)/shard_map/ppermute | solution.py:437
  56.3 14.6 %copy-start.21 = (f32[288,256]{1,0:T(8,128)}, f32[288,256]{1,0:T(8,128)S(1)}, u32[]{:S(2)}) copy-start(f32[288,256]{1,0:T(8,128)S(1)} %all-gather) | copy-start | bytes 884740
  77.6 12.0 %copy-start.23 = (bf16[4,72,256]{2,1,0:T(8,128)(2,1)S(1)}, bf16[4,72,256]{2,1,0:T(8,128)(2,1)}, u32[]{:S(2)}) copy-start(bf16[4,72,256]{2,1,0:T(8,128)(2,1)} %convert.4) | copy-start | bytes 442372
  85.9 9.0 %collective-permute-start.8 = (bf16[64,2048]{1,0:T(8,128)(2,1)}, bf16[64,2048]{1,0:T(8,128)(2,1)S(1)}, u32[]{:S(2)}, u32[]{:S(2)}) collective-permute-start(bf16[64,2048]{1,0:T(8,128)(2,1)} %get-tuple-element.95), channel_id=1, source_target_pairs={{0,3},{1,0},{2,1},{3,2},{4,7},{5,4},{6,5},{7,6},{8,11},{9,8},{10,9... | collective-permute-start | bytes 786440 | tf_op jit(solution)/shard_map/ppermute | solution.py:437
  88.0 7.4 %collective-permute-start.5 = (bf16[32,2048]{1,0:T(8,128)(2,1)S(1)}, bf16[32,2048]{1,0:T(8,128)(2,1)S(1)}, u32[]{:S(2)}, u32[]{:S(2)}) collective-permute-start(bf16[32,2048]{1,0:T(8,128)(2,1)S(1)} %aggregate.7), channel_id=1, source_target_pairs={{0,3},{1,0},{2,1},{3,2},{4,7},{5,4},{6,5},{7,6},{8,11},{9,8},{10,9... | collective-permute-start | bytes 393224 | tf_op jit(solution)/shard_map/ppermute | solution.py:437
  88.1 7.9 %collective-permute-start.4 = (bf16[32,2048]{1,0:T(8,128)(2,1)S(1)}, bf16[32,2048]{1,0:T(8,128)(2,1)S(1)}, u32[]{:S(2)}, u32[]{:S(2)}) collective-permute-start(bf16[32,2048]{1,0:T(8,128)(2,1)S(1)} %aggregate.6), channel_id=1, source_target_pairs={{0,2},{1,3},{2,0},{3,1},{4,6},{5,7},{6,4},{7,5},{8,10},{9,11},{10,... | collective-permute-start | bytes 393224 | tf_op jit(solution)/shard_map/ppermute | solution.py:437
  89.2 7.4 %copy-start.5 = (bf16[64,2048]{1,0:T(8,128)(2,1)}, bf16[64,2048]{1,0:T(8,128)(2,1)S(1)}, u32[]{:S(2)}) copy-start(bf16[64,2048]{1,0:T(8,128)(2,1)S(1)} %collective-permute-done.6.refs_9_) | copy-start | bytes 786436
  89.2 7.4 %collective-permute-start.3 = (bf16[32,2048]{1,0:T(8,128)(2,1)S(1)}, bf16[32,2048]{1,0:T(8,128)(2,1)}, u32[]{:S(2)}, u32[]{:S(2)}) collective-permute-start(bf16[32,2048]{1,0:T(8,128)(2,1)S(1)} %aggregate.5), channel_id=1, source_target_pairs={{0,1},{1,2},{2,3},{3,0},{4,5},{5,6},{6,7},{7,4},{8,9},{9,10},{10,1... | collective-permute-start | bytes 393224 | tf_op jit(solution)/shard_map/ppermute | solution.py:437
  90.7 6.0 %copy-start.18 = (bf16[32,2048]{1,0:T(8,128)(2,1)S(1)}, bf16[32,2048]{1,0:T(8,128)(2,1)}, u32[]{:S(2)}) copy-start(bf16[32,2048]{1,0:T(8,128)(2,1)} %copy-done.17) | copy-start | bytes 393220
  95.3 0.7 copy-start.12
  96.0 0.7 copy-start.14
  96.6 1.0 copy-start.6
  97.6 0.9 copy-start.13
  98.5 0.9 copy-start.15
  104.2 0.7 copy-start.9
  104.9 9.5 %copy-start.3 = (bf16[64,2048]{1,0:T(8,128)(2,1)}, bf16[64,2048]{1,0:T(8,128)(2,1)S(1)}, u32[]{:S(2)}) copy-start(bf16[64,2048]{1,0:T(8,128)(2,1)S(1)} %get-tuple-element.76) | copy-start | bytes 786436
  104.9 9.5 %copy-start.7 = (bf16[32,2048]{1,0:T(8,128)(2,1)}, bf16[32,2048]{1,0:T(8,128)(2,1)S(1)}, u32[]{:S(2)}) copy-start(bf16[32,2048]{1,0:T(8,128)(2,1)S(1)} %get-tuple-element.92) | copy-start | bytes 393220
  104.9 9.5 %copy-start.11 = (bf16[32,2048]{1,0:T(8,128)(2,1)}, bf16[32,2048]{1,0:T(8,128)(2,1)S(1)}, u32[]{:S(2)}) copy-start(bf16[32,2048]{1,0:T(8,128)(2,1)S(1)} %get-tuple-element.90) | copy-start | bytes 393220
  104.9 28.8 %copy-start.19 = (bf16[32,2048]{1,0:T(8,128)(2,1)}, bf16[32,2048]{1,0:T(8,128)(2,1)S(1)}, u32[]{:S(2)}) copy-start(bf16[32,2048]{1,0:T(8,128)(2,1)S(1)} %get-tuple-element.89.refs_0_) | copy-start | bytes 393220
  104.9 50.6 %copy-start.10 = (bf16[32,2048]{1,0:T(8,128)(2,1)S(1)}, bf16[32,2048]{1,0:T(8,128)(2,1)}, u32[]{:S(2)}) copy-start(bf16[32,2048]{1,0:T(8,128)(2,1)} %copy-done.9) | copy-start | bytes 393220
  104.9 7.0 %collective-permute-start.15 = (f32[72,256]{1,0:T(8,128)S(1)}, f32[72,256]{1,0:T(8,128)S(1)}, u32[]{:S(2)}, u32[]{:S(2)}) collective-permute-start(f32[72,256]{1,0:T(8,128)S(1)} %get-tuple-element.85), channel_id=1, source_target_pairs={{0,3},{1,0},{2,1},{3,2},{4,7},{5,4},{6,5},{7,6},{8,11},{9,8},{10,9... | collective-permute-start | bytes 221192 | tf_op jit(solution)/shard_map/ppermute | solution.py:437
  108.5 5.8 %collective-permute-start.16 = (f32[72,256]{1,0:T(8,128)S(1)}, f32[72,256]{1,0:T(8,128)S(1)}, u32[]{:S(2)}, u32[]{:S(2)}) collective-permute-start(f32[72,256]{1,0:T(8,128)S(1)} %get-tuple-element.86), channel_id=1, source_target_pairs={{0,2},{1,3},{2,0},{3,1},{4,6},{5,7},{6,4},{7,5},{8,10},{9,11},{10,... | collective-permute-start | bytes 221192 | tf_op jit(solution)/shard_map/ppermute | solution.py:437
  108.5 5.8 %collective-permute-start.17 = (f32[72,256]{1,0:T(8,128)S(1)}, f32[72,256]{1,0:T(8,128)S(1)}, u32[]{:S(2)}, u32[]{:S(2)}) collective-permute-start(f32[72,256]{1,0:T(8,128)S(1)} %get-tuple-element.87), channel_id=1, source_target_pairs={{0,1},{1,2},{2,3},{3,0},{4,5},{5,6},{6,7},{7,4},{8,9},{9,10},{10,1... | collective-permute-start | bytes 221192 | tf_op jit(solution)/shard_map/ppermute | solution.py:437
  109.3 6.2 %collective-permute-start.10 = (bf16[32,2048]{1,0:T(8,128)(2,1)S(1)}, bf16[32,2048]{1,0:T(8,128)(2,1)S(1)}, u32[]{:S(2)}, u32[]{:S(2)}) collective-permute-start(bf16[32,2048]{1,0:T(8,128)(2,1)S(1)} %get-tuple-element.65), channel_id=1, source_target_pairs={{0,2},{1,3},{2,0},{3,1},{4,6},{5,7},{6,4},{7,5},{8,10},{9,11},{10,... | collective-permute-start | bytes 393224 | tf_op jit(solution)/shard_map/ppermute | solution.py:437
  111.6 5.2 %collective-permute-start.11 = (bf16[32,2048]{1,0:T(8,128)(2,1)S(1)}, bf16[32,2048]{1,0:T(8,128)(2,1)S(1)}, u32[]{:S(2)}, u32[]{:S(2)}) collective-permute-start(bf16[32,2048]{1,0:T(8,128)(2,1)S(1)} %get-tuple-element.66), channel_id=1, source_target_pairs={{0,1},{1,2},{2,3},{3,0},{4,5},{5,6},{6,7},{7,4},{8,9},{9,10},{10,1... | collective-permute-start | bytes 393224 | tf_op jit(solution)/shard_map/ppermute | solution.py:437
  111.9 5.4 %collective-permute-start.9 = (bf16[32,2048]{1,0:T(8,128)(2,1)S(1)}, bf16[32,2048]{1,0:T(8,128)(2,1)S(1)}, u32[]{:S(2)}, u32[]{:S(2)}) collective-permute-start(bf16[32,2048]{1,0:T(8,128)(2,1)S(1)} %get-tuple-element.64), channel_id=1, source_target_pairs={{0,3},{1,0},{2,1},{3,2},{4,7},{5,4},{6,5},{7,6},{8,11},{9,8},{10,9... | collective-permute-start | bytes 393224 | tf_op jit(solution)/shard_map/ppermute | solution.py:437
  114.4 35.2 %copy-start.4 = (bf16[64,2048]{1,0:T(8,128)(2,1)S(1)}, bf16[64,2048]{1,0:T(8,128)(2,1)}, u32[]{:S(2)}) copy-start(bf16[64,2048]{1,0:T(8,128)(2,1)} %copy-done.3) | copy-start | bytes 786436
  114.4 48.7 %copy-start.8 = (bf16[32,2048]{1,0:T(8,128)(2,1)S(1)}, bf16[32,2048]{1,0:T(8,128)(2,1)}, u32[]{:S(2)}) copy-start(bf16[32,2048]{1,0:T(8,128)(2,1)} %copy-done.7) | copy-start | bytes 393220
  132.8 1.0 copy-start
  133.8 41.0 %all-to-all-start.1 = ((bf16[64,56,128]{2,1,0:T(8,128)(2,1)}), bf16[64,56,128]{2,1,0:T(8,128)(2,1)S(1)}, u32[]{:S(2)}, u32[]{:S(2)}) async-start(bf16[64,56,128]{2,1,0:T(8,128)(2,1)} %maximum_dynamic-update-slice_fusion), calls=%async_computation.1 | async-start | bytes 1835008 | tf_op jit(solution)/shard_map/all_to_all | solution.py:511
  149.5 13.5 %collective-permute-start.12 = (bf16[64,2048]{1,0:T(8,128)(2,1)S(1)}, bf16[64,2048]{1,0:T(8,128)(2,1)S(1)}, u32[]{:S(2)}, u32[]{:S(2)}) collective-permute-start(bf16[64,2048]{1,0:T(8,128)(2,1)S(1)} %copy-done.4), channel_id=1, source_target_pairs={{0,3},{1,0},{2,1},{3,2},{4,7},{5,4},{6,5},{7,6},{8,11},{9,8},{10,9... | collective-permute-start | bytes 786440 | tf_op jit(solution)/shard_map/ppermute | solution.py:437
  152.7 10.4 %collective-permute-start.13 = (bf16[64,2048]{1,0:T(8,128)(2,1)S(1)}, bf16[64,2048]{1,0:T(8,128)(2,1)S(1)}, u32[]{:S(2)}, u32[]{:S(2)}) collective-permute-start(bf16[64,2048]{1,0:T(8,128)(2,1)S(1)} %get-tuple-element.77), channel_id=1, source_target_pairs={{0,2},{1,3},{2,0},{3,1},{4,6},{5,7},{6,4},{7,5},{8,10},{9,11},{10,... | collective-permute-start | bytes 786440 | tf_op jit(solution)/shard_map/ppermute | solution.py:437
  152.8 15.4 %collective-permute-start.14 = (bf16[64,2048]{1,0:T(8,128)(2,1)S(1)}, bf16[64,2048]{1,0:T(8,128)(2,1)S(1)}, u32[]{:S(2)}, u32[]{:S(2)}) collective-permute-start(bf16[64,2048]{1,0:T(8,128)(2,1)S(1)} %get-tuple-element.78), channel_id=1, source_target_pairs={{0,1},{1,2},{2,3},{3,0},{4,5},{5,6},{6,7},{7,4},{8,9},{9,10},{10,1... | collective-permute-start | bytes 786440 | tf_op jit(solution)/shard_map/ppermute | solution.py:437
  153.4 28.7 %collective-permute-start.18 = (bf16[32,2048]{1,0:T(8,128)(2,1)}, bf16[32,2048]{1,0:T(8,128)(2,1)S(1)}, u32[]{:S(2)}, u32[]{:S(2)}) collective-permute-start(bf16[32,2048]{1,0:T(8,128)(2,1)} %copy-done.11), channel_id=1, source_target_pairs={{0,3},{1,0},{2,1},{3,2},{4,7},{5,4},{6,5},{7,6},{8,11},{9,8},{10,9... | collective-permute-start | bytes 393224 | tf_op jit(solution)/shard_map/ppermute | solution.py:437
  155.5 26.6 %collective-permute-start.19 = (bf16[32,2048]{1,0:T(8,128)(2,1)S(1)}, bf16[32,2048]{1,0:T(8,128)(2,1)S(1)}, u32[]{:S(2)}, u32[]{:S(2)}) collective-permute-start(bf16[32,2048]{1,0:T(8,128)(2,1)S(1)} %copy-done.10), channel_id=1, source_target_pairs={{0,2},{1,3},{2,0},{3,1},{4,6},{5,7},{6,4},{7,5},{8,10},{9,11},{10,... | collective-permute-start | bytes 393224 | tf_op jit(solution)/shard_map/ppermute | solution.py:437
  163.1 19.0 %collective-permute-start.20 = (bf16[32,2048]{1,0:T(8,128)(2,1)S(1)}, bf16[32,2048]{1,0:T(8,128)(2,1)S(1)}, u32[]{:S(2)}, u32[]{:S(2)}) collective-permute-start(bf16[32,2048]{1,0:T(8,128)(2,1)S(1)} %copy-done.8), channel_id=1, source_target_pairs={{0,1},{1,2},{2,3},{3,0},{4,5},{5,6},{6,7},{7,4},{8,9},{9,10},{10,1... | collective-permute-start | bytes 393224 | tf_op jit(solution)/shard_map/ppermute | solution.py:437
  175.6 21.3 %all-to-all-start.2 = ((f32[64,8,128]{2,1,0:T(8,128)}), f32[64,8,128]{2,1,0:T(8,128)S(1)}, u32[]{:S(2)}, u32[]{:S(2)}) async-start(f32[64,8,128]{2,1,0:T(8,128)} %broadcast_in_dim.22), calls=%async_computation.2 | async-start | bytes 524288 | tf_op jit(solution)/shard_map/all_to_all | solution.py:518
  182.1 1.2 copy-start.1
  183.4 0.9 copy-start.20

commit v2 on v0

v2 whole, which is shorter than its diff:
```python
import functools

import jax
import jax.numpy as jnp
from jax import lax
from jax.experimental import pallas as pl
from jax.experimental.pallas import tpu as pltpu
from jax.sharding import PartitionSpec as P

BF = jnp.bfloat16
F32 = jnp.float32
VMEM = pl.BlockSpec(memory_space=pltpu.VMEM)
ANY = pl.BlockSpec(memory_space=pl.ANY)
SMEM = pl.BlockSpec(memory_space=pltpu.SMEM)
LANES = 128
GROUP = 4


def params(mib=20):
    return pltpu.CompilerParams(vmem_limit_bytes=mib << 20)


def cost(flops, nbytes):
    return pl.CostEstimate(flops=int(flops), bytes_accessed=int(nbytes), transcendentals=0)


def low_half(shape):
    return lax.broadcasted_iota(jnp.int32, shape, len(shape) - 1) < LANES // 2


def split_rest(tile):
    half = tile.shape[0] // 2
    a, b = tile[:half], tile[half:]
    low = low_half(a.shape)
    even = jnp.where(low, a, pltpu.roll(b, LANES // 2, 1))
    odd = jnp.where(low, pltpu.roll(a, LANES // 2, 1), b)
    return even, odd


def join_rest(even, odd):
    low = low_half(even.shape)
    a = jnp.where(low, even, pltpu.roll(odd, LANES // 2, 1))
    b = jnp.where(low, pltpu.roll(even, LANES // 2, 1), odd)
    return jnp.concatenate([a, b], axis=0)


def one_hot_rows(lo, count):
    rows = lax.broadcasted_iota(jnp.int32, (count, lo.shape[1]), 0)
    return jnp.where(rows == lo, 1.0, 0.0).astype(BF)


class Copies:
    def __init__(self, src, dst, sems, first, parts):
        size = dst.shape[0] // parts
        self.parts = [
            pltpu.make_async_copy(
                src.at[pl.ds(n * size, size)], dst.at[pl.ds(n * size, size)], sems.at[first + n]
            )
            for n in range(parts)
        ]
        for part in self.parts:
            part.start()

    def wait(self):
        for part in self.parts:
            part.wait()


def turn(me, s):
    return lax.rem(me + 4 - s, 4)


def struct(shape, dtype):
    return jax.ShapeDtypeStruct(shape, dtype)


FOLD_IN = 256
FOLD_OUT = 512


def gather_kernel(
    where, quantized, scale, rows, counts, upstream, self_w, neighbor_w, bias,
    tiles_out, wire_out, idx_out, b0, b1, b2, b3,
    q_s, s_s, r_s, c_s, sw_s, nw_s, bias_s, rest_s, folded, feat_tiles, wire, idx, block_s, sems,
):
    pairs = [(scale, s_s), (rows, r_s), (counts, c_s)]
    pairs += [(self_w, sw_s), (neighbor_w, nw_s), (bias, bias_s)]
    for n in range(4):
        at = pl.ds(n * 2048, 2048)
        pairs.append((quantized.at[:, at], q_s.at[:, at]))
    copies = [pltpu.make_async_copy(src, dst, sems.at[n]) for n, (src, dst) in enumerate(pairs)]
    for copy in copies:
        copy.start()
    for copy in copies:
        copy.wait()
    me, odd = where[0], where[1]
    ups = []
    for s in range(4):
        at = pl.ds(pl.multiple_of(lax.rem(me + s, 4) * 2048, 2048), 2048)
        dst = block_s.at[s, pl.ds(32, 64)]
        ups.append(pltpu.make_async_copy(upstream.at[:, at], dst, sems.at[17 + s]))
        ups[s].start()
    feature_count, node_count = q_s.shape
    fold = node_count // FOLD_IN
    for c in range(fold):
        at = pl.ds(c * FOLD_IN, FOLD_IN)
        part = (q_s[:, at].astype(F32) * s_s[:, at]).astype(BF)
        folded[c * feature_count : (c + 1) * feature_count, :] = part
        for t in range(FOLD_IN // LANES):
            feat_tiles[c * (FOLD_IN // LANES) + t] = part[:, t * LANES : (t + 1) * LANES]

    peers = r_s.shape[1]
    spread_counts = jnp.broadcast_to(c_s[...], (peers, peers))
    diagonal = lax.broadcasted_iota(jnp.int32, (peers, peers), 0) == lax.broadcasted_iota(
        jnp.int32, (peers, peers), 1
    )
    limit = jnp.sum(jnp.where(diagonal, spread_counts, 0), axis=1, keepdims=True)
    lane = lax.broadcasted_iota(jnp.int32, (peers, LANES), 1)
    first = jnp.where(lane < limit, r_s[0, :, 0:LANES], -1)
    last = jnp.concatenate(
        [r_s[0, :, LANES : LANES + 64], jnp.full((peers, 64), -1, jnp.int32)], axis=1
    )
    last = jnp.where(lane + LANES < limit, last, -1)
    low = lane < 64
    moved = jnp.where(low, pltpu.roll(first, 64, 1), pltpu.roll(last, 64, 1))
    is_odd = jnp.full((peers, LANES), odd, jnp.int32) == 1
    idx[0:peers, :] = jnp.where(is_odd, moved, first)
    rest_s[...] = jnp.where(is_odd, first, last)
    even_rows = rest_s[pl.ds(0, peers // 2, stride=2), :]
    odd_rows = rest_s[pl.ds(1, peers // 2, stride=2), :]
    idx[peers : peers + peers // 2, :] = jnp.where(
        low[0 : peers // 2], even_rows, pltpu.roll(odd_rows, 64, 1)
    )

    per_block = node_count // 4 // LANES
    for s in range(4):
        begin = lax.rem(me + s, 4) * per_block
        for t in range(per_block):
            block_s[s, 0:32, t * LANES : (t + 1) * LANES] = feat_tiles[begin + t]
    whole_bias = jnp.broadcast_to(bias_s[...], (32, 64))
    for s in range(4):
        block_s[s, 96:128, 512:] = jnp.zeros((32, 1536), BF)
        block_s[s, 96:128, 0:256] = sw_s[...]
        block_s[s, 96:128, 256:512] = nw_s[...]
        left = whole_bias
        for n in range(3):
            part = left.astype(BF)
            block_s[s, 96:128, 512 + n * LANES : 576 + n * LANES] = part
            left = left - part.astype(F32)
    pairs = [(feat_tiles, tiles_out), (idx, idx_out)]
    for s, block in enumerate((b0, b1, b2, b3)):
        pairs.append((block_s.at[s], block))
    for copy in ups:
        copy.wait()
    sends = [
        pltpu.make_async_copy(src, dst, sems.at[21 + n]) for n, (src, dst) in enumerate(pairs)
    ]
    for send in sends:
        send.start()

    def pick(base):
        row = jnp.concatenate([idx[pl.ds(base + t, 1), :] for t in range(8)], axis=1)
        hi, lo = row >> 8, row & (FOLD_IN - 1)
        out = jnp.dot(folded[...], one_hot_rows(lo, FOLD_IN), preferred_element_type=F32)
        total = jnp.zeros((feature_count, row.shape[1]), F32)
        for c in range(fold):
            total = total + jnp.where(hi == c, out[c * feature_count : (c + 1) * feature_count], 0.0)
        return [total[:, t * LANES : (t + 1) * LANES] for t in range(8)]

    @pl.loop(0, 8, unroll=2)
    def _(g):
        tiles = pick(g * 8)
        for t in range(8):
            wire[g * 8 + t, 0:feature_count, :] = tiles[t].astype(BF)

    @pl.loop(0, 4, unroll=2)
    def _(g):
        tiles = pick(64 + g * 8)
        for t in range(8):
            even, odd_part = split_rest(tiles[t])
            wire[(g * 8 + t) * 2, feature_count:48, :] = even.astype(BF)
            wire[(g * 8 + t) * 2 + 1, feature_count:48, :] = odd_part.astype(BF)
        at = pl.ds(g * 16, 16)
        pltpu.make_async_copy(wire.at[at], wire_out.at[at], sems.at[13 + g]).start()

    for send in sends:
        send.wait()
    for g in range(4):
        at = pl.ds(g * 16, 16)
        pltpu.make_async_copy(wire.at[at], wire_out.at[at], sems.at[13 + g]).wait()


def gather(where, quantized, scale, rows, counts, *early):
    features, nodes = quantized.shape
    return pl.pallas_call(
        gather_kernel,
        out_shape=[
            struct((nodes // LANES, features, LANES), BF),
            struct((64, 48, LANES), BF),
            struct((96, LANES), jnp.int32),
        ]
        + [struct((128, nodes // 4), BF)] * 4,
        in_specs=[SMEM] + [ANY] * 8,
        out_specs=[ANY] * 7,
        scratch_shapes=[
            pltpu.VMEM(quantized.shape, BF),
            pltpu.VMEM(scale.shape, F32),
            pltpu.VMEM(rows.shape, jnp.int32),
            pltpu.VMEM(counts.shape, jnp.int32),
            pltpu.VMEM((32, 256), BF),
            pltpu.VMEM((32, 256), BF),
            pltpu.VMEM((1, 64), F32),
            pltpu.VMEM((64, LANES), jnp.int32),
            pltpu.VMEM((features * nodes // FOLD_IN, FOLD_IN), BF),
            pltpu.VMEM((nodes // LANES, features, LANES), BF),
            pltpu.VMEM((64, 48, LANES), BF),
            pltpu.VMEM((96, LANES), jnp.int32),
            pltpu.VMEM((4, 128, nodes // 4), BF),
            pltpu.SemaphoreType.DMA((27,)),
        ],
        compiler_params=params(60),
        cost_estimate=cost(6.4e9, 4 << 20),
        name="gather_rows",
    )(where, quantized, scale, rows, counts, *early)


def mask_kernel(edges, mask, degree, edges_s, mask_s, in_sems, out_sems):
    steps = edges.shape[0] // GROUP
    ones = jnp.ones((8, LANES), BF)
    loads = []
    stores = []
    for i in range(steps):
        at = pl.ds(i * GROUP, GROUP)
        loads.append(pltpu.make_async_copy(edges.at[at], edges_s.at[at], in_sems.at[i]))
        stores.append(pltpu.make_async_copy(mask_s.at[at], mask.at[at], out_sems.at[i]))
        loads[i].start()
    for i in range(steps):
        loads[i].wait()
        for r in range(i * GROUP, (i + 1) * GROUP):
            whole = edges_s[r]
            mask_s[r] = whole.astype(F32).astype(BF)
            total = (whole[0] + whole[1] + whole[2] + whole[3]).astype(F32).astype(BF)
            degree[r] = lax.dot_general(
                ones, total, (((1,), (1,)), ((), ())), preferred_element_type=F32
            )[0:1]
        stores[i].start()
    for store in stores:
        store.wait()


def masks(edges):
    tiles = edges.shape[0]
    length = 6 * tiles
    return pl.pallas_call(
        mask_kernel,
        out_shape=[struct((length,) + edges.shape[1:], BF), struct((tiles, 1, LANES), F32)],
        in_specs=[ANY],
        out_specs=[ANY, VMEM],
        scratch_shapes=[
            pltpu.VMEM(edges.shape, jnp.int32),
            pltpu.VMEM(edges.shape, BF),
            pltpu.SemaphoreType.DMA((tiles // GROUP,)),
            pltpu.SemaphoreType.DMA((tiles // GROUP,)),
        ],
        compiler_params=params(58),
        cost_estimate=cost(1e9, 24 << 20),
        name="mask_degree",
    )(edges)


QUARTER = 16


PARTS = 4


def fetch(me, shift, mask, chunk, sems, first=0):
    begin = lax.rem(me[0] + shift, 4) * QUARTER
    return Copies(mask.at[pl.ds(begin, QUARTER)], chunk, sems, first, PARTS)


CHUNK = struct((QUARTER, 4, LANES, LANES), BF)


def aggregate_tiles(begin, cols, joined, chunk, degree, out):
    totals = []
    for t in range(QUARTER):
        row = begin + t
        picked = jnp.concatenate([joined[cols[row, k]] for k in range(4)], axis=1)
        flat = jnp.concatenate([chunk[t, k] for k in range(4)], axis=1)
        totals.append(
            lax.dot_general(picked, flat, (((1,), (1,)), ((), ())), preferred_element_type=F32)
        )
    for t in range(QUARTER):
        row = begin + t
        out[:, t * LANES : (t + 1) * LANES] = (
            (totals[t] + joined[row].astype(F32)) / (degree[row] + 1.0)
        ).astype(BF)


ORDER = (2, 1, 3)


def aggregate_kernel(me, cols, feat_tiles, wire, degree, mask, *refs):
    outs, (joined, own_chunk, wire_s, chunks, sems) = refs[0:3], refs[3:]
    arriving = Copies(wire, wire_s, sems, 0, 2)
    local = feat_tiles.shape[0]
    own = Copies(feat_tiles, joined.at[pl.ds(0, local)], sems, 2, 1)
    tiles = [
        fetch(me, shift, mask, chunks.at[n], sems, 8 + PARTS * n) for n, shift in enumerate(ORDER)
    ]
    arriving.wait()

    @pl.loop(0, 32, unroll=8)
    def _(q):
        even, odd = wire_s[2 * q], wire_s[2 * q + 1]
        joined[local + 3 * q] = even[0:32]
        joined[local + 3 * q + 2] = odd[0:32]
        joined[local + 3 * q + 1] = join_rest(even[32:48].astype(F32), odd[32:48].astype(F32)).astype(BF)

    own.wait()
    for n, shift in enumerate(ORDER):
        tiles[n].wait()
        begin = lax.rem(me[0] + shift, 4) * QUARTER
        if n == 1:
            later = fetch(me, 0, mask, own_chunk, sems, 8 + PARTS * 3)
        aggregate_tiles(begin, cols, joined, chunks.at[n], degree, outs[shift - 1])
    later.wait()


def aggregate(me, cols, feat_tiles, wire, degree, mask):
    local, rows, _ = feat_tiles.shape
    got = pl.pallas_call(
        aggregate_kernel,
        out_shape=[struct((rows, 2048), BF)] * 3 + [struct((local + 96, rows, LANES), BF), CHUNK],
        in_specs=[SMEM, SMEM, ANY, ANY, VMEM, ANY],
        out_specs=[VMEM] * 5,
        scratch_shapes=[
            pltpu.VMEM(wire.shape, BF),
            pltpu.VMEM((3,) + CHUNK.shape, BF),
            pltpu.SemaphoreType.DMA((8 + PARTS * 4,)),
        ],
        compiler_params=params(),
        cost_estimate=cost(3e9, 12 << 20),
        name="aggregate",
    )(me, cols, feat_tiles, wire, degree, mask)
    return got[0:3], got[3], got[4]


def aggregate_own_kernel(me, cols, joined, chunk, degree, out):
    aggregate_tiles(me[0] * QUARTER, cols, joined, chunk, degree, out)


def aggregate_own(me, cols, joined, chunk, degree):
    return pl.pallas_call(
        aggregate_own_kernel,
        out_shape=struct((joined.shape[1], 2048), BF),
        in_specs=[SMEM, SMEM, VMEM, VMEM, VMEM],
        out_specs=VMEM,
        compiler_params=params(),
        cost_estimate=cost(1e9, 4 << 20),
        name="aggregate_own",
    )(me, cols, joined, chunk, degree)


def dense_kernel(me_ref, *refs):
    pieces, aggs, degree = refs[0:4], refs[4:8], refs[8]
    backs, hiddens, sums = refs[9:13], refs[13:17], refs[17:21]
    stage, agg, slope, hid_s, back_s, sum_s, sems = refs[21:]
    me = me_ref[0]
    both = (((1,), (1,)), ((), ()))
    nodes = slope.shape[1]
    copies = []
    for s in range(4):
        at = pl.ds(pl.multiple_of(turn(me, s) * 32, 32), 32)
        copies.append(pltpu.make_async_copy(aggs[s], agg.at[at, :], sems.at[s]))
        copies.append(pltpu.make_async_copy(pieces[s], stage.at[turn(me, s)], sems.at[4 + s]))
    for copy in copies:
        copy.start()
    for copy in copies:
        copy.wait()

    def joint(first, last, at):
        return jnp.concatenate([stage[b, first:last, at] for b in range(4)], axis=0)

    self_w = joint(96, 128, slice(0, 256))
    neighbor_w = joint(96, 128, slice(256, 512))
    self_t = self_w.astype(F32).T.astype(BF)
    neighbor_t = neighbor_w.astype(F32).T.astype(BF)
    diagonal = lax.broadcasted_iota(jnp.int32, (64, 64), 0) == lax.broadcasted_iota(
        jnp.int32, (64, 64), 1
    )
    columns = []
    for b in range(4):
        row = sum(
            stage[b, 96:112, 512 + n * LANES : 576 + n * LANES].astype(F32) for n in range(3)
        )[0:1]
        square = jnp.where(diagonal, jnp.broadcast_to(row, (64, 64)), 0.0)
        columns.append(jnp.sum(square, axis=1, keepdims=True))
    bias = jnp.concatenate(columns, axis=0)
    sends = []

    def send(pieces, whole, size, first):
        for s in range(4):
            if whole.shape[0] == 4:
                src = whole.at[turn(me, s)]
            else:
                src = whole.at[pl.ds(pl.multiple_of(turn(me, s) * size, size), size), :]
            sends.append(pltpu.make_async_copy(src, pieces[s], sems.at[first + s]))
            sends[-1].start()

    for n in range(4):
        at = slice(n * 512, (n + 1) * 512)
        preact = (
            jnp.dot(self_t, joint(0, 32, at), preferred_element_type=F32)
            + jnp.dot(neighbor_t, agg[:, at], preferred_element_type=F32)
            + bias
        )
        sig = jax.nn.sigmoid(preact)
        hid_s[:, at] = (preact * sig).astype(BF)
        part = (
            joint(32, 96, at).astype(F32) * sig * (1.0 + preact * (1.0 - sig))
        ).astype(BF)
        slope[:, at] = part
        below = jnp.concatenate([degree[me * 16 + n * 4 + t] for t in range(4)], axis=1) + 1.0
        whole = jnp.dot(neighbor_w, part, preferred_element_type=F32) / below
        for b in range(4):
            back_s[b, 0:32, at] = whole[b * 32 : (b + 1) * 32].astype(BF)
        own = jnp.dot(self_w, part, preferred_element_type=F32)
        sum_s[:, at] = (own + whole).astype(BF)
    send(hiddens, hid_s, 64, 12)
    send(sums, sum_s, 32, 16)
    all_nodes = slice(0, nodes)
    feat_grad = lax.dot_general(
        joint(0, 32, all_nodes), slope[...], both, preferred_element_type=F32
    )
    agg_grad = lax.dot_general(agg[...], slope[...], both, preferred_element_type=F32)
    bias_grad = lax.dot_general(
        jnp.ones((8, nodes), BF), slope[...], both, preferred_element_type=F32
    )
    bias_row = bias_grad[0:1]
    high = bias_row.astype(BF).astype(F32)
    for b in range(4):
        for n, grad in enumerate((feat_grad, agg_grad)):
            for h in range(2):
                first = b * 32 + h * 16
                at = slice((2 * n + h) * 256, (2 * n + h + 1) * 256)
                back_s[b, 32:48, at] = grad[first : first + 16].astype(BF)
        back_s[b, 32:48, 1024:1280] = jnp.broadcast_to(high, (16, 256)).astype(BF)
        back_s[b, 32:48, 1280:1536] = jnp.broadcast_to(bias_row - high, (16, 256)).astype(BF)
        back_s[b, 32:48, 1536:] = jnp.zeros((16, nodes - 1536), BF)
    send(backs, back_s, 48, 8)
    for copy in sends:
        copy.wait()


def dense(me, pieces, aggs, degree):
    nodes = aggs[0].shape[1]
    got = pl.pallas_call(
        dense_kernel,
        out_shape=[struct((48, nodes), BF)] * 4
        + [struct((64, nodes), BF)] * 4
        + [struct((32, nodes), BF)] * 4,
        in_specs=[SMEM] + [ANY] * 8 + [VMEM],
        out_specs=[ANY] * 12,
        scratch_shapes=[
            pltpu.VMEM((4, 128, nodes), BF),
            pltpu.VMEM((128, nodes), BF),
            pltpu.VMEM((256, nodes), BF),
            pltpu.VMEM((256, nodes), BF),
            pltpu.VMEM((4, 48, nodes), BF),
            pltpu.VMEM((128, nodes), BF),
            pltpu.SemaphoreType.DMA((20,)),
        ],
        compiler_params=params(56),
        cost_estimate=cost(1e9, 5 << 20),
        name="dense",
    )(me, *pieces, *aggs, degree)
    return got[0:4], got[4:8], got[8:12]


def own_quarter(me, row):
    half = jnp.where(me >= 2, row[:, LANES:], row[:, 0:LANES])
    half = jnp.broadcast_to(half, (8, LANES))
    return jnp.where(lax.rem(me, 2) == 1, pltpu.roll(half, 64, 1), half)[0:1, 0:64]


def pack_grads(me, grad, bias, pack_s):
    row = own_quarter(me, bias)
    diagonal = lax.broadcasted_iota(jnp.int32, (64, 64), 0) == lax.broadcasted_iota(
        jnp.int32, (64, 64), 1
    )
    column = jnp.sum(
        jnp.where(diagonal, jnp.broadcast_to(row, (64, 64)), 0.0), axis=1, keepdims=True
    )
    values = [grad[:, 0:LANES], grad[:, LANES:], jnp.broadcast_to(column, (64, LANES))]
    for n, value in enumerate(values):
        high = value.astype(BF).astype(F32)
        pack_s[:, n, :] = high
        pack_s[:, n + 3, :] = value - high
    for n in (6, 7):
        pack_s[:, n, :] = jnp.zeros((64, LANES), F32)


def spread_tiles(begin, cols, mean, chunk, total):
    for half in range(2):
        parts = []
        for t in range(half * 8, half * 8 + 8):
            flat = jnp.concatenate([chunk[t, k] for k in range(4)], axis=1)
            parts.append(
                jnp.dot(mean[0:32, t * LANES : (t + 1) * LANES], flat, preferred_element_type=F32)
            )
        for t in range(8):
            for k in range(4):
                at = cols[begin + half * 8 + t, k]
                total[at] = total[at] + parts[t][:, k * LANES : (k + 1) * LANES]


def spread_own_kernel(me, cols, mean, chunk, total):
    total[...] = jnp.zeros(total.shape, F32)
    spread_tiles(me[0] * QUARTER, cols, mean, chunk, total)


def spread_own(me, cols, mean, chunk):
    return pl.pallas_call(
        spread_own_kernel,
        out_shape=struct((160, 32, LANES), F32),
        in_specs=[SMEM, SMEM, VMEM, VMEM],
        out_specs=VMEM,
        compiler_params=params(),
        cost_estimate=cost(1e9, 4 << 20),
        name="spread_own",
    )(me, cols, mean, chunk)


def spread_kernel(me, cols, begun, mask, *refs):
    backs, (local, wire_out), refs = refs[0:4], refs[4:6], refs[6:]
    total, chunks, back_s, pack_s, wire, sems = refs
    pieces = []
    for s in range(4):
        pieces.append(pltpu.make_async_copy(backs[s], back_s.at[s], sems.at[s]))
        pieces[-1].start()
    tiles = [fetch(me, s, mask, chunks.at[s - 1], sems, 4 + PARTS * s) for s in (1, 2, 3)]
    total[...] = begun[...]
    for s in (1, 2, 3):
        begin = lax.rem(me[0] + s, 4) * QUARTER
        pieces[s].wait()
        tiles[s - 1].wait()
        spread_tiles(begin, cols, back_s.at[s], chunks.at[s - 1], total)
    own = Copies(total.at[pl.ds(0, 64)], local, sems, 4 + PARTS, 2)
    pieces[0].wait()
    grads = sum(back_s[s, 32:48, 0:1536].astype(F32) for s in range(4))
    grad = jnp.concatenate([grads[:, n * 256 : (n + 1) * 256] for n in range(4)], axis=0)
    pack_grads(me[0], grad, grads[0:1, 1024:1280] + grads[0:1, 1280:1536], pack_s)
    wire[:, 48:56, :] = pack_s[...].astype(BF)

    @pl.loop(0, 32, unroll=8)
    def _(q):
        wire[2 * q, 0:32, :] = total[64 + 3 * q].astype(BF)
        wire[2 * q + 1, 0:32, :] = total[64 + 3 * q + 2].astype(BF)
        even, odd = split_rest(total[64 + 3 * q + 1])
        wire[2 * q, 32:48, :] = even.astype(BF)
        wire[2 * q + 1, 32:48, :] = odd.astype(BF)

    leaving = Copies(wire, wire_out, sems, 0, 4)
    own.wait()
    leaving.wait()


def spread(me, cols, begun, mask, backs):
    _, rows, _ = begun.shape
    return pl.pallas_call(
        spread_kernel,
        out_shape=[struct((64, rows, LANES), F32), struct((64, 56, LANES), BF)],
        in_specs=[SMEM, SMEM, VMEM] + [ANY] * 5,
        out_specs=[ANY] * 2,
        scratch_shapes=[
            pltpu.VMEM(begun.shape, F32),
            pltpu.VMEM((3,) + CHUNK.shape, BF),
            pltpu.VMEM((4,) + backs[0].shape, BF),
            pltpu.VMEM((64, 8, LANES), F32),
            pltpu.VMEM((64, 56, LANES), BF),
            pltpu.SemaphoreType.DMA((4 + PARTS * 4,)),
        ],
        compiler_params=params(),
        cost_estimate=cost(3e9, 12 << 20),
        name="spread",
    )(me, cols, begun, mask, *backs)


def scatter_kernel(me_ref, idx, wire, local, *refs):
    sums, out, wire_s, sum_s, ret, acc, idx_s, own_s, out_s, sems = refs[0:4], *refs[4:]
    me = me_ref[0]
    index = Copies(idx, idx_s, sems, 0, 1)
    first = Copies(wire, wire_s, sems, 1, 2)
    later = [Copies(local, own_s, sems, 5, 2)]
    for s in range(4):
        later.append(Copies(sums[s], sum_s.at[lax.rem(me + s, 4)], sems, 9 + s, 1))
    nodes = out.shape[1]
    fold = nodes // FOLD_OUT
    acc[...] = jnp.zeros(acc.shape, F32)
    index.wait()
    first.wait()

    @pl.loop(0, 32, unroll=8)
    def _(q):
        even, odd = wire_s[2 * q], wire_s[2 * q + 1]
        ret[2 * q] = even[0:32].astype(F32)
        ret[2 * q + 1] = odd[0:32].astype(F32)
        ret[64 + q] = join_rest(even[32:48].astype(F32), odd[32:48].astype(F32))

    @pl.loop(0, 6)
    def _(g):
        row = jnp.concatenate([idx_s[pl.ds(g * 16 + t, 1), :] for t in range(16)], axis=1)
        hi, lo = row >> 9, row & (FOLD_OUT - 1)
        value = jnp.concatenate([ret[g * 16 + t] for t in range(16)], axis=1)
        folded = jnp.concatenate(
            [jnp.where(hi == c, value, 0.0).astype(BF) for c in range(fold)], axis=0
        )
        acc[...] += lax.dot_general(
            folded, one_hot_rows(lo, FOLD_OUT), (((1,), (1,)), ((), ())), preferred_element_type=F32
        )

    for copy in later:
        copy.wait()
    per = FOLD_OUT // LANES
    sends = []
    for quarter in range(4):
        for inner in range(fold // 4):
            c = quarter * (fold // 4) + inner
            inside = inner * FOLD_OUT
            own = jnp.concatenate([own_s[c * per + t] for t in range(per)], axis=1)
            extra = sum_s[quarter, :, inside : inside + FOLD_OUT].astype(F32)
            out_s[:, c * FOLD_OUT : (c + 1) * FOLD_OUT] = acc[c * 32 : (c + 1) * 32, :] + own + extra
        at = pl.ds(quarter * 2048, 2048)
        sends.append(pltpu.make_async_copy(out_s.at[:, at], out.at[:, at], sems.at[13 + quarter]))
        sends[-1].start()
    for send in sends:
        send.wait()


def scatter(me, idx, wire, local, sums):
    rows = sums[0].shape[0]
    return pl.pallas_call(
        scatter_kernel,
        out_shape=struct((rows, 8192), F32),
        in_specs=[SMEM] + [ANY] * 7,
        out_specs=ANY,
        scratch_shapes=[
            pltpu.VMEM(wire.shape, BF),
            pltpu.VMEM((4, rows, 2048), BF),
            pltpu.VMEM((96, rows, LANES), F32),
            pltpu.VMEM((rows * 8192 // FOLD_OUT, FOLD_OUT), F32),
            pltpu.VMEM((96, LANES), jnp.int32),
            pltpu.VMEM((64, rows, LANES), F32),
            pltpu.VMEM((rows, 8192), F32),
            pltpu.SemaphoreType.DMA((17,)),
        ],
        compiler_params=params(60),
        cost_estimate=cost(6.4e9, 5 << 20),
        name="scatter_rows",
    )(me, idx, wire, local, *sums)


def place_kernel(me_ref, a, b, c, d, out):
    for s, piece in enumerate((a, b, c, d)):
        at = pl.ds(pl.multiple_of(lax.rem(me_ref[0] + s, 4) * 2048, 2048), 2048)
        out[:, at] = piece[...]


def place(me, pieces):
    rows = pieces[0].shape[0]
    return pl.pallas_call(
        place_kernel,
        out_shape=struct((rows, 8192), BF),
        in_specs=[SMEM] + [VMEM] * 4,
        out_specs=VMEM,
        compiler_params=params(),
        cost_estimate=cost(1e6, 2 << 20),
        name="place",
    )(me, *pieces)


def final_kernel(returned, final, part_s, sems):
    Copies(returned, part_s, sems, 0, 1).wait()
    total = jnp.sum(part_s[:, 48:56, :].astype(F32), axis=0)
    final[...] = jnp.broadcast_to((total[0:4] + total[3:7])[None], final.shape)


def final_part(returned):
    return pl.pallas_call(
        final_kernel,
        out_shape=struct((64, 4, LANES), F32),
        in_specs=[ANY],
        out_specs=VMEM,
        scratch_shapes=[pltpu.VMEM(returned.shape, BF), pltpu.SemaphoreType.DMA((1,))],
        compiler_params=params(),
        cost_estimate=cost(1e6, 1 << 18),
        name="final_part",
    )(returned)


def unpack_kernel(everyone, grad_self, grad_neighbor, grad_bias, all_s, sem):
    copy = pltpu.make_async_copy(everyone, all_s, sem)
    copy.start()
    copy.wait()
    for h in range(2):
        at = pl.ds(h * LANES, LANES)
        grad_self[:, at] = all_s[0:32, h, :]
        grad_neighbor[:, at] = all_s[32:64, h, :]
    diagonal = lax.broadcasted_iota(jnp.int32, (64, LANES), 0) == lax.broadcasted_iota(
        jnp.int32, (64, LANES), 1
    )
    row = jnp.sum(jnp.where(diagonal, all_s[:, 2, :], 0.0), axis=0, keepdims=True)
    grad_bias[...] = row[:, 0:64]


def unpack(everyone):
    return pl.pallas_call(
        unpack_kernel,
        out_shape=[struct((32, 256), F32)] * 2 + [struct((1, 64), F32)],
        in_specs=[ANY],
        out_specs=[VMEM] * 3,
        scratch_shapes=[pltpu.VMEM(everyone.shape, F32), pltpu.SemaphoreType.DMA(())],
        compiler_params=params(),
        cost_estimate=cost(1e6, 1 << 18),
        name="unpack",
    )(everyone)


def exchange(pieces, sign):
    got = [pieces[0]]
    for s in range(1, 4):
        got.append(lax.ppermute(pieces[s], "feat", [(q, (q + sign * s) % 4) for q in range(4)]))
    return got


def per_device(
    quantized,
    node_scale,
    send_rows,
    send_count,
    tile_cols,
    edge_tiles,
    self_weight,
    neighbor_weight,
    hidden_bias,
    upstream,
):
    feat = lax.axis_index("feat").astype(jnp.int32)
    odd = lax.rem(lax.axis_index("dom").astype(jnp.int32), 2)
    me = feat.reshape(1)
    cols = tile_cols[0]

    feat_tiles, wire, idx, *blocks = gather(
        jnp.stack([feat, odd]),
        quantized,
        node_scale.reshape(1, -1),
        send_rows,
        send_count,
        upstream,
        self_weight,
        neighbor_weight,
        hidden_bias.reshape(1, -1),
    )
    halo = lax.all_to_all(wire, "dom", split_axis=0, concat_axis=0, tiled=True)
    pieces = exchange(blocks, 1)
    mask, degree = masks(edge_tiles)

    others, joined, chunk = aggregate(me, cols, feat_tiles, halo, degree, mask)
    aggs = exchange([aggregate_own(me, cols, joined, chunk, degree), *others], 1)
    backs, hiddens, sums = dense(me, pieces, aggs, degree)
    backs = exchange(backs, -1)
    begun = spread_own(me, cols, backs[0], chunk)
    local, back = spread(me, cols, begun, mask, backs)
    returned = lax.all_to_all(back, "dom", split_axis=0, concat_axis=0, tiled=True)
    local, hiddens, sums = lax.optimization_barrier((local, hiddens, sums))

    hidden = place(me, exchange(hiddens, -1))
    sums = exchange(sums, -1)
    everyone = lax.all_to_all(
        final_part(returned), "dom", split_axis=0, concat_axis=0, tiled=True
    )
    grad_features = scatter(me, idx, returned, local, sums)
    grad_self, grad_neighbor, grad_bias = unpack(everyone)
    return hidden, grad_features, grad_self, grad_neighbor, grad_bias.reshape(-1)


def solution(mesh):
    return jax.shard_map(
        per_device,
        mesh=mesh,
        in_specs=(
            P("feat", "dom"),
            P("dom"),
            P("dom", None, None),
            P("dom", None),
            P("dom", None, None),
            P("dom", None, None, None),
            P("feat", None),
            P("feat", None),
            P("feat"),
            P("feat", "dom"),
        ),
        out_specs=(P("feat", "dom"), P("feat", "dom"), P("feat", None), P("feat", None), P("feat")),
        check_vma=False,
    )
```

time: 556 us -> 148 us (0.27)
  waiting for transfers between devices: 234 us -> 37.6 us
  other arithmetic: 124 us -> 0.59 us
  local copies, waits for them, and re-layouts: 113 us -> 4.8 us
  Pallas kernels: 0 us -> 58.8 us
  matrix products: 44.2 us -> 0 us
  starting transfers between devices: 25 us -> 44.2 us
  between operations: 14 us -> 1.12 us
    scatter-add x2 -> x0, other arithmetic: 97.5 us -> none  [the longest x1 63.5 us: per_device(): jnp.zeros((feature_count, node_count), jnp.float32).at[:, flat_rows]]
    psum x1 -> x0, waiting for transfers between devices: 80.9 us -> none  [per_device(): lax.psum((local_self, local_neighbor, local_bias), 'dom')]
    unnamed x4 -> x0, waiting for transfers between devices: 77.4 us -> none
    pallas_call x0 -> x11, Pallas kernels: none -> 58.8 us  [the longest x1 12 us: gather(): pl.pallas_call(gather_kernel, out_shape=[struct((nodes // LANES, features...]
    all_gather x1 -> x0, waiting for transfers between devices: 50.5 us -> none  [per_device(): slope_full = lax.all_gather(slope, 'feat', axis=0, tiled=True)]
    gather x3 -> x0, local copies, waits for them, and re-layouts: 49.3 us -> none  [the longest x2 47.1 us: per_device(): outgoing = jnp.take(features, flat_rows, axis=1) * live_slots]
    dot_general x8 -> x0, matrix products: 44.2 us -> none  [the longest x1 9.32 us: tile_sum(): jnp.einsum('ftkj,tkij->fti', picked, mask_tiles, preferred_element_type=j...]
    unnamed x41 -> x47, local copies, waits for them, and re-layouts: 32.3 us -> 4.8 us
  transfers between devices with their start and end apart: 5 -> 18, of which waited for: 5 -> 10; matrix products, arithmetic and copies ran while one was open for 20% -> 0% of each run, Pallas kernels for 0% -> 22%
where the time goes in v2:
time: 148 us; the launch traced here: 147 us
  Pallas kernels  58.8 us (40%)
  starting transfers between devices  44.2 us (30%)
  waiting for transfers between devices  37.6 us (25%)
  local copies, waits for them, and re-layouts  4.8 us (3%)
    ppermute x15, waiting for transfers between devices, exchange(): lax.ppermute(pieces[s], 'feat', [(q, (q + sign * s) % 4) for q in range(4)])  22.5 us
    ppermute x15, starting transfers between devices, exchange(): lax.ppermute(pieces[s], 'feat', [(q, (q + sign * s) % 4) for q in range(4)])  18.3 us
    all_to_all x1, starting transfers between devices, per_device(): halo = lax.all_to_all(wire, 'dom', split_axis=0, concat_axis=0, tiled=True)  13.2 us
    pallas_call x1, Pallas kernels, gather(): pl.pallas_call(gather_kernel, out_shape=[struct((nodes // LANES, features...  12 us
    pallas_call x1, Pallas kernels, scatter(): pl.pallas_call(scatter_kernel, out_shape=struct((rows, 8192), F32), in_sp...  10.5 us
    pallas_call x1, Pallas kernels, masks(): pl.pallas_call(mask_kernel, out_shape=[struct((length,) + edges.shape[1:]...  10 us
    all_to_all x1, waiting for transfers between devices, per_device(): halo = lax.all_to_all(wire, 'dom', split_axis=0, concat_axis=0, tiled=True)  7.7 us
    all_to_all x1, waiting for transfers between devices, per_device(): lax.all_to_all(back, 'dom', split_axis=0, concat_axis=0, tiled=True)  7.42 us
  transfers between devices with their start and end apart: 18, of which 10 were waited for; matrix products, arithmetic and copies ran while one was open for 0% of the time, Pallas kernels for 22%

profile of v2, /device:TPU:1, one launch (start us, length us, event | category | flops | bytes accessed | tf_op | source)
XLA Modules:
  0.0 147.1 jit_solution(1170320394921156840)
XLA Ops:
  0.6 0.6 pad_add_fusion.where
  1.2 12.0 %gather_rows.1 = (bf16[64,32,128]{2,1,0:T(8,128)(2,1)}, bf16[64,48,128]{2,1,0:T(8,128)(2,1)}, s32[96,128]{1,0:T(8,128)}, bf16[128,2048]{1,0:T(8,128)(2,1)}, bf16...) custom-call(s32[2]{0:T(128)} %pad_add_fusion.where, bf16[32,8192]{1,0:T(8,128)(2,1)} %quantized.1, ...), custom_call_target="tpu_custom_call" | custom-call | flops 6400000000 | bytes 4194304 | tf_op jit(solution)/shard_map/gather_rows/pallas_call | solution.py:195
  13.3 13.2 %all-to-all-start = ((bf16[64,48,128]{2,1,0:T(8,128)(2,1)}), bf16[64,48,128]{2,1,0:T(8,128)(2,1)S(1)}, u32[]{:S(2)}, u32[]{:S(2)}) async-start(bf16[64,48,128]{2,1,0:T(8,128)(2,1)} %get-tuple-element.50), calls=%async_computation | async-start | bytes 1572864 | tf_op jit(solution)/shard_map/all_to_all | solution.py:766
  26.5 1.3 collective-permute-start
  27.7 2.5 %collective-permute-start.1 = (bf16[128,2048]{1,0:T(8,128)(2,1)}, bf16[128,2048]{1,0:T(8,128)(2,1)S(1)}, u32[]{:S(2)}, u32[]{:S(2)}) collective-permute-start(bf16[128,2048]{1,0:T(8,128)(2,1)} %get-tuple-element.47), channel_id=1, source_target_pairs={{0,2},{1,3},{2,0},{3,1},{4,6},{5,7},{6,4},{7,5},{8,10},{9,11},{10,... | collective-permute-start | bytes 1572872 | tf_op jit(solution)/shard_map/ppermute | solution.py:734
  30.2 1.2 collective-permute-start.2
  31.4 0.0 copy-done.7
  31.4 0.1 copy.15
  31.5 10.0 %mask_degree.1 = (bf16[384,4,128,128]{3,2,1,0:T(8,128)(2,1)}, f32[64,1,128]{2,1,0:T(1,128)}) custom-call(s32[64,4,128,128]{3,2,1,0:T(8,128)} %edges.1), custom_call_target="tpu_custom_call" | custom-call | flops 1000000000 | bytes 25165824 | tf_op jit(solution)/shard_map/mask_degree/pallas_call | solution.py:254
  41.5 7.7 %all-to-all-done.wire = bf16[64,48,128]{2,1,0:T(8,128)(2,1)S(1)} async-done(((bf16[64,48,128]{2,1,0:T(8,128)(2,1)}), bf16[64,48,128]{2,1,0:T(8,128)(2,1)S(1)}, u32[]{:S(2)}, u32[]{:S(2)}) %all-to-all-start) | async-done | bytes 786464 | tf_op jit(solution)/shard_map/all_to_all | solution.py:766
  49.2 0.8 copy-done.4
  50.0 6.2 %aggregate.1 = (bf16[32,2048]{1,0:T(8,128)(2,1)S(1)}, bf16[32,2048]{1,0:T(8,128)(2,1)S(1)}, bf16[32,2048]{1,0:T(8,128)(2,1)S(1)}, bf16[160,32,128]{2,1,0:T(8,128)(2,1)S(1)}, bf16[16,4,128,128]{3,2,1,0:T(8,128)(2,1)S(1)}) custom-call(s32[1]{0:T(128)} %bitcast.me.me_ref, s32[64,4]{1,0:T(8,128)S(1)} %bitcast.6, bf16[64,32,128]{2,1,0:T(8,128)(2,1)S(1)} %copy-done.2, ...), custom_call_target="tpu_custom_call" | custom-call | flops 3000000000 | bytes 12582912 | tf_op jit(solution)/shard_map/aggregate/pallas_call | solution.py:333
  56.2 1.3 collective-permute-start.3
  57.5 2.5 %collective-permute-start.4 = (bf16[32,2048]{1,0:T(8,128)(2,1)S(1)}, bf16[32,2048]{1,0:T(8,128)(2,1)S(1)}, u32[]{:S(2)}, u32[]{:S(2)}) collective-permute-start(bf16[32,2048]{1,0:T(8,128)(2,1)S(1)} %get-tuple-element.56), channel_id=1, source_target_pairs={{0,2},{1,3},{2,0},{3,1},{4,6},{5,7},{6,4},{7,5},{8,10},{9,11},{10,... | collective-permute-start | bytes 393224 | tf_op jit(solution)/shard_map/ppermute | solution.py:734
  59.9 0.0 collective-permute-done.refs_1_
  59.9 1.2 collective-permute-start.5
  61.1 1.9 %aggregate_own.1.refs_4_ = bf16[32,2048]{1,0:T(8,128)(2,1)S(1)} custom-call(s32[1]{0:T(128)} %bitcast.me.me_ref, s32[64,4]{1,0:T(8,128)S(1)} %bitcast.7, bf16[160,32,128]{2,1,0:T(8,128)(2,1)S(1)} %get-tuple-element.53.joined, bf16[16,4,128,128]{3,2,1,0:T(8,128)(2,1)S(1)} %get-tuple-element.54.chunk, f32[64,1,128]{2,1,0:T(1,128)S(1)} %copy-done.4), custom_call_target="tpu_custom_call" | custom-call | flops 1000000000 | bytes 4194304 | tf_op jit(solution)/shard_map/aggregate_own/pallas_call | solution.py:355
  63.0 0.6 copy-done.6
  63.6 0.0 collective-permute-done.1.refs_2_
  63.6 0.0 collective-permute-done.2.refs_3_
  63.6 0.0 copy-start.10
  63.6 0.0 collective-permute-done.3.refs_5_
  63.7 1.3 collective-permute-done.4.refs_6_
  65.0 0.4 collective-permute-done.5.refs_7_
  65.5 0.2 copy-done.20
  65.6 0.4 copy-done.22
  66.1 6.5 %dense.1 = (bf16[48,2048]{1,0:T(8,128)(2,1)}, bf16[48,2048]{1,0:T(8,128)(2,1)}, bf16[48,2048]{1,0:T(8,128)(2,1)}, bf16[48,2048]{1,0:T(8,128)(2,1)}, bf16[64,2048...) custom-call(s32[1]{0:T(128)} %bitcast.me.me_ref, ...), custom_call_target="tpu_custom_call" | custom-call | flops 1000000000 | bytes 5242880 | tf_op jit(solution)/shard_map/dense/pallas_call | solution.py:459
  72.6 2.7 %collective-permute-start.6 = (bf16[48,2048]{1,0:T(8,128)(2,1)}, bf16[48,2048]{1,0:T(8,128)(2,1)S(1)}, u32[]{:S(2)}, u32[]{:S(2)}) collective-permute-start(bf16[48,2048]{1,0:T(8,128)(2,1)} %get-tuple-element.59), channel_id=1, source_target_pairs={{0,3},{1,0},{2,1},{3,2},{4,7},{5,4},{6,5},{7,6},{8,11},{9,8},{10,9... | collective-permute-start | bytes 589832 | tf_op jit(solution)/shard_map/ppermute | solution.py:734
  75.2 0.3 collective-permute-start.7
  75.5 0.4 collective-permute-start.8
  75.9 0.9 copy-done.1
  76.8 1.7 %spread_own.1.begun = f32[160,32,128]{2,1,0:T(8,128)S(1)} custom-call(s32[1]{0:T(128)} %bitcast.me.me_ref, s32[64,4]{1,0:T(8,128)S(1)} %bitcast.8, bf16[48,2048]{1,0:T(8,128)(2,1)S(1)} %copy-done.1, bf16[16,4,128,128]{3,2,1,0:T(8,128)(2,1)S(1)} %get-tuple-element.54.chunk), custom_call_target="tpu_custom_call" | custom-call | flops 1000000000 | bytes 4194304 | tf_op jit(solution)/shard_map/spread_own/pallas_call | solution.py:525
  78.5 0.0 copy-start.13
  78.5 0.0 copy-start.12
  78.5 0.0 copy-start.11
  78.5 0.0 copy-start.16
  78.6 2.4 %collective-permute-done.6.refs_1_ = bf16[48,2048]{1,0:T(8,128)(2,1)S(1)} collective-permute-done((bf16[48,2048]{1,0:T(8,128)(2,1)}, bf16[48,2048]{1,0:T(8,128)(2,1)S(1)}, u32[]{:S(2)}, u32[]{:S(2)}) %collective-permute-start.6) | collective-permute-done | bytes 196640 | tf_op jit(solution)/shard_map/ppermute | solution.py:734
  81.0 0.6 collective-permute-done.7.refs_2_
  81.6 6.1 %collective-permute-done.8.refs_3_ = bf16[48,2048]{1,0:T(8,128)(2,1)S(1)} collective-permute-done((bf16[48,2048]{1,0:T(8,128)(2,1)}, bf16[48,2048]{1,0:T(8,128)(2,1)S(1)}, u32[]{:S(2)}, u32[]{:S(2)}) %collective-permute-start.8) | collective-permute-done | bytes 196640 | tf_op jit(solution)/shard_map/ppermute | solution.py:734
  87.6 7.1 %spread.1 = (f32[64,32,128]{2,1,0:T(8,128)S(1)}, bf16[64,56,128]{2,1,0:T(8,128)(2,1)}) custom-call(s32[1]{0:T(128)} %bitcast.me.me_ref, s32[64,4]{1,0:T(8,128)S(1)} %bitcast.9, f32[160,32,128]{2,1,0:T(8,128)S(1)} %spread_own.1.begun, bf16[384,4,128,128]{3,2,1,0:T(8,128)(2,1)} %get-tuple-element.52.mask, bf16[48,2048]{1,0:T(8,128)(2,1)S(1)} %copy-done.1, ...), custom_call_target="tpu_custom_call" | custom-call | flops 3000000000 | bytes 12582912 | tf_op jit(solution)/shard_map/spread/pallas_call | solution.py:572
  94.8 1.0 copy-done.5
  95.8 6.2 %all-to-all-start.1 = ((bf16[64,56,128]{2,1,0:T(8,128)(2,1)}), bf16[64,56,128]{2,1,0:T(8,128)(2,1)S(1)}, u32[]{:S(2)}, u32[]{:S(2)}) async-start(bf16[64,56,128]{2,1,0:T(8,128)(2,1)} %get-tuple-element.76), calls=%async_computation.1 | async-start | bytes 1835008 | tf_op jit(solution)/shard_map/all_to_all | solution.py:776
  102.0 0.4 collective-permute-start.9
  102.4 0.9 collective-permute-start.10
  103.3 0.5 collective-permute-start.11
  103.8 2.2 %collective-permute-start.12 = (bf16[32,2048]{1,0:T(8,128)(2,1)S(1)}, bf16[32,2048]{1,0:T(8,128)(2,1)S(1)}, u32[]{:S(2)}, u32[]{:S(2)}) collective-permute-start(bf16[32,2048]{1,0:T(8,128)(2,1)S(1)} %copy-done.16), channel_id=1, source_target_pairs={{0,3},{1,0},{2,1},{3,2},{4,7},{5,4},{6,5},{7,6},{8,11},{9,8},{10,9... | collective-permute-start | bytes 393224 | tf_op jit(solution)/shard_map/ppermute | solution.py:734
  106.1 1.2 collective-permute-start.13
  107.2 2.3 %collective-permute-done.9.b = bf16[64,2048]{1,0:T(8,128)(2,1)S(1)} collective-permute-done((bf16[64,2048]{1,0:T(8,128)(2,1)S(1)}, bf16[64,2048]{1,0:T(8,128)(2,1)S(1)}, u32[]{:S(2)}, u32[]{:S(2)}) %collective-permute-start.9) | collective-permute-done | bytes 262176 | tf_op jit(solution)/shard_map/ppermute | solution.py:734
  109.5 0.0 collective-permute-start.14
  109.5 1.5 %collective-permute-done.10.c = bf16[64,2048]{1,0:T(8,128)(2,1)S(1)} collective-permute-done((bf16[64,2048]{1,0:T(8,128)(2,1)S(1)}, bf16[64,2048]{1,0:T(8,128)(2,1)S(1)}, u32[]{:S(2)}, u32[]{:S(2)}) %collective-permute-start.10) | collective-permute-done | bytes 262176 | tf_op jit(solution)/shard_map/ppermute | solution.py:734
  111.1 7.8 %collective-permute-done.11.d = bf16[64,2048]{1,0:T(8,128)(2,1)S(1)} collective-permute-done((bf16[64,2048]{1,0:T(8,128)(2,1)S(1)}, bf16[64,2048]{1,0:T(8,128)(2,1)S(1)}, u32[]{:S(2)}, u32[]{:S(2)}) %collective-permute-start.11) | collective-permute-done | bytes 262176 | tf_op jit(solution)/shard_map/ppermute | solution.py:734
  118.8 1.0 place.1
  119.9 7.4 %all-to-all-done.1.wire.returned = bf16[64,56,128]{2,1,0:T(8,128)(2,1)S(1)} async-done(((bf16[64,56,128]{2,1,0:T(8,128)(2,1)}), bf16[64,56,128]{2,1,0:T(8,128)(2,1)S(1)}, u32[]{:S(2)}, u32[]{:S(2)}) %all-to-all-start.1) | async-done | bytes 917536 | tf_op jit(solution)/shard_map/all_to_all | solution.py:776
  127.3 1.0 final_part.1
  128.3 6.5 %all-to-all-start.2 = ((f32[64,4,128]{2,1,0:T(4,128)}), f32[64,4,128]{2,1,0:T(4,128)S(1)}, u32[]{:S(2)}, u32[]{:S(2)}) async-start(f32[64,4,128]{2,1,0:T(4,128)} %final_part.1), calls=%async_computation.2 | async-start | bytes 262144 | tf_op jit(solution)/shard_map/all_to_all | solution.py:781
  134.8 0.0 collective-permute-done.12.refs_1_
  134.8 0.0 collective-permute-done.13.refs_2_
  134.8 0.0 collective-permute-done.14.refs_3_
  134.9 0.6 copy-done.17
  135.5 0.1 copy-done.19
  135.5 0.0 copy-done.21
  135.6 10.5 %scatter_rows.1 = f32[32,8192]{1,0:T(8,128)} custom-call(s32[1]{0:T(128)} %bitcast.me.me_ref, s32[96,128]{1,0:T(8,128)} %get-tuple-element.75.idx, bf16[64,56,128]{2,1,0:T(8,128)(2,1)} %copy-done, f32[64,32,128]{2,1,0:T(8,128)} %copy-done.5, bf16[32,2048]{1,0:T(8,128)(2,1)} %get-tuple-element.78.refs_0_, bf16[32,2048]{1,0:T(8,128)(2,1)} %copy-done.17, ...), custom_call_target="tpu_custom_call" | custom-call | flops 6400000000 | bytes 5242880 | tf_op jit(solution)/shard_map/scatter_rows/pallas_call | solution.py:644
  146.1 0.0 all-to-all-done.2.everyone
  146.1 0.8 unpack.1
  (31 shorter events, 0.1 us)
Async XLA Ops:
  1.2 30.1 %copy-start.7 = (s32[1,64,4]{1,2,0:T(4,128)S(1)}, s32[1,64,4]{1,2,0:T(4,128)}, u32[]{:S(2)}) copy-start(s32[1,64,4]{1,2,0:T(4,128)} %param.14) | copy-start | bytes 3076
  13.3 35.9 %all-to-all-start = ((bf16[64,48,128]{2,1,0:T(8,128)(2,1)}), bf16[64,48,128]{2,1,0:T(8,128)(2,1)S(1)}, u32[]{:S(2)}, u32[]{:S(2)}) async-start(bf16[64,48,128]{2,1,0:T(8,128)(2,1)} %get-tuple-element.50), calls=%async_computation | async-start | bytes 1572864 | tf_op jit(solution)/shard_map/all_to_all | solution.py:766
  26.5 33.5 %collective-permute-start = (bf16[128,2048]{1,0:T(8,128)(2,1)}, bf16[128,2048]{1,0:T(8,128)(2,1)S(1)}, u32[]{:S(2)}, u32[]{:S(2)}) collective-permute-start(bf16[128,2048]{1,0:T(8,128)(2,1)} %get-tuple-element.46), channel_id=1, source_target_pairs={{0,1},{1,2},{2,3},{3,0},{4,5},{5,6},{6,7},{7,4},{8,9},{9,10},{10,1... | collective-permute-start | bytes 1572872 | tf_op jit(solution)/shard_map/ppermute | solution.py:734
  27.7 35.9 %collective-permute-start.1 = (bf16[128,2048]{1,0:T(8,128)(2,1)}, bf16[128,2048]{1,0:T(8,128)(2,1)S(1)}, u32[]{:S(2)}, u32[]{:S(2)}) collective-permute-start(bf16[128,2048]{1,0:T(8,128)(2,1)} %get-tuple-element.47), channel_id=1, source_target_pairs={{0,2},{1,3},{2,0},{3,1},{4,6},{5,7},{6,4},{7,5},{8,10},{9,11},{10,... | collective-permute-start | bytes 1572872 | tf_op jit(solution)/shard_map/ppermute | solution.py:734
  30.2 33.4 %collective-permute-start.2 = (bf16[128,2048]{1,0:T(8,128)(2,1)}, bf16[128,2048]{1,0:T(8,128)(2,1)S(1)}, u32[]{:S(2)}, u32[]{:S(2)}) collective-permute-start(bf16[128,2048]{1,0:T(8,128)(2,1)} %get-tuple-element.48), channel_id=1, source_target_pairs={{0,3},{1,0},{2,1},{3,2},{4,7},{5,4},{6,5},{7,6},{8,11},{9,8},{10,9... | collective-permute-start | bytes 1572872 | tf_op jit(solution)/shard_map/ppermute | solution.py:734
  31.4 17.8 %copy-start.2 = (bf16[64,32,128]{2,1,0:T(8,128)(2,1)S(1)}, bf16[64,32,128]{2,1,0:T(8,128)(2,1)}, u32[]{:S(2)}) copy-start(bf16[64,32,128]{2,1,0:T(8,128)(2,1)} %get-tuple-element.49.feat_tiles) | copy-start | bytes 1572868
  49.2 0.8 copy-start.4
  56.2 7.5 %collective-permute-start.3 = (bf16[32,2048]{1,0:T(8,128)(2,1)S(1)}, bf16[32,2048]{1,0:T(8,128)(2,1)S(1)}, u32[]{:S(2)}, u32[]{:S(2)}) collective-permute-start(bf16[32,2048]{1,0:T(8,128)(2,1)S(1)} %get-tuple-element.55), channel_id=1, source_target_pairs={{0,1},{1,2},{2,3},{3,0},{4,5},{5,6},{6,7},{7,4},{8,9},{9,10},{10,1... | collective-permute-start | bytes 393224 | tf_op jit(solution)/shard_map/ppermute | solution.py:734
  57.5 7.5 %collective-permute-start.4 = (bf16[32,2048]{1,0:T(8,128)(2,1)S(1)}, bf16[32,2048]{1,0:T(8,128)(2,1)S(1)}, u32[]{:S(2)}, u32[]{:S(2)}) collective-permute-start(bf16[32,2048]{1,0:T(8,128)(2,1)S(1)} %get-tuple-element.56), channel_id=1, source_target_pairs={{0,2},{1,3},{2,0},{3,1},{4,6},{5,7},{6,4},{7,5},{8,10},{9,11},{10,... | collective-permute-start | bytes 393224 | tf_op jit(solution)/shard_map/ppermute | solution.py:734
  59.9 5.5 %copy-start.8 = (bf16[128,2048]{1,0:T(8,128)(2,1)}, bf16[128,2048]{1,0:T(8,128)(2,1)S(1)}, u32[]{:S(2)}) copy-start(bf16[128,2048]{1,0:T(8,128)(2,1)S(1)} %collective-permute-done.refs_1_) | copy-start | bytes 1572868
  59.9 5.5 %collective-permute-start.5 = (bf16[32,2048]{1,0:T(8,128)(2,1)S(1)}, bf16[32,2048]{1,0:T(8,128)(2,1)S(1)}, u32[]{:S(2)}, u32[]{:S(2)}) collective-permute-start(bf16[32,2048]{1,0:T(8,128)(2,1)S(1)} %get-tuple-element.57), channel_id=1, source_target_pairs={{0,3},{1,0},{2,1},{3,2},{4,7},{5,4},{6,5},{7,6},{8,11},{9,8},{10,9... | collective-permute-start | bytes 393224 | tf_op jit(solution)/shard_map/ppermute | solution.py:734
  63.0 0.7 copy-start.6
  63.6 1.8 %copy-start.9 = (bf16[128,2048]{1,0:T(8,128)(2,1)}, bf16[128,2048]{1,0:T(8,128)(2,1)S(1)}, u32[]{:S(2)}) copy-start(bf16[128,2048]{1,0:T(8,128)(2,1)S(1)} %collective-permute-done.1.refs_2_) | copy-start | bytes 1572868
  63.6 1.8 %copy-start.10 = (bf16[128,2048]{1,0:T(8,128)(2,1)}, bf16[128,2048]{1,0:T(8,128)(2,1)S(1)}, u32[]{:S(2)}) copy-start(bf16[128,2048]{1,0:T(8,128)(2,1)S(1)} %collective-permute-done.2.refs_3_) | copy-start | bytes 1572868
  63.7 1.8 %copy-start.18 = (bf16[32,2048]{1,0:T(8,128)(2,1)}, bf16[32,2048]{1,0:T(8,128)(2,1)S(1)}, u32[]{:S(2)}) copy-start(bf16[32,2048]{1,0:T(8,128)(2,1)S(1)} %collective-permute-done.3.refs_5_) | copy-start | bytes 393220
  65.0 0.6 copy-start.20
  65.4 0.6 copy-start.22
  72.6 8.4 %collective-permute-start.6 = (bf16[48,2048]{1,0:T(8,128)(2,1)}, bf16[48,2048]{1,0:T(8,128)(2,1)S(1)}, u32[]{:S(2)}, u32[]{:S(2)}) collective-permute-start(bf16[48,2048]{1,0:T(8,128)(2,1)} %get-tuple-element.59), channel_id=1, source_target_pairs={{0,3},{1,0},{2,1},{3,2},{4,7},{5,4},{6,5},{7,6},{8,11},{9,8},{10,9... | collective-permute-start | bytes 589832 | tf_op jit(solution)/shard_map/ppermute | solution.py:734
  75.2 6.3 %collective-permute-start.7 = (bf16[48,2048]{1,0:T(8,128)(2,1)}, bf16[48,2048]{1,0:T(8,128)(2,1)S(1)}, u32[]{:S(2)}, u32[]{:S(2)}) collective-permute-start(bf16[48,2048]{1,0:T(8,128)(2,1)} %get-tuple-element.60), channel_id=1, source_target_pairs={{0,2},{1,3},{2,0},{3,1},{4,6},{5,7},{6,4},{7,5},{8,10},{9,11},{10,... | collective-permute-start | bytes 589832 | tf_op jit(solution)/shard_map/ppermute | solution.py:734
  75.5 12.1 %collective-permute-start.8 = (bf16[48,2048]{1,0:T(8,128)(2,1)}, bf16[48,2048]{1,0:T(8,128)(2,1)S(1)}, u32[]{:S(2)}, u32[]{:S(2)}) collective-permute-start(bf16[48,2048]{1,0:T(8,128)(2,1)} %get-tuple-element.61), channel_id=1, source_target_pairs={{0,1},{1,2},{2,3},{3,0},{4,5},{5,6},{6,7},{7,4},{8,9},{9,10},{10,1... | collective-permute-start | bytes 589832 | tf_op jit(solution)/shard_map/ppermute | solution.py:734
  75.9 0.9 copy-start.1
  78.5 23.5 %copy-start.13 = (bf16[64,2048]{1,0:T(8,128)(2,1)S(1)}, bf16[64,2048]{1,0:T(8,128)(2,1)}, u32[]{:S(2)}) copy-start(bf16[64,2048]{1,0:T(8,128)(2,1)} %get-tuple-element.72) | copy-start | bytes 786436
  78.5 23.9 %copy-start.12 = (bf16[64,2048]{1,0:T(8,128)(2,1)S(1)}, bf16[64,2048]{1,0:T(8,128)(2,1)}, u32[]{:S(2)}) copy-start(bf16[64,2048]{1,0:T(8,128)(2,1)} %get-tuple-element.73) | copy-start | bytes 786436
  78.5 24.7 %copy-start.11 = (bf16[64,2048]{1,0:T(8,128)(2,1)S(1)}, bf16[64,2048]{1,0:T(8,128)(2,1)}, u32[]{:S(2)}) copy-start(bf16[64,2048]{1,0:T(8,128)(2,1)} %get-tuple-element.74) | copy-start | bytes 786436
  78.5 25.3 %copy-start.16 = (bf16[32,2048]{1,0:T(8,128)(2,1)S(1)}, bf16[32,2048]{1,0:T(8,128)(2,1)}, u32[]{:S(2)}) copy-start(bf16[32,2048]{1,0:T(8,128)(2,1)} %get-tuple-element.79) | copy-start | bytes 393220
  78.6 27.5 %copy-start.15 = (bf16[32,2048]{1,0:T(8,128)(2,1)S(1)}, bf16[32,2048]{1,0:T(8,128)(2,1)}, u32[]{:S(2)}) copy-start(bf16[32,2048]{1,0:T(8,128)(2,1)} %get-tuple-element.80) | copy-start | bytes 393220
  78.6 31.0 %copy-start.14 = (bf16[32,2048]{1,0:T(8,128)(2,1)S(1)}, bf16[32,2048]{1,0:T(8,128)(2,1)}, u32[]{:S(2)}) copy-start(bf16[32,2048]{1,0:T(8,128)(2,1)} %get-tuple-element.81) | copy-start | bytes 393220
  78.6 40.3 %copy-start.3 = (bf16[64,2048]{1,0:T(8,128)(2,1)S(1)}, bf16[64,2048]{1,0:T(8,128)(2,1)}, u32[]{:S(2)}) copy-start(bf16[64,2048]{1,0:T(8,128)(2,1)} %get-tuple-element.71.a) | copy-start | bytes 786436
  94.8 1.0 copy-start.5
  95.8 31.5 %all-to-all-start.1 = ((bf16[64,56,128]{2,1,0:T(8,128)(2,1)}), bf16[64,56,128]{2,1,0:T(8,128)(2,1)S(1)}, u32[]{:S(2)}, u32[]{:S(2)}) async-start(bf16[64,56,128]{2,1,0:T(8,128)(2,1)} %get-tuple-element.76), calls=%async_computation.1 | async-start | bytes 1835008 | tf_op jit(solution)/shard_map/all_to_all | solution.py:776
  102.0 7.5 %collective-permute-start.9 = (bf16[64,2048]{1,0:T(8,128)(2,1)S(1)}, bf16[64,2048]{1,0:T(8,128)(2,1)S(1)}, u32[]{:S(2)}, u32[]{:S(2)}) collective-permute-start(bf16[64,2048]{1,0:T(8,128)(2,1)S(1)} %copy-done.13), channel_id=1, source_target_pairs={{0,3},{1,0},{2,1},{3,2},{4,7},{5,4},{6,5},{7,6},{8,11},{9,8},{10,9... | collective-permute-start | bytes 786440 | tf_op jit(solution)/shard_map/ppermute | solution.py:734
  102.4 8.7 %collective-permute-start.10 = (bf16[64,2048]{1,0:T(8,128)(2,1)S(1)}, bf16[64,2048]{1,0:T(8,128)(2,1)S(1)}, u32[]{:S(2)}, u32[]{:S(2)}) collective-permute-start(bf16[64,2048]{1,0:T(8,128)(2,1)S(1)} %copy-done.12), channel_id=1, source_target_pairs={{0,2},{1,3},{2,0},{3,1},{4,6},{5,7},{6,4},{7,5},{8,10},{9,11},{10,... | collective-permute-start | bytes 786440 | tf_op jit(solution)/shard_map/ppermute | solution.py:734
  103.3 15.6 %collective-permute-start.11 = (bf16[64,2048]{1,0:T(8,128)(2,1)S(1)}, bf16[64,2048]{1,0:T(8,128)(2,1)S(1)}, u32[]{:S(2)}, u32[]{:S(2)}) collective-permute-start(bf16[64,2048]{1,0:T(8,128)(2,1)S(1)} %copy-done.11), channel_id=1, source_target_pairs={{0,1},{1,2},{2,3},{3,0},{4,5},{5,6},{6,7},{7,4},{8,9},{9,10},{10,1... | collective-permute-start | bytes 786440 | tf_op jit(solution)/shard_map/ppermute | solution.py:734
  103.8 31.0 %collective-permute-start.12 = (bf16[32,2048]{1,0:T(8,128)(2,1)S(1)}, bf16[32,2048]{1,0:T(8,128)(2,1)S(1)}, u32[]{:S(2)}, u32[]{:S(2)}) collective-permute-start(bf16[32,2048]{1,0:T(8,128)(2,1)S(1)} %copy-done.16), channel_id=1, source_target_pairs={{0,3},{1,0},{2,1},{3,2},{4,7},{5,4},{6,5},{7,6},{8,11},{9,8},{10,9... | collective-permute-start | bytes 393224 | tf_op jit(solution)/shard_map/ppermute | solution.py:734
  106.1 28.8 %collective-permute-start.13 = (bf16[32,2048]{1,0:T(8,128)(2,1)S(1)}, bf16[32,2048]{1,0:T(8,128)(2,1)S(1)}, u32[]{:S(2)}, u32[]{:S(2)}) collective-permute-start(bf16[32,2048]{1,0:T(8,128)(2,1)S(1)} %copy-done.15), channel_id=1, source_target_pairs={{0,2},{1,3},{2,0},{3,1},{4,6},{5,7},{6,4},{7,5},{8,10},{9,11},{10,... | collective-permute-start | bytes 393224 | tf_op jit(solution)/shard_map/ppermute | solution.py:734
  109.5 25.3 %collective-permute-start.14 = (bf16[32,2048]{1,0:T(8,128)(2,1)S(1)}, bf16[32,2048]{1,0:T(8,128)(2,1)S(1)}, u32[]{:S(2)}, u32[]{:S(2)}) collective-permute-start(bf16[32,2048]{1,0:T(8,128)(2,1)S(1)} %copy-done.14), channel_id=1, source_target_pairs={{0,1},{1,2},{2,3},{3,0},{4,5},{5,6},{6,7},{7,4},{8,9},{9,10},{10,1... | collective-permute-start | bytes 393224 | tf_op jit(solution)/shard_map/ppermute | solution.py:734
  127.3 7.6 %copy-start = (bf16[64,56,128]{2,1,0:T(8,128)(2,1)}, bf16[64,56,128]{2,1,0:T(8,128)(2,1)S(1)}, u32[]{:S(2)}) copy-start(bf16[64,56,128]{2,1,0:T(8,128)(2,1)S(1)} %all-to-all-done.1.wire.returned) | copy-start | bytes 2752516
  128.3 17.7 %all-to-all-start.2 = ((f32[64,4,128]{2,1,0:T(4,128)}), f32[64,4,128]{2,1,0:T(4,128)S(1)}, u32[]{:S(2)}, u32[]{:S(2)}) async-start(f32[64,4,128]{2,1,0:T(4,128)} %final_part.1), calls=%async_computation.2 | async-start | bytes 262144 | tf_op jit(solution)/shard_map/all_to_all | solution.py:781
  134.8 0.7 copy-start.17
  134.8 0.7 copy-start.19
  134.9 0.7 copy-start.21

commit v3 on v2

--- a/solution.py
+++ b/solution.py
@@ -16,7 +16,7 @@
 GROUP = 4
 
 
-def params(mib=20):
+def params(mib=48):
     return pltpu.CompilerParams(vmem_limit_bytes=mib << 20)
 
 
@@ -74,12 +74,16 @@
     return jax.ShapeDtypeStruct(shape, dtype)
 
 
+DEGREE_ROWS = 36864
+LOCAL_TILES = 1152
+
+
 FOLD_IN = 256
 FOLD_OUT = 512
 
 
 def gather_kernel(
-    where, quantized, scale, rows, counts, upstream, self_w, neighbor_w, bias,
+    quantized, scale, rows, counts, upstream, self_w, neighbor_w, bias,
     tiles_out, wire_out, idx_out, b0, b1, b2, b3,
     q_s, s_s, r_s, c_s, sw_s, nw_s, bias_s, rest_s, folded, feat_tiles, wire, idx, block_s, sems,
 ):
@@ -93,7 +97,8 @@
         copy.start()
     for copy in copies:
         copy.wait()
-    me, odd = where[0], where[1]
+    me = lax.axis_index("feat").astype(jnp.int32)
+    odd = lax.rem(lax.axis_index("dom").astype(jnp.int32), 2)
     ups = []
     for s in range(4):
         at = pl.ds(pl.multiple_of(lax.rem(me + s, 4) * 2048, 2048), 2048)
@@ -159,38 +164,38 @@
         send.start()
 
     def pick(base):
-        row = jnp.concatenate([idx[pl.ds(base + t, 1), :] for t in range(8)], axis=1)
+        row = jnp.concatenate([idx[pl.ds(base + t, 1), :] for t in range(16)], axis=1)
         hi, lo = row >> 8, row & (FOLD_IN - 1)
         out = jnp.dot(folded[...], one_hot_rows(lo, FOLD_IN), preferred_element_type=F32)
         total = jnp.zeros((feature_count, row.shape[1]), F32)
         for c in range(fold):
             total = total + jnp.where(hi == c, out[c * feature_count : (c + 1) * feature_count], 0.0)
-        return [total[:, t * LANES : (t + 1) * LANES] for t in range(8)]
-
-    @pl.loop(0, 8, unroll=2)
-    def _(g):
-        tiles = pick(g * 8)
-        for t in range(8):
-            wire[g * 8 + t, 0:feature_count, :] = tiles[t].astype(BF)
+        return [total[:, t * LANES : (t + 1) * LANES] for t in range(16)]
 
     @pl.loop(0, 4, unroll=2)
     def _(g):
-        tiles = pick(64 + g * 8)
-        for t in range(8):
+        tiles = pick(g * 16)
+        for t in range(16):
+            wire[g * 16 + t, 0:feature_count, :] = tiles[t].astype(BF)
+
+    @pl.loop(0, 2, unroll=2)
+    def _(g):
+        tiles = pick(64 + g * 16)
+        for t in range(16):
             even, odd_part = split_rest(tiles[t])
-            wire[(g * 8 + t) * 2, feature_count:48, :] = even.astype(BF)
-            wire[(g * 8 + t) * 2 + 1, feature_count:48, :] = odd_part.astype(BF)
-        at = pl.ds(g * 16, 16)
+            wire[(g * 16 + t) * 2, feature_count:48, :] = even.astype(BF)
+            wire[(g * 16 + t) * 2 + 1, feature_count:48, :] = odd_part.astype(BF)
+        at = pl.ds(g * 32, 32)
         pltpu.make_async_copy(wire.at[at], wire_out.at[at], sems.at[13 + g]).start()
 
     for send in sends:
         send.wait()
-    for g in range(4):
-        at = pl.ds(g * 16, 16)
+    for g in range(2):
+        at = pl.ds(g * 32, 32)
         pltpu.make_async_copy(wire.at[at], wire_out.at[at], sems.at[13 + g]).wait()
 
 
-def gather(where, quantized, scale, rows, counts, *early):
+def gather(quantized, scale, rows, counts, *early):
     features, nodes = quantized.shape
     return pl.pallas_call(
         gather_kernel,
@@ -200,7 +205,7 @@
             struct((96, LANES), jnp.int32),
         ]
         + [struct((128, nodes // 4), BF)] * 4,
-        in_specs=[SMEM] + [ANY] * 8,
+        in_specs=[ANY] * 8,
         out_specs=[ANY] * 7,
         scratch_shapes=[
             pltpu.VMEM(quantized.shape, BF),
@@ -221,10 +226,10 @@
         compiler_params=params(60),
         cost_estimate=cost(6.4e9, 4 << 20),
         name="gather_rows",
-    )(where, quantized, scale, rows, counts, *early)
-
-
-def mask_kernel(edges, mask, degree, edges_s, mask_s, in_sems, out_sems):
+    )(quantized, scale, rows, counts, *early)
+
+
+def mask_kernel(edges, mask, degree_out, edges_s, mask_s, degree, in_sems, out_sems):
     steps = edges.shape[0] // GROUP
     ones = jnp.ones((8, LANES), BF)
     loads = []
@@ -244,21 +249,26 @@
                 ones, total, (((1,), (1,)), ((), ())), preferred_element_type=F32
             )[0:1]
         stores[i].start()
+    stores.append(
+        pltpu.make_async_copy(degree, degree_out.at[pl.ds(0, degree.shape[0])], in_sems.at[0])
+    )
+    stores[-1].start()
     for store in stores:
         store.wait()
 
 
 def masks(edges):
     tiles = edges.shape[0]
-    length = 6 * tiles
+    length = 3 * tiles
     return pl.pallas_call(
         mask_kernel,
-        out_shape=[struct((length,) + edges.shape[1:], BF), struct((tiles, 1, LANES), F32)],
+        out_shape=[struct((length,) + edges.shape[1:], BF), struct((DEGREE_ROWS, 1, LANES), F32)],
         in_specs=[ANY],
-        out_specs=[ANY, VMEM],
+        out_specs=[ANY, ANY],
         scratch_shapes=[
             pltpu.VMEM(edges.shape, jnp.int32),
             pltpu.VMEM(edges.shape, BF),
+            pltpu.VMEM((tiles, 1, LANES), F32),
             pltpu.SemaphoreType.DMA((tiles // GROUP,)),
             pltpu.SemaphoreType.DMA((tiles // GROUP,)),
         ],
@@ -301,10 +311,11 @@
 ORDER = (2, 1, 3)
 
 
-def aggregate_kernel(me, cols, feat_tiles, wire, degree, mask, *refs):
-    outs, (joined, own_chunk, wire_s, chunks, sems) = refs[0:3], refs[3:]
+def aggregate_kernel(me, cols, feat_tiles, wire, degree_in, mask, *refs):
+    outs, (joined, own_chunk, degree, wire_s, chunks, sems) = refs[0:3], refs[3:]
     arriving = Copies(wire, wire_s, sems, 0, 2)
-    local = feat_tiles.shape[0]
+    counts = Copies(degree_in.at[pl.ds(0, 64)], degree, sems, 3, 1)
+    local = 64
     own = Copies(feat_tiles, joined.at[pl.ds(0, local)], sems, 2, 1)
     tiles = [
         fetch(me, shift, mask, chunks.at[n], sems, 8 + PARTS * n) for n, shift in enumerate(ORDER)
@@ -319,6 +330,7 @@
         joined[local + 3 * q + 1] = join_rest(even[32:48].astype(F32), odd[32:48].astype(F32)).astype(BF)
 
     own.wait()
+    counts.wait()
     for n, shift in enumerate(ORDER):
         tiles[n].wait()
         begin = lax.rem(me[0] + shift, 4) * QUARTER
@@ -329,12 +341,13 @@
 
 
 def aggregate(me, cols, feat_tiles, wire, degree, mask):
-    local, rows, _ = feat_tiles.shape
+    rows = feat_tiles.shape[1]
     got = pl.pallas_call(
         aggregate_kernel,
-        out_shape=[struct((rows, 2048), BF)] * 3 + [struct((local + 96, rows, LANES), BF), CHUNK],
-        in_specs=[SMEM, SMEM, ANY, ANY, VMEM, ANY],
-        out_specs=[VMEM] * 5,
+        out_shape=[struct((rows, 2048), BF)] * 3 + [struct((160, rows, LANES), BF), CHUNK]
+        + [struct((64, 1, LANES), F32)],
+        in_specs=[SMEM, SMEM] + [ANY] * 4,
+        out_specs=[VMEM] * 6,
         scratch_shapes=[
             pltpu.VMEM(wire.shape, BF),
             pltpu.VMEM((3,) + CHUNK.shape, BF),
@@ -344,7 +357,7 @@
         cost_estimate=cost(3e9, 12 << 20),
         name="aggregate",
     )(me, cols, feat_tiles, wire, degree, mask)
-    return got[0:3], got[3], got[4]
+    return got[0:3], got[3], got[4], got[5]
 
 
 def aggregate_own_kernel(me, cols, joined, chunk, degree, out):
@@ -442,14 +455,15 @@
     high = bias_row.astype(BF).astype(F32)
     for b in range(4):
         for n, grad in enumerate((feat_grad, agg_grad)):
-            for h in range(2):
-                first = b * 32 + h * 16
-                at = slice((2 * n + h) * 256, (2 * n + h + 1) * 256)
-                back_s[b, 32:48, at] = grad[first : first + 16].astype(BF)
-        back_s[b, 32:48, 1024:1280] = jnp.broadcast_to(high, (16, 256)).astype(BF)
-        back_s[b, 32:48, 1280:1536] = jnp.broadcast_to(bias_row - high, (16, 256)).astype(BF)
-        back_s[b, 32:48, 1536:] = jnp.zeros((16, nodes - 1536), BF)
-    send(backs, back_s, 48, 8)
+            for h in range(4):
+                first = b * 32 + h * 8
+                at = slice((4 * n + h) * 256, (4 * n + h + 1) * 256)
+                back_s[b, 32:40, at] = grad[first : first + 8].astype(BF)
+        own = slice(b * 64, (b + 1) * 64)
+        both_parts = jnp.concatenate([high[:, own], (bias_row - high)[:, own]], axis=1)
+        back_s[b, 0:32, nodes:] = jnp.zeros((32, LANES), BF)
+        back_s[b, 32:40, nodes:] = jnp.broadcast_to(both_parts, (8, LANES)).astype(BF)
+    send(backs, back_s, 40, 8)
     for copy in sends:
         copy.wait()
 
@@ -458,7 +472,7 @@
     nodes = aggs[0].shape[1]
     got = pl.pallas_call(
         dense_kernel,
-        out_shape=[struct((48, nodes), BF)] * 4
+        out_shape=[struct((40, nodes + LANES), BF)] * 4
         + [struct((64, nodes), BF)] * 4
         + [struct((32, nodes), BF)] * 4,
         in_specs=[SMEM] + [ANY] * 8 + [VMEM],
@@ -468,7 +482,7 @@
             pltpu.VMEM((128, nodes), BF),
             pltpu.VMEM((256, nodes), BF),
             pltpu.VMEM((256, nodes), BF),
-            pltpu.VMEM((4, 48, nodes), BF),
+            pltpu.VMEM((4, 40, nodes + LANES), BF),
             pltpu.VMEM((128, nodes), BF),
             pltpu.SemaphoreType.DMA((20,)),
         ],
@@ -479,14 +493,7 @@
     return got[0:4], got[4:8], got[8:12]
 
 
-def own_quarter(me, row):
-    half = jnp.where(me >= 2, row[:, LANES:], row[:, 0:LANES])
-    half = jnp.broadcast_to(half, (8, LANES))
-    return jnp.where(lax.rem(me, 2) == 1, pltpu.roll(half, 64, 1), half)[0:1, 0:64]
-
-
-def pack_grads(me, grad, bias, pack_s):
-    row = own_quarter(me, bias)
+def pack_grads(grad, row, pack_s):
     diagonal = lax.broadcasted_iota(jnp.int32, (64, 64), 0) == lax.broadcasted_iota(
         jnp.int32, (64, 64), 1
     )
@@ -547,11 +554,11 @@
         pieces[s].wait()
         tiles[s - 1].wait()
         spread_tiles(begin, cols, back_s.at[s], chunks.at[s - 1], total)
-    own = Copies(total.at[pl.ds(0, 64)], local, sems, 4 + PARTS, 2)
+    own = Copies(total.at[pl.ds(0, 64)], local.at[pl.ds(0, 64)], sems, 4 + PARTS, 2)
     pieces[0].wait()
-    grads = sum(back_s[s, 32:48, 0:1536].astype(F32) for s in range(4))
-    grad = jnp.concatenate([grads[:, n * 256 : (n + 1) * 256] for n in range(4)], axis=0)
-    pack_grads(me[0], grad, grads[0:1, 1024:1280] + grads[0:1, 1280:1536], pack_s)
+    grads = sum(back_s[s, 32:40, :].astype(F32) for s in range(4))
+    grad = jnp.concatenate([grads[:, n * 256 : (n + 1) * 256] for n in range(8)], axis=0)
+    pack_grads(grad, grads[0:1, 2048:2112] + grads[0:1, 2112:2176], pack_s)
     wire[:, 48:56, :] = pack_s[...].astype(BF)
 
     @pl.loop(0, 32, unroll=8)
@@ -571,7 +578,7 @@
     _, rows, _ = begun.shape
     return pl.pallas_call(
         spread_kernel,
-        out_shape=[struct((64, rows, LANES), F32), struct((64, 56, LANES), BF)],
+        out_shape=[struct((LOCAL_TILES, rows, LANES), F32), struct((64, 56, LANES), BF)],
         in_specs=[SMEM, SMEM, VMEM] + [ANY] * 5,
         out_specs=[ANY] * 2,
         scratch_shapes=[
@@ -593,7 +600,7 @@
     me = me_ref[0]
     index = Copies(idx, idx_s, sems, 0, 1)
     first = Copies(wire, wire_s, sems, 1, 2)
-    later = [Copies(local, own_s, sems, 5, 2)]
+    later = [Copies(local.at[pl.ds(0, 64)], own_s, sems, 5, 2)]
     for s in range(4):
         later.append(Copies(sums[s], sum_s.at[lax.rem(me + s, 4)], sems, 9 + s, 1))
     nodes = out.shape[1]
@@ -609,7 +616,7 @@
         ret[2 * q + 1] = odd[0:32].astype(F32)
         ret[64 + q] = join_rest(even[32:48].astype(F32), odd[32:48].astype(F32))
 
-    @pl.loop(0, 6)
+    @pl.loop(0, 6, unroll=2)
     def _(g):
         row = jnp.concatenate([idx_s[pl.ds(g * 16 + t, 1), :] for t in range(16)], axis=1)
         hi, lo = row >> 9, row & (FOLD_OUT - 1)
@@ -656,7 +663,7 @@
             pltpu.VMEM((rows, 8192), F32),
             pltpu.SemaphoreType.DMA((17,)),
         ],
-        compiler_params=params(60),
+        compiler_params=params(),
         cost_estimate=cost(6.4e9, 5 << 20),
         name="scatter_rows",
     )(me, idx, wire, local, *sums)
@@ -681,9 +688,8 @@
     )(me, *pieces)
 
 
-def final_kernel(returned, final, part_s, sems):
-    Copies(returned, part_s, sems, 0, 1).wait()
-    total = jnp.sum(part_s[:, 48:56, :].astype(F32), axis=0)
+def final_kernel(returned, final):
+    total = jnp.sum(returned[:, 48:56, :].astype(F32), axis=0)
     final[...] = jnp.broadcast_to((total[0:4] + total[3:7])[None], final.shape)
 
 
@@ -691,9 +697,8 @@
     return pl.pallas_call(
         final_kernel,
         out_shape=struct((64, 4, LANES), F32),
-        in_specs=[ANY],
+        in_specs=[VMEM],
         out_specs=VMEM,
-        scratch_shapes=[pltpu.VMEM(returned.shape, BF), pltpu.SemaphoreType.DMA((1,))],
         compiler_params=params(),
         cost_estimate=cost(1e6, 1 << 18),
         name="final_part",
@@ -748,12 +753,10 @@
     upstream,
 ):
     feat = lax.axis_index("feat").astype(jnp.int32)
-    odd = lax.rem(lax.axis_index("dom").astype(jnp.int32), 2)
     me = feat.reshape(1)
     cols = tile_cols[0]
 
     feat_tiles, wire, idx, *blocks = gather(
-        jnp.stack([feat, odd]),
         quantized,
         node_scale.reshape(1, -1),
         send_rows,
@@ -767,7 +770,7 @@
     pieces = exchange(blocks, 1)
     mask, degree = masks(edge_tiles)
 
-    others, joined, chunk = aggregate(me, cols, feat_tiles, halo, degree, mask)
+    others, joined, chunk, degree = aggregate(me, cols, feat_tiles, halo, degree, mask)
     aggs = exchange([aggregate_own(me, cols, joined, chunk, degree), *others], 1)
     backs, hiddens, sums = dense(me, pieces, aggs, degree)
     backs = exchange(backs, -1)

time: 148 us -> 143 us (0.966)
  local copies, waits for them, and re-layouts: 4.8 us -> 2.34 us
  Pallas kernels: 58.8 us -> 56.4 us
    unnamed x47 -> x41, local copies, waits for them, and re-layouts: 4.8 us -> 2.34 us
  transfers between devices with their start and end apart: 18 -> 18, of which waited for: 10 -> 11; matrix products, arithmetic and copies ran while one was open for 0% -> 0% of each run, Pallas kernels for 22% -> 22%
where the time goes in v3:
time: 143 us
  Pallas kernels  56.4 us (39%)
  starting transfers between devices  44.8 us (31%)
  waiting for transfers between devices  38.1 us (27%)
  local copies, waits for them, and re-layouts  2.34 us (2%)
    ppermute x15, waiting for transfers between devices, exchange(): lax.ppermute(pieces[s], 'feat', [(q, (q + sign * s) % 4) for q in range(4)])  21.2 us
    ppermute x15, starting transfers between devices, exchange(): lax.ppermute(pieces[s], 'feat', [(q, (q + sign * s) % 4) for q in range(4)])  18.5 us
    all_to_all x1, starting transfers between devices, per_device(): halo = lax.all_to_all(wire, 'dom', split_axis=0, concat_axis=0, tiled=True)  13.3 us
    pallas_call x1, Pallas kernels, gather(): pl.pallas_call(gather_kernel, out_shape=[struct((nodes // LANES, features...  11 us
    pallas_call x1, Pallas kernels, scatter(): pl.pallas_call(scatter_kernel, out_shape=struct((rows, 8192), F32), in_sp...  10 us
    pallas_call x1, Pallas kernels, masks(): pl.pallas_call(mask_kernel, out_shape=[struct((length,) + edges.shape[1:]...  9.38 us
    all_to_all x1, waiting for transfers between devices, per_device(): halo = lax.all_to_all(wire, 'dom', split_axis=0, concat_axis=0, tiled=True)  8.37 us
    all_to_all x1, waiting for transfers between devices, per_device(): lax.all_to_all(back, 'dom', split_axis=0, concat_axis=0, tiled=True)  7.45 us
  transfers between devices with their start and end apart: 18, of which 11 were waited for; matrix products, arithmetic and copies ran while one was open for 0% of the time, Pallas kernels for 22%

profile of v3, /device:TPU:1, one launch (start us, length us, event | category | flops | bytes accessed | tf_op | source)
XLA Modules:
  0.0 142.7 jit_solution(18760376278352831)
XLA Ops:
  0.6 11.0 %gather_rows.1 = (bf16[64,32,128]{2,1,0:T(8,128)(2,1)}, bf16[64,48,128]{2,1,0:T(8,128)(2,1)}, s32[96,128]{1,0:T(8,128)}, bf16[128,2048]{1,0:T(8,128)(2,1)}, bf16...) custom-call(bf16[32,8192]{1,0:T(8,128)(2,1)} %quantized.1, f32[1,8192]{1,0:T(1,128)} %bitcast.9, ...), custom_call_target="tpu_custom_call" | custom-call | flops 6400000000 | bytes 4194304 | tf_op jit(solution)/shard_map/gather_rows/pallas_call | solution.py:200
  11.6 0.0 copy-start.1
  11.6 13.3 %all-to-all-start = ((bf16[64,48,128]{2,1,0:T(8,128)(2,1)}), bf16[64,48,128]{2,1,0:T(8,128)(2,1)S(1)}, u32[]{:S(2)}, u32[]{:S(2)}) async-start(bf16[64,48,128]{2,1,0:T(8,128)(2,1)} %get-tuple-element.51), calls=%async_computation | async-start | bytes 1572864 | tf_op jit(solution)/shard_map/all_to_all | solution.py:769
  24.9 1.3 collective-permute-start
  26.2 2.4 %collective-permute-start.1 = (bf16[128,2048]{1,0:T(8,128)(2,1)}, bf16[128,2048]{1,0:T(8,128)(2,1)S(1)}, u32[]{:S(2)}, u32[]{:S(2)}) collective-permute-start(bf16[128,2048]{1,0:T(8,128)(2,1)} %get-tuple-element.48), channel_id=1, source_target_pairs={{0,2},{1,3},{2,0},{3,1},{4,6},{5,7},{6,4},{7,5},{8,10},{9,11},{10,... | collective-permute-start | bytes 1572872 | tf_op jit(solution)/shard_map/ppermute | solution.py:739
  28.7 1.2 collective-permute-start.2
  29.8 0.1 copy.15
  29.9 9.4 %mask_degree.1 = (bf16[192,4,128,128]{3,2,1,0:T(8,128)(2,1)}, f32[36864,1,128]{2,1,0:T(1,128)}) custom-call(s32[64,4,128,128]{3,2,1,0:T(8,128)} %edges.1), custom_call_target="tpu_custom_call" | custom-call | flops 1000000000 | bytes 25165824 | tf_op jit(solution)/shard_map/mask_degree/pallas_call | solution.py:263
  39.3 8.4 %all-to-all-done.wire = bf16[64,48,128]{2,1,0:T(8,128)(2,1)S(1)} async-done(((bf16[64,48,128]{2,1,0:T(8,128)(2,1)}), bf16[64,48,128]{2,1,0:T(8,128)(2,1)S(1)}, u32[]{:S(2)}, u32[]{:S(2)}) %all-to-all-start) | async-done | bytes 786464 | tf_op jit(solution)/shard_map/all_to_all | solution.py:769
  47.7 6.2 %aggregate.1 = (bf16[32,2048]{1,0:T(8,128)(2,1)S(1)}, bf16[32,2048]{1,0:T(8,128)(2,1)S(1)}, bf16[32,2048]{1,0:T(8,128)(2,1)S(1)}, bf16[160,32,128]{2,1,0:T(8,128...) custom-call(s32[1]{0:T(128)} %bitcast.me.me_ref, s32[64,4]{1,0:T(8,128)S(1)} %bitcast.5, ...), custom_call_target="tpu_custom_call" | custom-call | flops 3000000000 | bytes 12582912 | tf_op jit(solution)/shard_map/aggregate/pallas_call | solution.py:345
  53.9 0.0 copy-start.3
  53.9 1.5 %collective-permute-start.3 = (bf16[32,2048]{1,0:T(8,128)(2,1)S(1)}, bf16[32,2048]{1,0:T(8,128)(2,1)S(1)}, u32[]{:S(2)}, u32[]{:S(2)}) collective-permute-start(bf16[32,2048]{1,0:T(8,128)(2,1)S(1)} %get-tuple-element.57), channel_id=1, source_target_pairs={{0,1},{1,2},{2,3},{3,0},{4,5},{5,6},{6,7},{7,4},{8,9},{9,10},{10,1... | collective-permute-start | bytes 393224 | tf_op jit(solution)/shard_map/ppermute | solution.py:739
  55.4 2.4 %collective-permute-start.4 = (bf16[32,2048]{1,0:T(8,128)(2,1)S(1)}, bf16[32,2048]{1,0:T(8,128)(2,1)S(1)}, u32[]{:S(2)}, u32[]{:S(2)}) collective-permute-start(bf16[32,2048]{1,0:T(8,128)(2,1)S(1)} %get-tuple-element.58), channel_id=1, source_target_pairs={{0,2},{1,3},{2,0},{3,1},{4,6},{5,7},{6,4},{7,5},{8,10},{9,11},{10,... | collective-permute-start | bytes 393224 | tf_op jit(solution)/shard_map/ppermute | solution.py:739
  57.8 0.0 collective-permute-done.refs_1_
  57.8 1.2 collective-permute-start.5
  59.0 1.9 %aggregate_own.1.refs_4_ = bf16[32,2048]{1,0:T(8,128)(2,1)S(1)} custom-call(s32[1]{0:T(128)} %bitcast.me.me_ref, s32[64,4]{1,0:T(8,128)S(1)} %bitcast.6, bf16[160,32,128]{2,1,0:T(8,128)(2,1)S(1)} %get-tuple-element.54.joined, bf16[16,4,128,128]{3,2,1,0:T(8,128)(2,1)S(1)} %get-tuple-element.55.chunk, f32[64,1,128]{2,1,0:T(1,128)S(1)} %get-tuple-element.56.degree.refs_8_), custom_call_target="tpu_custom_call" | custom-call | flops 1000000000 | bytes 4194304 | tf_op jit(solution)/shard_map/aggregate_own/pallas_call | solution.py:368
  60.9 0.0 copy-start.4
  60.9 0.6 copy-done.4
  61.5 0.0 collective-permute-done.1.refs_2_
  61.5 0.0 collective-permute-done.2.refs_3_
  61.5 0.0 copy-start.10
  61.5 0.0 collective-permute-done.3.refs_5_
  61.6 1.3 collective-permute-done.4.refs_6_
  62.9 0.4 collective-permute-done.5.refs_7_
  63.4 0.0 copy-done.3
  63.4 0.0 copy-done.9
  63.4 0.2 copy-done.18
  63.6 0.4 copy-done.19
  64.0 6.8 %dense.1 = (bf16[40,2176]{1,0:T(8,128)(2,1)}, bf16[40,2176]{1,0:T(8,128)(2,1)}, bf16[40,2176]{1,0:T(8,128)(2,1)}, bf16[40,2176]{1,0:T(8,128)(2,1)}, bf16[64,2048...) custom-call(s32[1]{0:T(128)} %bitcast.me.me_ref, ...), custom_call_target="tpu_custom_call" | custom-call | flops 1000000000 | bytes 5242880 | tf_op jit(solution)/shard_map/dense/pallas_call | solution.py:473
  70.8 2.7 %collective-permute-start.6 = (bf16[40,2176]{1,0:T(8,128)(2,1)}, bf16[40,2176]{1,0:T(8,128)(2,1)S(1)}, u32[]{:S(2)}, u32[]{:S(2)}) collective-permute-start(bf16[40,2176]{1,0:T(8,128)(2,1)} %get-tuple-element.61), channel_id=1, source_target_pairs={{0,3},{1,0},{2,1},{3,2},{4,7},{5,4},{6,5},{7,6},{8,11},{9,8},{10,9... | collective-permute-start | bytes 522248 | tf_op jit(solution)/shard_map/ppermute | solution.py:739
  73.5 0.3 collective-permute-start.7
  73.8 0.4 collective-permute-start.8
  74.2 0.9 copy-done
  75.1 0.0 copy-start.15
  75.1 0.0 copy-start.14
  75.1 0.0 copy-start.2
  75.1 1.6 %spread_own.1.begun = f32[160,32,128]{2,1,0:T(8,128)S(1)} custom-call(s32[1]{0:T(128)} %bitcast.me.me_ref, s32[64,4]{1,0:T(8,128)S(1)} %bitcast.7, bf16[40,2176]{1,0:T(8,128)(2,1)S(1)} %copy-done, bf16[16,4,128,128]{3,2,1,0:T(8,128)(2,1)S(1)} %get-tuple-element.55.chunk), custom_call_target="tpu_custom_call" | custom-call | flops 1000000000 | bytes 4194304 | tf_op jit(solution)/shard_map/spread_own/pallas_call | solution.py:532
  76.8 2.1 %collective-permute-done.6.refs_1_ = bf16[40,2176]{1,0:T(8,128)(2,1)S(1)} collective-permute-done((bf16[40,2176]{1,0:T(8,128)(2,1)}, bf16[40,2176]{1,0:T(8,128)(2,1)S(1)}, u32[]{:S(2)}, u32[]{:S(2)}) %collective-permute-start.6) | collective-permute-done | bytes 174112 | tf_op jit(solution)/shard_map/ppermute | solution.py:739
  78.9 0.7 collective-permute-done.7.refs_2_
  79.6 5.1 %collective-permute-done.8.refs_3_ = bf16[40,2176]{1,0:T(8,128)(2,1)S(1)} collective-permute-done((bf16[40,2176]{1,0:T(8,128)(2,1)}, bf16[40,2176]{1,0:T(8,128)(2,1)S(1)}, u32[]{:S(2)}, u32[]{:S(2)}) %collective-permute-start.8) | collective-permute-done | bytes 174112 | tf_op jit(solution)/shard_map/ppermute | solution.py:739
  84.6 6.9 %spread.1 = (f32[1152,32,128]{2,1,0:T(8,128)}, bf16[64,56,128]{2,1,0:T(8,128)(2,1)}) custom-call(s32[1]{0:T(128)} %bitcast.me.me_ref, s32[64,4]{1,0:T(8,128)S(1)} %bitcast.8, f32[160,32,128]{2,1,0:T(8,128)S(1)} %spread_own.1.begun, bf16[192,4,128,128]{3,2,1,0:T(8,128)(2,1)} %get-tuple-element.53.mask, bf16[40,2176]{1,0:T(8,128)(2,1)S(1)} %copy-done, ...), custom_call_target="tpu_custom_call" | custom-call | flops 3000000000 | bytes 12582912 | tf_op jit(solution)/shard_map/spread/pallas_call | solution.py:579
  91.6 6.5 %all-to-all-start.1 = ((bf16[64,56,128]{2,1,0:T(8,128)(2,1)}), bf16[64,56,128]{2,1,0:T(8,128)(2,1)S(1)}, u32[]{:S(2)}, u32[]{:S(2)}) async-start(bf16[64,56,128]{2,1,0:T(8,128)(2,1)} %get-tuple-element.78), calls=%async_computation.1 | async-start | bytes 1835008 | tf_op jit(solution)/shard_map/all_to_all | solution.py:779
  98.1 0.4 collective-permute-start.9
  98.5 0.9 collective-permute-start.10
  99.3 0.6 collective-permute-start.11
  99.9 2.4 %collective-permute-start.12 = (bf16[32,2048]{1,0:T(8,128)(2,1)S(1)}, bf16[32,2048]{1,0:T(8,128)(2,1)S(1)}, u32[]{:S(2)}, u32[]{:S(2)}) collective-permute-start(bf16[32,2048]{1,0:T(8,128)(2,1)S(1)} %copy-done.16), channel_id=1, source_target_pairs={{0,3},{1,0},{2,1},{3,2},{4,7},{5,4},{6,5},{7,6},{8,11},{9,8},{10,9... | collective-permute-start | bytes 393224 | tf_op jit(solution)/shard_map/ppermute | solution.py:739
  102.3 0.0 copy-done.15
  102.3 1.0 collective-permute-start.13
  103.3 2.3 %collective-permute-done.9.b = bf16[64,2048]{1,0:T(8,128)(2,1)S(1)} collective-permute-done((bf16[64,2048]{1,0:T(8,128)(2,1)S(1)}, bf16[64,2048]{1,0:T(8,128)(2,1)S(1)}, u32[]{:S(2)}, u32[]{:S(2)}) %collective-permute-start.9) | collective-permute-done | bytes 262176 | tf_op jit(solution)/shard_map/ppermute | solution.py:739
  105.6 0.0 collective-permute-start.14
  105.6 1.5 %collective-permute-done.10.c = bf16[64,2048]{1,0:T(8,128)(2,1)S(1)} collective-permute-done((bf16[64,2048]{1,0:T(8,128)(2,1)S(1)}, bf16[64,2048]{1,0:T(8,128)(2,1)S(1)}, u32[]{:S(2)}, u32[]{:S(2)}) %collective-permute-start.10) | collective-permute-done | bytes 262176 | tf_op jit(solution)/shard_map/ppermute | solution.py:739
  107.1 7.8 %collective-permute-done.11.d = bf16[64,2048]{1,0:T(8,128)(2,1)S(1)} collective-permute-done((bf16[64,2048]{1,0:T(8,128)(2,1)S(1)}, bf16[64,2048]{1,0:T(8,128)(2,1)S(1)}, u32[]{:S(2)}, u32[]{:S(2)}) %collective-permute-start.11) | collective-permute-done | bytes 262176 | tf_op jit(solution)/shard_map/ppermute | solution.py:739
  114.9 0.0 copy-done.2
  114.9 1.0 place.1
  115.9 7.5 %all-to-all-done.1.wire.returned = bf16[64,56,128]{2,1,0:T(8,128)(2,1)S(1)} async-done(((bf16[64,56,128]{2,1,0:T(8,128)(2,1)}), bf16[64,56,128]{2,1,0:T(8,128)(2,1)S(1)}, u32[]{:S(2)}, u32[]{:S(2)}) %all-to-all-start.1) | async-done | bytes 917536 | tf_op jit(solution)/shard_map/all_to_all | solution.py:779
  123.4 0.7 final_part.1
  124.1 6.5 %all-to-all-start.2 = ((f32[64,4,128]{2,1,0:T(4,128)}), f32[64,4,128]{2,1,0:T(4,128)S(1)}, u32[]{:S(2)}, u32[]{:S(2)}) async-start(f32[64,4,128]{2,1,0:T(4,128)} %final_part.1), calls=%async_computation.2 | async-start | bytes 262144 | tf_op jit(solution)/shard_map/all_to_all | solution.py:784
  130.6 0.0 collective-permute-done.12.refs_1_
  130.6 0.0 collective-permute-done.13.refs_2_
  130.6 0.0 collective-permute-done.14.refs_3_
  130.6 0.0 copy-done.5
  130.6 10.0 %scatter_rows.1 = f32[32,8192]{1,0:T(8,128)} custom-call(s32[1]{0:T(128)} %bitcast.me.me_ref, s32[96,128]{1,0:T(8,128)S(1)} %copy-done.6, bf16[64,56,128]{2,1,0:T(8,128)(2,1)S(1)} %all-to-all-done.1.wire.returned, f32[1152,32,128]{2,1,0:T(8,128)} %get-tuple-element.79.local, bf16[32,2048]{1,0:T(8,128)(2,1)S(1)} %copy-done.5, ...), custom_call_target="tpu_custom_call" | custom-call | flops 6400000000 | bytes 5242880 | tf_op jit(solution)/shard_map/scatter_rows/pallas_call | solution.py:651
  140.7 1.0 all-to-all-done.2.everyone
  141.7 0.8 unpack.1
  (24 shorter events, 0.0 us)
Async XLA Ops:
  0.6 29.2 %copy-start.7 = (s32[1,64,4]{1,2,0:T(4,128)S(1)}, s32[1,64,4]{1,2,0:T(4,128)}, u32[]{:S(2)}) copy-start(s32[1,64,4]{1,2,0:T(4,128)} %param.14) | copy-start | bytes 3076
  11.6 36.1 %copy-start.1 = (bf16[64,32,128]{2,1,0:T(8,128)(2,1)S(1)}, bf16[64,32,128]{2,1,0:T(8,128)(2,1)}, u32[]{:S(2)}) copy-start(bf16[64,32,128]{2,1,0:T(8,128)(2,1)} %get-tuple-element.50.feat_tiles) | copy-start | bytes 1572868
  11.6 36.1 %all-to-all-start = ((bf16[64,48,128]{2,1,0:T(8,128)(2,1)}), bf16[64,48,128]{2,1,0:T(8,128)(2,1)S(1)}, u32[]{:S(2)}, u32[]{:S(2)}) async-start(bf16[64,48,128]{2,1,0:T(8,128)(2,1)} %get-tuple-element.51), calls=%async_computation | async-start | bytes 1572864 | tf_op jit(solution)/shard_map/all_to_all | solution.py:769
  24.9 32.9 %collective-permute-start = (bf16[128,2048]{1,0:T(8,128)(2,1)}, bf16[128,2048]{1,0:T(8,128)(2,1)S(1)}, u32[]{:S(2)}, u32[]{:S(2)}) collective-permute-start(bf16[128,2048]{1,0:T(8,128)(2,1)} %get-tuple-element.47), channel_id=1, source_target_pairs={{0,1},{1,2},{2,3},{3,0},{4,5},{5,6},{6,7},{7,4},{8,9},{9,10},{10,1... | collective-permute-start | bytes 1572872 | tf_op jit(solution)/shard_map/ppermute | solution.py:739
  26.2 35.3 %collective-permute-start.1 = (bf16[128,2048]{1,0:T(8,128)(2,1)}, bf16[128,2048]{1,0:T(8,128)(2,1)S(1)}, u32[]{:S(2)}, u32[]{:S(2)}) collective-permute-start(bf16[128,2048]{1,0:T(8,128)(2,1)} %get-tuple-element.48), channel_id=1, source_target_pairs={{0,2},{1,3},{2,0},{3,1},{4,6},{5,7},{6,4},{7,5},{8,10},{9,11},{10,... | collective-permute-start | bytes 1572872 | tf_op jit(solution)/shard_map/ppermute | solution.py:739
  28.7 32.9 %collective-permute-start.2 = (bf16[128,2048]{1,0:T(8,128)(2,1)}, bf16[128,2048]{1,0:T(8,128)(2,1)S(1)}, u32[]{:S(2)}, u32[]{:S(2)}) collective-permute-start(bf16[128,2048]{1,0:T(8,128)(2,1)} %get-tuple-element.49), channel_id=1, source_target_pairs={{0,3},{1,0},{2,1},{3,2},{4,7},{5,4},{6,5},{7,6},{8,11},{9,8},{10,9... | collective-permute-start | bytes 1572872 | tf_op jit(solution)/shard_map/ppermute | solution.py:739
  53.9 9.5 %copy-start.3 = (f32[64,1,128]{2,1,0:T(1,128)}, f32[64,1,128]{2,1,0:T(1,128)S(1)}, u32[]{:S(2)}) copy-start(f32[64,1,128]{2,1,0:T(1,128)S(1)} %get-tuple-element.56.degree.refs_8_) | copy-start | bytes 98308
  53.9 7.6 %collective-permute-start.3 = (bf16[32,2048]{1,0:T(8,128)(2,1)S(1)}, bf16[32,2048]{1,0:T(8,128)(2,1)S(1)}, u32[]{:S(2)}, u32[]{:S(2)}) collective-permute-start(bf16[32,2048]{1,0:T(8,128)(2,1)S(1)} %get-tuple-element.57), channel_id=1, source_target_pairs={{0,1},{1,2},{2,3},{3,0},{4,5},{5,6},{6,7},{7,4},{8,9},{9,10},{10,1... | collective-permute-start | bytes 393224 | tf_op jit(solution)/shard_map/ppermute | solution.py:739
  55.4 7.5 %collective-permute-start.4 = (bf16[32,2048]{1,0:T(8,128)(2,1)S(1)}, bf16[32,2048]{1,0:T(8,128)(2,1)S(1)}, u32[]{:S(2)}, u32[]{:S(2)}) collective-permute-start(bf16[32,2048]{1,0:T(8,128)(2,1)S(1)} %get-tuple-element.58), channel_id=1, source_target_pairs={{0,2},{1,3},{2,0},{3,1},{4,6},{5,7},{6,4},{7,5},{8,10},{9,11},{10,... | collective-permute-start | bytes 393224 | tf_op jit(solution)/shard_map/ppermute | solution.py:739
  57.8 5.5 %copy-start.8 = (bf16[128,2048]{1,0:T(8,128)(2,1)}, bf16[128,2048]{1,0:T(8,128)(2,1)S(1)}, u32[]{:S(2)}) copy-start(bf16[128,2048]{1,0:T(8,128)(2,1)S(1)} %collective-permute-done.refs_1_) | copy-start | bytes 1572868
  57.8 5.5 %collective-permute-start.5 = (bf16[32,2048]{1,0:T(8,128)(2,1)S(1)}, bf16[32,2048]{1,0:T(8,128)(2,1)S(1)}, u32[]{:S(2)}, u32[]{:S(2)}) collective-permute-start(bf16[32,2048]{1,0:T(8,128)(2,1)S(1)} %get-tuple-element.59), channel_id=1, source_target_pairs={{0,3},{1,0},{2,1},{3,2},{4,7},{5,4},{6,5},{7,6},{8,11},{9,8},{10,9... | collective-permute-start | bytes 393224 | tf_op jit(solution)/shard_map/ppermute | solution.py:739
  60.9 0.6 copy-start.4
  61.5 1.8 %copy-start.9 = (bf16[128,2048]{1,0:T(8,128)(2,1)}, bf16[128,2048]{1,0:T(8,128)(2,1)S(1)}, u32[]{:S(2)}) copy-start(bf16[128,2048]{1,0:T(8,128)(2,1)S(1)} %collective-permute-done.1.refs_2_) | copy-start | bytes 1572868
  61.5 1.8 %copy-start.10 = (bf16[128,2048]{1,0:T(8,128)(2,1)}, bf16[128,2048]{1,0:T(8,128)(2,1)S(1)}, u32[]{:S(2)}) copy-start(bf16[128,2048]{1,0:T(8,128)(2,1)S(1)} %collective-permute-done.2.refs_3_) | copy-start | bytes 1572868
  61.5 1.8 %copy-start.17 = (bf16[32,2048]{1,0:T(8,128)(2,1)}, bf16[32,2048]{1,0:T(8,128)(2,1)S(1)}, u32[]{:S(2)}) copy-start(bf16[32,2048]{1,0:T(8,128)(2,1)S(1)} %collective-permute-done.3.refs_5_) | copy-start | bytes 393220
  62.9 0.7 copy-start.18
  63.4 0.7 copy-start.19
  70.8 8.1 %collective-permute-start.6 = (bf16[40,2176]{1,0:T(8,128)(2,1)}, bf16[40,2176]{1,0:T(8,128)(2,1)S(1)}, u32[]{:S(2)}, u32[]{:S(2)}) collective-permute-start(bf16[40,2176]{1,0:T(8,128)(2,1)} %get-tuple-element.61), channel_id=1, source_target_pairs={{0,3},{1,0},{2,1},{3,2},{4,7},{5,4},{6,5},{7,6},{8,11},{9,8},{10,9... | collective-permute-start | bytes 522248 | tf_op jit(solution)/shard_map/ppermute | solution.py:739
  73.5 6.1 %collective-permute-start.7 = (bf16[40,2176]{1,0:T(8,128)(2,1)}, bf16[40,2176]{1,0:T(8,128)(2,1)S(1)}, u32[]{:S(2)}, u32[]{:S(2)}) collective-permute-start(bf16[40,2176]{1,0:T(8,128)(2,1)} %get-tuple-element.62), channel_id=1, source_target_pairs={{0,2},{1,3},{2,0},{3,1},{4,6},{5,7},{6,4},{7,5},{8,10},{9,11},{10,... | collective-permute-start | bytes 522248 | tf_op jit(solution)/shard_map/ppermute | solution.py:739
  73.8 10.9 %collective-permute-start.8 = (bf16[40,2176]{1,0:T(8,128)(2,1)}, bf16[40,2176]{1,0:T(8,128)(2,1)S(1)}, u32[]{:S(2)}, u32[]{:S(2)}) collective-permute-start(bf16[40,2176]{1,0:T(8,128)(2,1)} %get-tuple-element.63), channel_id=1, source_target_pairs={{0,1},{1,2},{2,3},{3,0},{4,5},{5,6},{6,7},{7,4},{8,9},{9,10},{10,1... | collective-permute-start | bytes 522248 | tf_op jit(solution)/shard_map/ppermute | solution.py:739
  74.2 0.9 copy-start
  75.1 23.0 %copy-start.13 = (bf16[64,2048]{1,0:T(8,128)(2,1)S(1)}, bf16[64,2048]{1,0:T(8,128)(2,1)}, u32[]{:S(2)}) copy-start(bf16[64,2048]{1,0:T(8,128)(2,1)} %get-tuple-element.74) | copy-start | bytes 786436
  75.1 23.4 %copy-start.12 = (bf16[64,2048]{1,0:T(8,128)(2,1)S(1)}, bf16[64,2048]{1,0:T(8,128)(2,1)}, u32[]{:S(2)}) copy-start(bf16[64,2048]{1,0:T(8,128)(2,1)} %get-tuple-element.75) | copy-start | bytes 786436
  75.1 24.2 %copy-start.11 = (bf16[64,2048]{1,0:T(8,128)(2,1)S(1)}, bf16[64,2048]{1,0:T(8,128)(2,1)}, u32[]{:S(2)}) copy-start(bf16[64,2048]{1,0:T(8,128)(2,1)} %get-tuple-element.76) | copy-start | bytes 786436
  75.1 24.8 %copy-start.16 = (bf16[32,2048]{1,0:T(8,128)(2,1)S(1)}, bf16[32,2048]{1,0:T(8,128)(2,1)}, u32[]{:S(2)}) copy-start(bf16[32,2048]{1,0:T(8,128)(2,1)} %get-tuple-element.81) | copy-start | bytes 393220
  75.1 27.3 %copy-start.15 = (bf16[32,2048]{1,0:T(8,128)(2,1)S(1)}, bf16[32,2048]{1,0:T(8,128)(2,1)}, u32[]{:S(2)}) copy-start(bf16[32,2048]{1,0:T(8,128)(2,1)} %get-tuple-element.82) | copy-start | bytes 393220
  75.1 30.5 %copy-start.14 = (bf16[32,2048]{1,0:T(8,128)(2,1)S(1)}, bf16[32,2048]{1,0:T(8,128)(2,1)}, u32[]{:S(2)}) copy-start(bf16[32,2048]{1,0:T(8,128)(2,1)} %get-tuple-element.83) | copy-start | bytes 393220
  75.1 39.8 %copy-start.2 = (bf16[64,2048]{1,0:T(8,128)(2,1)S(1)}, bf16[64,2048]{1,0:T(8,128)(2,1)}, u32[]{:S(2)}) copy-start(bf16[64,2048]{1,0:T(8,128)(2,1)} %get-tuple-element.73.a) | copy-start | bytes 786436
  76.8 53.9 %copy-start.5 = (bf16[32,2048]{1,0:T(8,128)(2,1)S(1)}, bf16[32,2048]{1,0:T(8,128)(2,1)}, u32[]{:S(2)}) copy-start(bf16[32,2048]{1,0:T(8,128)(2,1)} %get-tuple-element.80.refs_0_) | copy-start | bytes 393220
  76.8 53.9 %copy-start.6 = (s32[96,128]{1,0:T(8,128)S(1)}, s32[96,128]{1,0:T(8,128)}, u32[]{:S(2)}) copy-start(s32[96,128]{1,0:T(8,128)} %get-tuple-element.77.idx) | copy-start | bytes 147460
  91.6 31.8 %all-to-all-start.1 = ((bf16[64,56,128]{2,1,0:T(8,128)(2,1)}), bf16[64,56,128]{2,1,0:T(8,128)(2,1)S(1)}, u32[]{:S(2)}, u32[]{:S(2)}) async-start(bf16[64,56,128]{2,1,0:T(8,128)(2,1)} %get-tuple-element.78), calls=%async_computation.1 | async-start | bytes 1835008 | tf_op jit(solution)/shard_map/all_to_all | solution.py:779
  98.1 7.5 %collective-permute-start.9 = (bf16[64,2048]{1,0:T(8,128)(2,1)S(1)}, bf16[64,2048]{1,0:T(8,128)(2,1)S(1)}, u32[]{:S(2)}, u32[]{:S(2)}) collective-permute-start(bf16[64,2048]{1,0:T(8,128)(2,1)S(1)} %copy-done.13), channel_id=1, source_target_pairs={{0,3},{1,0},{2,1},{3,2},{4,7},{5,4},{6,5},{7,6},{8,11},{9,8},{10,9... | collective-permute-start | bytes 786440 | tf_op jit(solution)/shard_map/ppermute | solution.py:739
  98.5 8.7 %collective-permute-start.10 = (bf16[64,2048]{1,0:T(8,128)(2,1)S(1)}, bf16[64,2048]{1,0:T(8,128)(2,1)S(1)}, u32[]{:S(2)}, u32[]{:S(2)}) collective-permute-start(bf16[64,2048]{1,0:T(8,128)(2,1)S(1)} %copy-done.12), channel_id=1, source_target_pairs={{0,2},{1,3},{2,0},{3,1},{4,6},{5,7},{6,4},{7,5},{8,10},{9,11},{10,... | collective-permute-start | bytes 786440 | tf_op jit(solution)/shard_map/ppermute | solution.py:739
  99.3 15.6 %collective-permute-start.11 = (bf16[64,2048]{1,0:T(8,128)(2,1)S(1)}, bf16[64,2048]{1,0:T(8,128)(2,1)S(1)}, u32[]{:S(2)}, u32[]{:S(2)}) collective-permute-start(bf16[64,2048]{1,0:T(8,128)(2,1)S(1)} %copy-done.11), channel_id=1, source_target_pairs={{0,1},{1,2},{2,3},{3,0},{4,5},{5,6},{6,7},{7,4},{8,9},{9,10},{10,1... | collective-permute-start | bytes 786440 | tf_op jit(solution)/shard_map/ppermute | solution.py:739
  99.9 30.7 %collective-permute-start.12 = (bf16[32,2048]{1,0:T(8,128)(2,1)S(1)}, bf16[32,2048]{1,0:T(8,128)(2,1)S(1)}, u32[]{:S(2)}, u32[]{:S(2)}) collective-permute-start(bf16[32,2048]{1,0:T(8,128)(2,1)S(1)} %copy-done.16), channel_id=1, source_target_pairs={{0,3},{1,0},{2,1},{3,2},{4,7},{5,4},{6,5},{7,6},{8,11},{9,8},{10,9... | collective-permute-start | bytes 393224 | tf_op jit(solution)/shard_map/ppermute | solution.py:739
  102.3 28.3 %collective-permute-start.13 = (bf16[32,2048]{1,0:T(8,128)(2,1)S(1)}, bf16[32,2048]{1,0:T(8,128)(2,1)S(1)}, u32[]{:S(2)}, u32[]{:S(2)}) collective-permute-start(bf16[32,2048]{1,0:T(8,128)(2,1)S(1)} %copy-done.15), channel_id=1, source_target_pairs={{0,2},{1,3},{2,0},{3,1},{4,6},{5,7},{6,4},{7,5},{8,10},{9,11},{10,... | collective-permute-start | bytes 393224 | tf_op jit(solution)/shard_map/ppermute | solution.py:739
  105.6 25.0 %collective-permute-start.14 = (bf16[32,2048]{1,0:T(8,128)(2,1)S(1)}, bf16[32,2048]{1,0:T(8,128)(2,1)S(1)}, u32[]{:S(2)}, u32[]{:S(2)}) collective-permute-start(bf16[32,2048]{1,0:T(8,128)(2,1)S(1)} %copy-done.14), channel_id=1, source_target_pairs={{0,1},{1,2},{2,3},{3,0},{4,5},{5,6},{6,7},{7,4},{8,9},{9,10},{10,1... | collective-permute-start | bytes 393224 | tf_op jit(solution)/shard_map/ppermute | solution.py:739
  124.1 17.6 %all-to-all-start.2 = ((f32[64,4,128]{2,1,0:T(4,128)}), f32[64,4,128]{2,1,0:T(4,128)S(1)}, u32[]{:S(2)}, u32[]{:S(2)}) async-start(f32[64,4,128]{2,1,0:T(4,128)} %final_part.1), calls=%async_computation.2 | async-start | bytes 262144 | tf_op jit(solution)/shard_map/all_to_all | solution.py:784

commit v4 on v3

--- a/solution.py
+++ b/solution.py
@@ -16,7 +16,7 @@
 GROUP = 4
 
 
-def params(mib=48):
+def params(mib=40):
     return pltpu.CompilerParams(vmem_limit_bytes=mib << 20)
 
 
@@ -74,8 +74,8 @@
     return jax.ShapeDtypeStruct(shape, dtype)
 
 
-DEGREE_ROWS = 36864
-LOCAL_TILES = 1152
+DEGREE_ROWS = 53248
+LOCAL_TILES = 1664
 
 
 FOLD_IN = 256
@@ -259,7 +259,7 @@
 
 def masks(edges):
     tiles = edges.shape[0]
-    length = 3 * tiles
+    length = 4 * tiles
     return pl.pallas_call(
         mask_kernel,
         out_shape=[struct((length,) + edges.shape[1:], BF), struct((DEGREE_ROWS, 1, LANES), F32)],
@@ -312,19 +312,17 @@
 
 
 def aggregate_kernel(me, cols, feat_tiles, wire, degree_in, mask, *refs):
-    outs, (joined, own_chunk, degree, wire_s, chunks, sems) = refs[0:3], refs[3:]
-    arriving = Copies(wire, wire_s, sems, 0, 2)
+    outs, (joined, own_chunk, degree, chunks, sems) = refs[0:3], refs[3:]
     counts = Copies(degree_in.at[pl.ds(0, 64)], degree, sems, 3, 1)
     local = 64
     own = Copies(feat_tiles, joined.at[pl.ds(0, local)], sems, 2, 1)
     tiles = [
         fetch(me, shift, mask, chunks.at[n], sems, 8 + PARTS * n) for n, shift in enumerate(ORDER)
     ]
-    arriving.wait()
 
     @pl.loop(0, 32, unroll=8)
     def _(q):
-        even, odd = wire_s[2 * q], wire_s[2 * q + 1]
+        even, odd = wire[2 * q], wire[2 * q + 1]
         joined[local + 3 * q] = even[0:32]
         joined[local + 3 * q + 2] = odd[0:32]
         joined[local + 3 * q + 1] = join_rest(even[32:48].astype(F32), odd[32:48].astype(F32)).astype(BF)
@@ -346,10 +344,9 @@
         aggregate_kernel,
         out_shape=[struct((rows, 2048), BF)] * 3 + [struct((160, rows, LANES), BF), CHUNK]
         + [struct((64, 1, LANES), F32)],
-        in_specs=[SMEM, SMEM] + [ANY] * 4,
+        in_specs=[SMEM, SMEM, ANY, VMEM, ANY, ANY],
         out_specs=[VMEM] * 6,
         scratch_shapes=[
-            pltpu.VMEM(wire.shape, BF),
             pltpu.VMEM((3,) + CHUNK.shape, BF),
             pltpu.SemaphoreType.DMA((8 + PARTS * 4,)),
         ],
@@ -523,38 +520,42 @@
                 total[at] = total[at] + parts[t][:, k * LANES : (k + 1) * LANES]
 
 
-def spread_own_kernel(me, cols, mean, chunk, total):
+def spread_own_kernel(me, cols, mean, chunk, mask, total, *refs):
+    later, sems = refs[0:3], refs[3]
+    tiles = [fetch(me, s, mask, later[s - 1], sems, PARTS * (s - 1)) for s in (1, 2, 3)]
     total[...] = jnp.zeros(total.shape, F32)
     spread_tiles(me[0] * QUARTER, cols, mean, chunk, total)
-
-
-def spread_own(me, cols, mean, chunk):
-    return pl.pallas_call(
+    for copy in tiles:
+        copy.wait()
+
+
+def spread_own(me, cols, mean, chunk, mask):
+    got = pl.pallas_call(
         spread_own_kernel,
-        out_shape=struct((160, 32, LANES), F32),
-        in_specs=[SMEM, SMEM, VMEM, VMEM],
-        out_specs=VMEM,
+        out_shape=[struct((160, 32, LANES), F32)] + [CHUNK] * 3,
+        in_specs=[SMEM, SMEM, VMEM, VMEM, ANY],
+        out_specs=[VMEM] * 4,
+        scratch_shapes=[pltpu.SemaphoreType.DMA((3 * PARTS,))],
         compiler_params=params(),
-        cost_estimate=cost(1e9, 4 << 20),
+        cost_estimate=cost(1e9, 8 << 20),
         name="spread_own",
-    )(me, cols, mean, chunk)
-
-
-def spread_kernel(me, cols, begun, mask, *refs):
-    backs, (local, wire_out), refs = refs[0:4], refs[4:6], refs[6:]
-    total, chunks, back_s, pack_s, wire, sems = refs
+    )(me, cols, mean, chunk, mask)
+    return got[0], got[1:4]
+
+
+def spread_kernel(me, cols, begun, *refs):
+    chunks, backs, (local, wire_out), refs = refs[0:3], refs[3:7], refs[7:9], refs[9:]
+    total, back_s, pack_s, wire, sems = refs
     pieces = []
     for s in range(4):
         pieces.append(pltpu.make_async_copy(backs[s], back_s.at[s], sems.at[s]))
         pieces[-1].start()
-    tiles = [fetch(me, s, mask, chunks.at[s - 1], sems, 4 + PARTS * s) for s in (1, 2, 3)]
     total[...] = begun[...]
     for s in (1, 2, 3):
         begin = lax.rem(me[0] + s, 4) * QUARTER
         pieces[s].wait()
-        tiles[s - 1].wait()
-        spread_tiles(begin, cols, back_s.at[s], chunks.at[s - 1], total)
-    own = Copies(total.at[pl.ds(0, 64)], local.at[pl.ds(0, 64)], sems, 4 + PARTS, 2)
+        spread_tiles(begin, cols, back_s.at[s], chunks[s - 1], total)
+    own = Copies(total.at[pl.ds(0, 64)], local.at[pl.ds(0, 64)], sems, 8, 2)
     pieces[0].wait()
     grads = sum(back_s[s, 32:40, :].astype(F32) for s in range(4))
     grad = jnp.concatenate([grads[:, n * 256 : (n + 1) * 256] for n in range(8)], axis=0)
@@ -569,37 +570,35 @@
         wire[2 * q, 32:48, :] = even.astype(BF)
         wire[2 * q + 1, 32:48, :] = odd.astype(BF)
 
-    leaving = Copies(wire, wire_out, sems, 0, 4)
+    leaving = Copies(wire, wire_out, sems, 4, 4)
     own.wait()
     leaving.wait()
 
 
-def spread(me, cols, begun, mask, backs):
+def spread(me, cols, begun, chunks, backs):
     _, rows, _ = begun.shape
     return pl.pallas_call(
         spread_kernel,
         out_shape=[struct((LOCAL_TILES, rows, LANES), F32), struct((64, 56, LANES), BF)],
-        in_specs=[SMEM, SMEM, VMEM] + [ANY] * 5,
+        in_specs=[SMEM, SMEM] + [VMEM] * 4 + [ANY] * 4,
         out_specs=[ANY] * 2,
         scratch_shapes=[
             pltpu.VMEM(begun.shape, F32),
-            pltpu.VMEM((3,) + CHUNK.shape, BF),
             pltpu.VMEM((4,) + backs[0].shape, BF),
             pltpu.VMEM((64, 8, LANES), F32),
             pltpu.VMEM((64, 56, LANES), BF),
-            pltpu.SemaphoreType.DMA((4 + PARTS * 4,)),
+            pltpu.SemaphoreType.DMA((10,)),
         ],
         compiler_params=params(),
         cost_estimate=cost(3e9, 12 << 20),
         name="spread",
-    )(me, cols, begun, mask, *backs)
+    )(me, cols, begun, *chunks, *backs)
 
 
 def scatter_kernel(me_ref, idx, wire, local, *refs):
-    sums, out, wire_s, sum_s, ret, acc, idx_s, own_s, out_s, sems = refs[0:4], *refs[4:]
+    sums, out, sum_s, ret, acc, idx_s, own_s, out_s, sems = refs[0:4], *refs[4:]
     me = me_ref[0]
     index = Copies(idx, idx_s, sems, 0, 1)
-    first = Copies(wire, wire_s, sems, 1, 2)
     later = [Copies(local.at[pl.ds(0, 64)], own_s, sems, 5, 2)]
     for s in range(4):
         later.append(Copies(sums[s], sum_s.at[lax.rem(me + s, 4)], sems, 9 + s, 1))
@@ -607,11 +606,10 @@
     fold = nodes // FOLD_OUT
     acc[...] = jnp.zeros(acc.shape, F32)
     index.wait()
-    first.wait()
 
     @pl.loop(0, 32, unroll=8)
     def _(q):
-        even, odd = wire_s[2 * q], wire_s[2 * q + 1]
+        even, odd = wire[2 * q], wire[2 * q + 1]
         ret[2 * q] = even[0:32].astype(F32)
         ret[2 * q + 1] = odd[0:32].astype(F32)
         ret[64 + q] = join_rest(even[32:48].astype(F32), odd[32:48].astype(F32))
@@ -651,10 +649,9 @@
     return pl.pallas_call(
         scatter_kernel,
         out_shape=struct((rows, 8192), F32),
-        in_specs=[SMEM] + [ANY] * 7,
+        in_specs=[SMEM, ANY, VMEM] + [ANY] * 5,
         out_specs=ANY,
         scratch_shapes=[
-            pltpu.VMEM(wire.shape, BF),
             pltpu.VMEM((4, rows, 2048), BF),
             pltpu.VMEM((96, rows, LANES), F32),
             pltpu.VMEM((rows * 8192 // FOLD_OUT, FOLD_OUT), F32),
@@ -774,8 +771,8 @@
     aggs = exchange([aggregate_own(me, cols, joined, chunk, degree), *others], 1)
     backs, hiddens, sums = dense(me, pieces, aggs, degree)
     backs = exchange(backs, -1)
-    begun = spread_own(me, cols, backs[0], chunk)
-    local, back = spread(me, cols, begun, mask, backs)
+    begun, chunks = spread_own(me, cols, backs[0], chunk, mask)
+    local, back = spread(me, cols, begun, chunks, backs)
     returned = lax.all_to_all(back, "dom", split_axis=0, concat_axis=0, tiled=True)
     local, hiddens, sums = lax.optimization_barrier((local, hiddens, sums))
 

time: 143 us -> 141 us (0.986)
  waiting for transfers between devices: 38.1 us -> 35.7 us
    pallas_call x1, Pallas kernels: 1.65 us -> 4.49 us  [spread_own(): pl.pallas_call(spread_own_kernel, out_shape=[struct((160, 32, LANES), F32...]
    ppermute x15, waiting for transfers between devices: 21.2 us -> 18.4 us  [exchange(): lax.ppermute(pieces[s], 'feat', [(q, (q + sign * s) % 4) for q in range(4)])]
    pallas_call x1, Pallas kernels: 6.92 us -> 5.22 us  [spread(): pl.pallas_call(spread_kernel, out_shape=[struct((LOCAL_TILES, rows, LANES...]
  transfers between devices with their start and end apart: 18 -> 18, of which waited for: 11 -> 9; matrix products, arithmetic and copies ran while one was open for 0% -> 0% of each run, Pallas kernels for 22% -> 23%
where the time goes in v4:
time: 141 us
  Pallas kernels  56.7 us (40%)
  starting transfers between devices  44.8 us (32%)
  waiting for transfers between devices  35.7 us (25%)
  local copies, waits for them, and re-layouts  2.33 us (2%)
    ppermute x15, starting transfers between devices, exchange(): lax.ppermute(pieces[s], 'feat', [(q, (q + sign * s) % 4) for q in range(4)])  18.5 us
    ppermute x15, waiting for transfers between devices, exchange(): lax.ppermute(pieces[s], 'feat', [(q, (q + sign * s) % 4) for q in range(4)])  18.4 us
    all_to_all x1, starting transfers between devices, per_device(): halo = lax.all_to_all(wire, 'dom', split_axis=0, concat_axis=0, tiled=True)  13.2 us
    pallas_call x1, Pallas kernels, gather(): pl.pallas_call(gather_kernel, out_shape=[struct((nodes // LANES, features...  11 us
    pallas_call x1, Pallas kernels, scatter(): pl.pallas_call(scatter_kernel, out_shape=struct((rows, 8192), F32), in_sp...  9.47 us
    pallas_call x1, Pallas kernels, masks(): pl.pallas_call(mask_kernel, out_shape=[struct((length,) + edges.shape[1:]...  9.45 us
    all_to_all x1, waiting for transfers between devices, per_device(): halo = lax.all_to_all(wire, 'dom', split_axis=0, concat_axis=0, tiled=True)  8.3 us
    all_to_all x1, waiting for transfers between devices, per_device(): lax.all_to_all(back, 'dom', split_axis=0, concat_axis=0, tiled=True)  7.45 us
  transfers between devices with their start and end apart: 18, of which 9 were waited for; matrix products, arithmetic and copies ran while one was open for 0% of the time, Pallas kernels for 23%

profile of v4, /device:TPU:1, one launch (start us, length us, event | category | flops | bytes accessed | tf_op | source)
XLA Modules:
  0.0 140.6 jit_solution(15062491056641061146)
XLA Ops:
  0.6 0.0 copy-start.7
  0.6 11.0 %gather_rows.1 = (bf16[64,32,128]{2,1,0:T(8,128)(2,1)}, bf16[64,48,128]{2,1,0:T(8,128)(2,1)}, s32[96,128]{1,0:T(8,128)}, bf16[128,2048]{1,0:T(8,128)(2,1)}, bf16...) custom-call(bf16[32,8192]{1,0:T(8,128)(2,1)} %quantized.1, f32[1,8192]{1,0:T(1,128)} %bitcast.9, ...), custom_call_target="tpu_custom_call" | custom-call | flops 6400000000 | bytes 4194304 | tf_op jit(solution)/shard_map/gather_rows/pallas_call | solution.py:200
  11.6 13.2 %all-to-all-start = ((bf16[64,48,128]{2,1,0:T(8,128)(2,1)}), bf16[64,48,128]{2,1,0:T(8,128)(2,1)S(1)}, u32[]{:S(2)}, u32[]{:S(2)}) async-start(bf16[64,48,128]{2,1,0:T(8,128)(2,1)} %get-tuple-element.55), calls=%async_computation | async-start | bytes 1572864 | tf_op jit(solution)/shard_map/all_to_all | solution.py:766
  24.8 1.3 collective-permute-start
  26.1 2.4 %collective-permute-start.1 = (bf16[128,2048]{1,0:T(8,128)(2,1)}, bf16[128,2048]{1,0:T(8,128)(2,1)S(1)}, u32[]{:S(2)}, u32[]{:S(2)}) collective-permute-start(bf16[128,2048]{1,0:T(8,128)(2,1)} %get-tuple-element.52), channel_id=1, source_target_pairs={{0,2},{1,3},{2,0},{3,1},{4,6},{5,7},{6,4},{7,5},{8,10},{9,11},{10,... | collective-permute-start | bytes 1572872 | tf_op jit(solution)/shard_map/ppermute | solution.py:736
  28.5 1.2 collective-permute-start.2
  29.7 0.1 copy.15
  29.8 9.4 %mask_degree.1 = (bf16[256,4,128,128]{3,2,1,0:T(8,128)(2,1)}, f32[53248,1,128]{2,1,0:T(1,128)}) custom-call(s32[64,4,128,128]{3,2,1,0:T(8,128)} %edges.1), custom_call_target="tpu_custom_call" | custom-call | flops 1000000000 | bytes 25165824 | tf_op jit(solution)/shard_map/mask_degree/pallas_call | solution.py:263
  39.2 8.3 %all-to-all-done.wire = bf16[64,48,128]{2,1,0:T(8,128)(2,1)S(1)} async-done(((bf16[64,48,128]{2,1,0:T(8,128)(2,1)}), bf16[64,48,128]{2,1,0:T(8,128)(2,1)S(1)}, u32[]{:S(2)}, u32[]{:S(2)}) %all-to-all-start) | async-done | bytes 786464 | tf_op jit(solution)/shard_map/all_to_all | solution.py:766
  47.5 5.8 %aggregate.1 = (bf16[32,2048]{1,0:T(8,128)(2,1)S(1)}, bf16[32,2048]{1,0:T(8,128)(2,1)S(1)}, bf16[32,2048]{1,0:T(8,128)(2,1)S(1)}, bf16[160,32,128]{2,1,0:T(8,128...) custom-call(s32[1]{0:T(128)} %bitcast.me.me_ref, s32[64,4]{1,0:T(8,128)S(1)} %bitcast.5, ...), custom_call_target="tpu_custom_call" | custom-call | flops 3000000000 | bytes 12582912 | tf_op jit(solution)/shard_map/aggregate/pallas_call | solution.py:343
  53.4 0.0 copy-start.5
  53.4 1.5 %collective-permute-start.3 = (bf16[32,2048]{1,0:T(8,128)(2,1)S(1)}, bf16[32,2048]{1,0:T(8,128)(2,1)S(1)}, u32[]{:S(2)}, u32[]{:S(2)}) collective-permute-start(bf16[32,2048]{1,0:T(8,128)(2,1)S(1)} %get-tuple-element.61), channel_id=1, source_target_pairs={{0,1},{1,2},{2,3},{3,0},{4,5},{5,6},{6,7},{7,4},{8,9},{9,10},{10,1... | collective-permute-start | bytes 393224 | tf_op jit(solution)/shard_map/ppermute | solution.py:736
  54.9 2.4 %collective-permute-start.4 = (bf16[32,2048]{1,0:T(8,128)(2,1)S(1)}, bf16[32,2048]{1,0:T(8,128)(2,1)S(1)}, u32[]{:S(2)}, u32[]{:S(2)}) collective-permute-start(bf16[32,2048]{1,0:T(8,128)(2,1)S(1)} %get-tuple-element.62), channel_id=1, source_target_pairs={{0,2},{1,3},{2,0},{3,1},{4,6},{5,7},{6,4},{7,5},{8,10},{9,11},{10,... | collective-permute-start | bytes 393224 | tf_op jit(solution)/shard_map/ppermute | solution.py:736
  57.3 0.0 collective-permute-done.refs_1_
  57.3 1.2 collective-permute-start.5
  58.5 1.9 %aggregate_own.1.refs_4_ = bf16[32,2048]{1,0:T(8,128)(2,1)S(1)} custom-call(s32[1]{0:T(128)} %bitcast.me.me_ref, s32[64,4]{1,0:T(8,128)S(1)} %bitcast.6, bf16[160,32,128]{2,1,0:T(8,128)(2,1)S(1)} %get-tuple-element.58.joined, bf16[16,4,128,128]{3,2,1,0:T(8,128)(2,1)S(1)} %get-tuple-element.59.chunk, f32[64,1,128]{2,1,0:T(1,128)S(1)} %get-tuple-element.60.degree.refs_8_), custom_call_target="tpu_custom_call" | custom-call | flops 1000000000 | bytes 4194304 | tf_op jit(solution)/shard_map/aggregate_own/pallas_call | solution.py:365
  60.4 0.6 copy-done.6
  61.0 0.0 collective-permute-done.1.refs_2_
  61.0 0.0 collective-permute-done.2.refs_3_
  61.0 0.0 collective-permute-done.3.refs_5_
  61.0 1.3 collective-permute-done.4.refs_6_
  62.4 0.5 collective-permute-done.5.refs_7_
  62.8 0.0 copy-done.9
  62.9 0.2 copy-done.18
  63.0 0.4 copy-done.19
  63.5 6.8 %dense.1 = (bf16[40,2176]{1,0:T(8,128)(2,1)}, bf16[40,2176]{1,0:T(8,128)(2,1)}, bf16[40,2176]{1,0:T(8,128)(2,1)}, bf16[40,2176]{1,0:T(8,128)(2,1)}, bf16[64,2048...) custom-call(s32[1]{0:T(128)} %bitcast.me.me_ref, ...), custom_call_target="tpu_custom_call" | custom-call | flops 1000000000 | bytes 5242880 | tf_op jit(solution)/shard_map/dense/pallas_call | solution.py:470
  70.3 2.6 %collective-permute-start.6 = (bf16[40,2176]{1,0:T(8,128)(2,1)}, bf16[40,2176]{1,0:T(8,128)(2,1)S(1)}, u32[]{:S(2)}, u32[]{:S(2)}) collective-permute-start(bf16[40,2176]{1,0:T(8,128)(2,1)} %get-tuple-element.69), channel_id=1, source_target_pairs={{0,3},{1,0},{2,1},{3,2},{4,7},{5,4},{6,5},{7,6},{8,11},{9,8},{10,9... | collective-permute-start | bytes 522248 | tf_op jit(solution)/shard_map/ppermute | solution.py:736
  73.0 0.3 collective-permute-start.7
  73.2 0.4 collective-permute-start.8
  73.6 0.9 copy-done.2
  74.5 4.5 %spread_own.1 = (f32[160,32,128]{2,1,0:T(8,128)S(1)}, bf16[16,4,128,128]{3,2,1,0:T(8,128)(2,1)S(1)}, bf16[16,4,128,128]{3,2,1,0:T(8,128)(2,1)S(1)}, bf16[16,4,128,128]{3,2,1,0:T(8,128)(2,1)S(1)}) custom-call(s32[1]{0:T(128)} %bitcast.me.me_ref, s32[64,4]{1,0:T(8,128)S(1)} %bitcast.7, bf16[40,2176]{1,0:T(8,128)(2,1)S(1)} %copy-done.2, ...), custom_call_target="tpu_custom_call" | custom-call | flops 1000000000 | bytes 8388608 | tf_op jit(solution)/shard_map/spread_own/pallas_call | solution.py:533
  79.0 0.0 collective-permute-done.6.refs_4_
  79.1 0.0 collective-permute-done.7.refs_5_
  79.1 5.1 %collective-permute-done.8.refs_6_ = bf16[40,2176]{1,0:T(8,128)(2,1)S(1)} collective-permute-done((bf16[40,2176]{1,0:T(8,128)(2,1)}, bf16[40,2176]{1,0:T(8,128)(2,1)S(1)}, u32[]{:S(2)}, u32[]{:S(2)}) %collective-permute-start.8) | collective-permute-done | bytes 174112 | tf_op jit(solution)/shard_map/ppermute | solution.py:736
  84.1 0.0 copy-start.15
  84.1 0.0 copy-start.14
  84.2 0.0 copy-start.1
  84.2 5.2 %spread.1 = (f32[1664,32,128]{2,1,0:T(8,128)}, bf16[64,56,128]{2,1,0:T(8,128)(2,1)}) custom-call(s32[1]{0:T(128)} %bitcast.me.me_ref, s32[64,4]{1,0:T(8,128)S(1)} %bitcast.8, f32[160,32,128]{2,1,0:T(8,128)S(1)} %get-tuple-element.65.begun, bf16[16,4,128,128]{3,2,1,0:T(8,128)(2,1)S(1)} %get-tuple-element.66.refs_0_, ...), custom_call_target="tpu_custom_call" | custom-call | flops 3000000000 | bytes 12582912 | tf_op jit(solution)/shard_map/spread/pallas_call | solution.py:580
  89.4 0.0 copy-start.3
  89.4 0.0 copy-start.4
  89.4 6.6 %all-to-all-start.1 = ((bf16[64,56,128]{2,1,0:T(8,128)(2,1)}), bf16[64,56,128]{2,1,0:T(8,128)(2,1)S(1)}, u32[]{:S(2)}, u32[]{:S(2)}) async-start(bf16[64,56,128]{2,1,0:T(8,128)(2,1)} %get-tuple-element.86), calls=%async_computation.1 | async-start | bytes 1835008 | tf_op jit(solution)/shard_map/all_to_all | solution.py:776
  96.1 0.0 copy-done.13
  96.1 0.4 collective-permute-start.9
  96.4 0.8 collective-permute-start.10
  97.3 0.6 collective-permute-start.11
  97.9 2.5 %collective-permute-start.12 = (bf16[32,2048]{1,0:T(8,128)(2,1)S(1)}, bf16[32,2048]{1,0:T(8,128)(2,1)S(1)}, u32[]{:S(2)}, u32[]{:S(2)}) collective-permute-start(bf16[32,2048]{1,0:T(8,128)(2,1)S(1)} %copy-done.16), channel_id=1, source_target_pairs={{0,3},{1,0},{2,1},{3,2},{4,7},{5,4},{6,5},{7,6},{8,11},{9,8},{10,9... | collective-permute-start | bytes 393224 | tf_op jit(solution)/shard_map/ppermute | solution.py:736
  100.3 1.0 collective-permute-start.13
  101.3 2.3 %collective-permute-done.9.b = bf16[64,2048]{1,0:T(8,128)(2,1)S(1)} collective-permute-done((bf16[64,2048]{1,0:T(8,128)(2,1)S(1)}, bf16[64,2048]{1,0:T(8,128)(2,1)S(1)}, u32[]{:S(2)}, u32[]{:S(2)}) %collective-permute-start.9) | collective-permute-done | bytes 262176 | tf_op jit(solution)/shard_map/ppermute | solution.py:736
  103.6 0.0 copy-done.14
  103.6 0.0 collective-permute-start.14
  103.6 1.5 %collective-permute-done.10.c = bf16[64,2048]{1,0:T(8,128)(2,1)S(1)} collective-permute-done((bf16[64,2048]{1,0:T(8,128)(2,1)S(1)}, bf16[64,2048]{1,0:T(8,128)(2,1)S(1)}, u32[]{:S(2)}, u32[]{:S(2)}) %collective-permute-start.10) | collective-permute-done | bytes 262176 | tf_op jit(solution)/shard_map/ppermute | solution.py:736
  105.1 7.8 %collective-permute-done.11.d = bf16[64,2048]{1,0:T(8,128)(2,1)S(1)} collective-permute-done((bf16[64,2048]{1,0:T(8,128)(2,1)S(1)}, bf16[64,2048]{1,0:T(8,128)(2,1)S(1)}, u32[]{:S(2)}, u32[]{:S(2)}) %collective-permute-start.11) | collective-permute-done | bytes 262176 | tf_op jit(solution)/shard_map/ppermute | solution.py:736
  112.9 1.0 place.1
  113.9 7.5 %all-to-all-done.1.wire.returned = bf16[64,56,128]{2,1,0:T(8,128)(2,1)S(1)} async-done(((bf16[64,56,128]{2,1,0:T(8,128)(2,1)}), bf16[64,56,128]{2,1,0:T(8,128)(2,1)S(1)}, u32[]{:S(2)}, u32[]{:S(2)}) %all-to-all-start.1) | async-done | bytes 917536 | tf_op jit(solution)/shard_map/all_to_all | solution.py:776
  121.4 0.7 final_part.1
  122.1 6.5 %all-to-all-start.2 = ((f32[64,4,128]{2,1,0:T(4,128)}), f32[64,4,128]{2,1,0:T(4,128)S(1)}, u32[]{:S(2)}, u32[]{:S(2)}) async-start(f32[64,4,128]{2,1,0:T(4,128)} %final_part.1), calls=%async_computation.2 | async-start | bytes 262144 | tf_op jit(solution)/shard_map/all_to_all | solution.py:781
  128.6 0.0 collective-permute-done.12.refs_1_
  128.6 0.0 collective-permute-done.13.refs_2_
  128.6 0.0 collective-permute-done.14.refs_3_
  128.6 0.0 copy-done.3
  128.6 0.0 copy-done.4
  128.6 9.5 %scatter_rows.1 = f32[32,8192]{1,0:T(8,128)} custom-call(s32[1]{0:T(128)} %bitcast.me.me_ref, s32[96,128]{1,0:T(8,128)S(1)} %copy-done.4, bf16[64,56,128]{2,1,0:T(8,128)(2,1)S(1)} %all-to-all-done.1.wire.returned, f32[1664,32,128]{2,1,0:T(8,128)} %get-tuple-element.87.local, bf16[32,2048]{1,0:T(8,128)(2,1)S(1)} %copy-done.3, ...), custom_call_target="tpu_custom_call" | custom-call | flops 6400000000 | bytes 5242880 | tf_op jit(solution)/shard_map/scatter_rows/pallas_call | solution.py:649
  138.1 1.6 %all-to-all-done.2.everyone = f32[64,4,128]{2,1,0:T(4,128)S(1)} async-done(((f32[64,4,128]{2,1,0:T(4,128)}), f32[64,4,128]{2,1,0:T(4,128)S(1)}, u32[]{:S(2)}, u32[]{:S(2)}) %all-to-all-start.2) | async-done | bytes 131104 | tf_op jit(solution)/shard_map/all_to_all | solution.py:781
  139.6 0.8 unpack.1
  (24 shorter events, 0.0 us)
Async XLA Ops:
  0.6 29.0 %copy-start.7 = (s32[1,64,4]{1,2,0:T(4,128)S(1)}, s32[1,64,4]{1,2,0:T(4,128)}, u32[]{:S(2)}) copy-start(s32[1,64,4]{1,2,0:T(4,128)} %param.14) | copy-start | bytes 3076
  11.6 35.9 %all-to-all-start = ((bf16[64,48,128]{2,1,0:T(8,128)(2,1)}), bf16[64,48,128]{2,1,0:T(8,128)(2,1)S(1)}, u32[]{:S(2)}, u32[]{:S(2)}) async-start(bf16[64,48,128]{2,1,0:T(8,128)(2,1)} %get-tuple-element.55), calls=%async_computation | async-start | bytes 1572864 | tf_op jit(solution)/shard_map/all_to_all | solution.py:766
  24.8 32.5 %collective-permute-start = (bf16[128,2048]{1,0:T(8,128)(2,1)}, bf16[128,2048]{1,0:T(8,128)(2,1)S(1)}, u32[]{:S(2)}, u32[]{:S(2)}) collective-permute-start(bf16[128,2048]{1,0:T(8,128)(2,1)} %get-tuple-element.51), channel_id=1, source_target_pairs={{0,1},{1,2},{2,3},{3,0},{4,5},{5,6},{6,7},{7,4},{8,9},{9,10},{10,1... | collective-permute-start | bytes 1572872 | tf_op jit(solution)/shard_map/ppermute | solution.py:736
  26.1 34.9 %collective-permute-start.1 = (bf16[128,2048]{1,0:T(8,128)(2,1)}, bf16[128,2048]{1,0:T(8,128)(2,1)S(1)}, u32[]{:S(2)}, u32[]{:S(2)}) collective-permute-start(bf16[128,2048]{1,0:T(8,128)(2,1)} %get-tuple-element.52), channel_id=1, source_target_pairs={{0,2},{1,3},{2,0},{3,1},{4,6},{5,7},{6,4},{7,5},{8,10},{9,11},{10,... | collective-permute-start | bytes 1572872 | tf_op jit(solution)/shard_map/ppermute | solution.py:736
  28.5 32.5 %collective-permute-start.2 = (bf16[128,2048]{1,0:T(8,128)(2,1)}, bf16[128,2048]{1,0:T(8,128)(2,1)S(1)}, u32[]{:S(2)}, u32[]{:S(2)}) collective-permute-start(bf16[128,2048]{1,0:T(8,128)(2,1)} %get-tuple-element.53), channel_id=1, source_target_pairs={{0,3},{1,0},{2,1},{3,2},{4,7},{5,4},{6,5},{7,6},{8,11},{9,8},{10,9... | collective-permute-start | bytes 1572872 | tf_op jit(solution)/shard_map/ppermute | solution.py:736
  29.8 17.8 %copy-start = (bf16[64,32,128]{2,1,0:T(8,128)(2,1)S(1)}, bf16[64,32,128]{2,1,0:T(8,128)(2,1)}, u32[]{:S(2)}) copy-start(bf16[64,32,128]{2,1,0:T(8,128)(2,1)} %get-tuple-element.54.feat_tiles) | copy-start | bytes 1572868
  53.4 9.5 %copy-start.5 = (f32[64,1,128]{2,1,0:T(1,128)}, f32[64,1,128]{2,1,0:T(1,128)S(1)}, u32[]{:S(2)}) copy-start(f32[64,1,128]{2,1,0:T(1,128)S(1)} %get-tuple-element.60.degree.refs_8_) | copy-start | bytes 98308
  53.4 7.6 %collective-permute-start.3 = (bf16[32,2048]{1,0:T(8,128)(2,1)S(1)}, bf16[32,2048]{1,0:T(8,128)(2,1)S(1)}, u32[]{:S(2)}, u32[]{:S(2)}) collective-permute-start(bf16[32,2048]{1,0:T(8,128)(2,1)S(1)} %get-tuple-element.61), channel_id=1, source_target_pairs={{0,1},{1,2},{2,3},{3,0},{4,5},{5,6},{6,7},{7,4},{8,9},{9,10},{10,1... | collective-permute-start | bytes 393224 | tf_op jit(solution)/shard_map/ppermute | solution.py:736
  54.9 7.5 %collective-permute-start.4 = (bf16[32,2048]{1,0:T(8,128)(2,1)S(1)}, bf16[32,2048]{1,0:T(8,128)(2,1)S(1)}, u32[]{:S(2)}, u32[]{:S(2)}) collective-permute-start(bf16[32,2048]{1,0:T(8,128)(2,1)S(1)} %get-tuple-element.62), channel_id=1, source_target_pairs={{0,2},{1,3},{2,0},{3,1},{4,6},{5,7},{6,4},{7,5},{8,10},{9,11},{10,... | collective-permute-start | bytes 393224 | tf_op jit(solution)/shard_map/ppermute | solution.py:736
  57.3 5.5 %copy-start.8 = (bf16[128,2048]{1,0:T(8,128)(2,1)}, bf16[128,2048]{1,0:T(8,128)(2,1)S(1)}, u32[]{:S(2)}) copy-start(bf16[128,2048]{1,0:T(8,128)(2,1)S(1)} %collective-permute-done.refs_1_) | copy-start | bytes 1572868
  57.3 5.5 %collective-permute-start.5 = (bf16[32,2048]{1,0:T(8,128)(2,1)S(1)}, bf16[32,2048]{1,0:T(8,128)(2,1)S(1)}, u32[]{:S(2)}, u32[]{:S(2)}) collective-permute-start(bf16[32,2048]{1,0:T(8,128)(2,1)S(1)} %get-tuple-element.63), channel_id=1, source_target_pairs={{0,3},{1,0},{2,1},{3,2},{4,7},{5,4},{6,5},{7,6},{8,11},{9,8},{10,9... | collective-permute-start | bytes 393224 | tf_op jit(solution)/shard_map/ppermute | solution.py:736
  60.4 0.6 copy-start.6
  61.0 1.8 %copy-start.9 = (bf16[128,2048]{1,0:T(8,128)(2,1)}, bf16[128,2048]{1,0:T(8,128)(2,1)S(1)}, u32[]{:S(2)}) copy-start(bf16[128,2048]{1,0:T(8,128)(2,1)S(1)} %collective-permute-done.1.refs_2_) | copy-start | bytes 1572868
  61.0 1.8 %copy-start.10 = (bf16[128,2048]{1,0:T(8,128)(2,1)}, bf16[128,2048]{1,0:T(8,128)(2,1)S(1)}, u32[]{:S(2)}) copy-start(bf16[128,2048]{1,0:T(8,128)(2,1)S(1)} %collective-permute-done.2.refs_3_) | copy-start | bytes 1572868
  61.0 1.8 %copy-start.17 = (bf16[32,2048]{1,0:T(8,128)(2,1)}, bf16[32,2048]{1,0:T(8,128)(2,1)S(1)}, u32[]{:S(2)}) copy-start(bf16[32,2048]{1,0:T(8,128)(2,1)S(1)} %collective-permute-done.3.refs_5_) | copy-start | bytes 393220
  62.4 0.7 copy-start.18
  62.8 0.6 copy-start.19
  70.3 8.7 %collective-permute-start.6 = (bf16[40,2176]{1,0:T(8,128)(2,1)}, bf16[40,2176]{1,0:T(8,128)(2,1)S(1)}, u32[]{:S(2)}, u32[]{:S(2)}) collective-permute-start(bf16[40,2176]{1,0:T(8,128)(2,1)} %get-tuple-element.69), channel_id=1, source_target_pairs={{0,3},{1,0},{2,1},{3,2},{4,7},{5,4},{6,5},{7,6},{8,11},{9,8},{10,9... | collective-permute-start | bytes 522248 | tf_op jit(solution)/shard_map/ppermute | solution.py:736
  73.0 6.1 %collective-permute-start.7 = (bf16[40,2176]{1,0:T(8,128)(2,1)}, bf16[40,2176]{1,0:T(8,128)(2,1)S(1)}, u32[]{:S(2)}, u32[]{:S(2)}) collective-permute-start(bf16[40,2176]{1,0:T(8,128)(2,1)} %get-tuple-element.70), channel_id=1, source_target_pairs={{0,2},{1,3},{2,0},{3,1},{4,6},{5,7},{6,4},{7,5},{8,10},{9,11},{10,... | collective-permute-start | bytes 522248 | tf_op jit(solution)/shard_map/ppermute | solution.py:736
  73.2 10.9 %collective-permute-start.8 = (bf16[40,2176]{1,0:T(8,128)(2,1)}, bf16[40,2176]{1,0:T(8,128)(2,1)S(1)}, u32[]{:S(2)}, u32[]{:S(2)}) collective-permute-start(bf16[40,2176]{1,0:T(8,128)(2,1)} %get-tuple-element.71), channel_id=1, source_target_pairs={{0,1},{1,2},{2,3},{3,0},{4,5},{5,6},{6,7},{7,4},{8,9},{9,10},{10,1... | collective-permute-start | bytes 522248 | tf_op jit(solution)/shard_map/ppermute | solution.py:736
  73.6 0.9 copy-start.2
  84.1 11.9 %copy-start.13 = (bf16[64,2048]{1,0:T(8,128)(2,1)S(1)}, bf16[64,2048]{1,0:T(8,128)(2,1)}, u32[]{:S(2)}) copy-start(bf16[64,2048]{1,0:T(8,128)(2,1)} %get-tuple-element.82) | copy-start | bytes 786436
  84.1 12.3 %copy-start.12 = (bf16[64,2048]{1,0:T(8,128)(2,1)S(1)}, bf16[64,2048]{1,0:T(8,128)(2,1)}, u32[]{:S(2)}) copy-start(bf16[64,2048]{1,0:T(8,128)(2,1)} %get-tuple-element.83) | copy-start | bytes 786436
  84.1 13.2 %copy-start.11 = (bf16[64,2048]{1,0:T(8,128)(2,1)S(1)}, bf16[64,2048]{1,0:T(8,128)(2,1)}, u32[]{:S(2)}) copy-start(bf16[64,2048]{1,0:T(8,128)(2,1)} %get-tuple-element.84) | copy-start | bytes 786436
  84.1 13.7 %copy-start.16 = (bf16[32,2048]{1,0:T(8,128)(2,1)S(1)}, bf16[32,2048]{1,0:T(8,128)(2,1)}, u32[]{:S(2)}) copy-start(bf16[32,2048]{1,0:T(8,128)(2,1)} %get-tuple-element.89) | copy-start | bytes 393220
  84.1 16.2 %copy-start.15 = (bf16[32,2048]{1,0:T(8,128)(2,1)S(1)}, bf16[32,2048]{1,0:T(8,128)(2,1)}, u32[]{:S(2)}) copy-start(bf16[32,2048]{1,0:T(8,128)(2,1)} %get-tuple-element.90) | copy-start | bytes 393220
  84.1 19.4 %copy-start.14 = (bf16[32,2048]{1,0:T(8,128)(2,1)S(1)}, bf16[32,2048]{1,0:T(8,128)(2,1)}, u32[]{:S(2)}) copy-start(bf16[32,2048]{1,0:T(8,128)(2,1)} %get-tuple-element.91) | copy-start | bytes 393220
  84.2 28.7 %copy-start.1 = (bf16[64,2048]{1,0:T(8,128)(2,1)S(1)}, bf16[64,2048]{1,0:T(8,128)(2,1)}, u32[]{:S(2)}) copy-start(bf16[64,2048]{1,0:T(8,128)(2,1)} %get-tuple-element.81.a) | copy-start | bytes 786436
  89.4 39.2 %copy-start.3 = (bf16[32,2048]{1,0:T(8,128)(2,1)S(1)}, bf16[32,2048]{1,0:T(8,128)(2,1)}, u32[]{:S(2)}) copy-start(bf16[32,2048]{1,0:T(8,128)(2,1)} %get-tuple-element.88.refs_0_) | copy-start | bytes 393220
  89.4 39.2 %copy-start.4 = (s32[96,128]{1,0:T(8,128)S(1)}, s32[96,128]{1,0:T(8,128)}, u32[]{:S(2)}) copy-start(s32[96,128]{1,0:T(8,128)} %get-tuple-element.85.idx) | copy-start | bytes 147460
  89.4 31.9 %all-to-all-start.1 = ((bf16[64,56,128]{2,1,0:T(8,128)(2,1)}), bf16[64,56,128]{2,1,0:T(8,128)(2,1)S(1)}, u32[]{:S(2)}, u32[]{:S(2)}) async-start(bf16[64,56,128]{2,1,0:T(8,128)(2,1)} %get-tuple-element.86), calls=%async_computation.1 | async-start | bytes 1835008 | tf_op jit(solution)/shard_map/all_to_all | solution.py:776
  96.1 7.5 %collective-permute-start.9 = (bf16[64,2048]{1,0:T(8,128)(2,1)S(1)}, bf16[64,2048]{1,0:T(8,128)(2,1)S(1)}, u32[]{:S(2)}, u32[]{:S(2)}) collective-permute-start(bf16[64,2048]{1,0:T(8,128)(2,1)S(1)} %copy-done.13), channel_id=1, source_target_pairs={{0,3},{1,0},{2,1},{3,2},{4,7},{5,4},{6,5},{7,6},{8,11},{9,8},{10,9... | collective-permute-start | bytes 786440 | tf_op jit(solution)/shard_map/ppermute | solution.py:736
  96.4 8.7 %collective-permute-start.10 = (bf16[64,2048]{1,0:T(8,128)(2,1)S(1)}, bf16[64,2048]{1,0:T(8,128)(2,1)S(1)}, u32[]{:S(2)}, u32[]{:S(2)}) collective-permute-start(bf16[64,2048]{1,0:T(8,128)(2,1)S(1)} %copy-done.12), channel_id=1, source_target_pairs={{0,2},{1,3},{2,0},{3,1},{4,6},{5,7},{6,4},{7,5},{8,10},{9,11},{10,... | collective-permute-start | bytes 786440 | tf_op jit(solution)/shard_map/ppermute | solution.py:736
  97.3 15.6 %collective-permute-start.11 = (bf16[64,2048]{1,0:T(8,128)(2,1)S(1)}, bf16[64,2048]{1,0:T(8,128)(2,1)S(1)}, u32[]{:S(2)}, u32[]{:S(2)}) collective-permute-start(bf16[64,2048]{1,0:T(8,128)(2,1)S(1)} %copy-done.11), channel_id=1, source_target_pairs={{0,1},{1,2},{2,3},{3,0},{4,5},{5,6},{6,7},{7,4},{8,9},{9,10},{10,1... | collective-permute-start | bytes 786440 | tf_op jit(solution)/shard_map/ppermute | solution.py:736
  97.9 30.7 %collective-permute-start.12 = (bf16[32,2048]{1,0:T(8,128)(2,1)S(1)}, bf16[32,2048]{1,0:T(8,128)(2,1)S(1)}, u32[]{:S(2)}, u32[]{:S(2)}) collective-permute-start(bf16[32,2048]{1,0:T(8,128)(2,1)S(1)} %copy-done.16), channel_id=1, source_target_pairs={{0,3},{1,0},{2,1},{3,2},{4,7},{5,4},{6,5},{7,6},{8,11},{9,8},{10,9... | collective-permute-start | bytes 393224 | tf_op jit(solution)/shard_map/ppermute | solution.py:736
  100.3 28.2 %collective-permute-start.13 = (bf16[32,2048]{1,0:T(8,128)(2,1)S(1)}, bf16[32,2048]{1,0:T(8,128)(2,1)S(1)}, u32[]{:S(2)}, u32[]{:S(2)}) collective-permute-start(bf16[32,2048]{1,0:T(8,128)(2,1)S(1)} %copy-done.15), channel_id=1, source_target_pairs={{0,2},{1,3},{2,0},{3,1},{4,6},{5,7},{6,4},{7,5},{8,10},{9,11},{10,... | collective-permute-start | bytes 393224 | tf_op jit(solution)/shard_map/ppermute | solution.py:736
  103.6 25.0 %collective-permute-start.14 = (bf16[32,2048]{1,0:T(8,128)(2,1)S(1)}, bf16[32,2048]{1,0:T(8,128)(2,1)S(1)}, u32[]{:S(2)}, u32[]{:S(2)}) collective-permute-start(bf16[32,2048]{1,0:T(8,128)(2,1)S(1)} %copy-done.14), channel_id=1, source_target_pairs={{0,1},{1,2},{2,3},{3,0},{4,5},{5,6},{6,7},{7,4},{8,9},{9,10},{10,1... | collective-permute-start | bytes 393224 | tf_op jit(solution)/shard_map/ppermute | solution.py:736
  122.1 17.5 %all-to-all-start.2 = ((f32[64,4,128]{2,1,0:T(4,128)}), f32[64,4,128]{2,1,0:T(4,128)S(1)}, u32[]{:S(2)}, u32[]{:S(2)}) async-start(f32[64,4,128]{2,1,0:T(4,128)} %final_part.1), calls=%async_computation.2 | async-start | bytes 262144 | tf_op jit(solution)/shard_map/all_to_all | solution.py:781
